TPU v7x, 256 devices: a whole 4x4x8 slice. The times are simulated.
256 devices in a mesh: lvl: 32 (over x, y, core), mid: 8 (over z).
Axes of the slice: x: 4, y: 4, z: 8, core: 2. Of those that a mesh axis runs over, the one named last changes fastest.
Arguments:
- signal: bfloat16 [8192, 64, 128], P(('lvl', 'mid')), may hold values from -6 to 6
- leaf_in: bfloat16 [8192, 64, 128], P(('lvl', 'mid')), may hold values from -0.5 to 0.5
- upper_w: bfloat16 [3, 8192, 64, 256], P(None, ('lvl', 'mid')), may hold values from -0.375 to 0.375
- middle_w: bfloat16 [2, 8192, 64, 256], P(None, ('lvl', 'mid')), may hold values from -0.375 to 0.375
- lower_w: bfloat16 [2, 8192, 64, 256], P(None, ('lvl', 'mid')), may hold values from -0.375 to 0.375
- leaf_out: bfloat16 [8192, 64, 128], P(('lvl', 'mid')), may hold values from -0.5 to 0.5
Outputs:
- applied: bfloat16 [8192, 64, 128], P(('lvl', 'mid'))
All inputs are finite; a program needn't handle non-finite values.
Results may differ from a plain program's by a relative error of at most 0.018.
Values may be sent and summed in bfloat16 or wider, within the bound.
No kernel may reach another device: no remote copies, remote signals or barrier semaphores. Data moves between devices by JAX's collectives and lax.ppermute only.
A program may use at most 64 MiB of HBM per device.

v0:
```python
import jax
import jax.numpy as jnp
from jax import lax
from jax.sharding import PartitionSpec as P


def from_partner(block, axis, stride):
    count = lax.axis_size(axis)
    route = []
    for low in range(count):
        high = low | 1 << stride
        if high != low and high < count:
            route += [(low, high), (high, low)]
    return lax.ppermute(block, axis, route)


def turning_table(width):
    half = width // 2
    row_ids = lax.broadcasted_iota(jnp.int32, (width, width), 0)
    col_ids = lax.broadcasted_iota(jnp.int32, (width, width), 1)
    minus = jnp.where(row_ids == col_ids + half, -1.0, 0.0)
    plus = jnp.where(row_ids + half == col_ids, 1.0, 0.0)
    return (minus + plus).astype(jnp.bfloat16)


def mix(weights, parts):
    table = turning_table(parts[0].shape[-1])
    turned = [
        jnp.einsum("nkc,cd->nkd", piece, table, preferred_element_type=jnp.float32).astype(
            jnp.bfloat16
        )
        for piece in parts
    ]
    stacked = jnp.concatenate(list(parts) + turned, axis=1)
    total = jnp.einsum("nrk,nkc->nrc", weights, stacked, preferred_element_type=jnp.float32)
    return total.astype(jnp.bfloat16)


def partner(field, outer, inner):
    shaped = field.reshape((outer, -1, 2, inner) + field.shape[-2:])
    return jnp.flip(shaped, 2).reshape(field.shape)


def across(field, weights, bit):
    other = from_partner(field, "lvl", bit)
    return mix(weights, (field, other))


def on_device(signal, leaf_in, upper_w, middle_w, lower_w, leaf_out):
    field = mix(leaf_in, (signal,))
    box_count = field.shape[0]
    lvl_bits = lax.axis_size("lvl").bit_length() - 1
    mid_size = lax.axis_size("mid")
    mid_bits = mid_size.bit_length() - 1
    for step in range(upper_w.shape[0]):
        field = across(field, upper_w[step], lvl_bits - 1 - step)
    blocks = field.reshape((mid_size, box_count // mid_size) + field.shape[1:])
    blocks = lax.all_to_all(blocks, "mid", split_axis=0, concat_axis=0, tiled=True)
    field = blocks.reshape(field.shape)
    for step in range(middle_w.shape[0]):
        bit = mid_bits - 1 - step
        other = partner(field, 1, (1 << bit) * (box_count // mid_size))
        field = mix(middle_w[step], (field, other))
    lower_count = lower_w.shape[0]
    for step in range(lower_count):
        field = across(field, lower_w[step], lower_count - 1 - step)
    return mix(leaf_out, (field,))


def solution(mesh):
    placed = (
        P(("lvl", "mid"), None, None),
        P(("lvl", "mid"), None, None),
        P(None, ("lvl", "mid"), None, None),
        P(None, ("lvl", "mid"), None, None),
        P(None, ("lvl", "mid"), None, None),
        P(("lvl", "mid"), None, None),
    )
    return jax.shard_map(
        on_device,
        mesh=mesh,
        in_specs=placed,
        out_specs=P(("lvl", "mid"), None, None),
        check_vma=False,
    )
```

profile of v0, /device:TPU:1, one launch (start us, length us, event | category | flops | bytes accessed | tf_op | source)
XLA Modules:
  0.0 90.8 jit_solution(18102956792038194101)
XLA Ops:
  0.0 0.0 copy-start
  0.0 1.5 %fusion.92 = bf16[32,64,128]{2,1,0:T(8,128)(2,1)S(1)} fusion(bf16[32,64,128]{2,1,0:T(8,128)(2,1)} %param.6, s32[128]{0:T(128)S(1)} %iota_add_fusion), kind=kOutput, calls=%fused_computation.86 | convolution fusion | flops 67469312 | bytes 1049088 | tf_op jit(solution)/shard_map/nkc,cd->nkd/dot_general | solution.py:29
  1.5 0.0 copy-done
  1.5 0.0 copy-start.1
  1.5 1.6 %fusion.93 = bf16[32,64,128]{2,1,0:T(8,128)(2,1)S(1)} fusion(bf16[32,64,128]{2,1,0:T(8,128)(2,1)S(1)} %copy-done, bf16[32,64,128]{2,1,0:T(8,128)(2,1)S(1)} %fusion.92, bf16[32,64,128]{2,1,0:T(8,128)(2,1)} %param.6), kind=kOutput, calls=%fused_computation.87 | convolution fusion | flops 69468160 | bytes 2097152 | tf_op jit(solution)/shard_map/nrk,nkc->nrc/dot_general | solution.py:35
  3.1 3.7 %collective-permute-start = (bf16[32,64,128]{2,1,0:T(8,128)(2,1)S(1)}, bf16[32,64,128]{2,1,0:T(8,128)(2,1)S(1)}, u32[]{:S(2)}, u32[]{:S(2)}) collective-permute-start(bf16[32,64,128]{2,1,0:T(8,128)(2,1)S(1)} %fusion.93), channel_id=1, source_target_pairs={{0,128},{128,0},{8,136},{136,8},{16,144},{144,16},{24,152},{152,24... | collective-permute-start | bytes 1572872 | tf_op jit(solution)/shard_map/ppermute | solution.py:14
  6.8 0.4 convolution_convert_fusion.16
  7.1 10.2 %collective-permute-done = bf16[32,64,128]{2,1,0:T(8,128)(2,1)S(1)} collective-permute-done((bf16[32,64,128]{2,1,0:T(8,128)(2,1)S(1)}, bf16[32,64,128]{2,1,0:T(8,128)(2,1)S(1)}, u32[]{:S(2)}, u32[]{:S(2)}) %collective-permute-start) | collective-permute-done | bytes 524320 | tf_op jit(solution)/shard_map/ppermute | solution.py:14
  17.3 0.3 convolution_convert_fusion.15
  17.7 0.0 copy-done.1
  17.7 0.5 fusion.77
  18.2 2.3 %collective-permute-start.1 = (bf16[32,64,128]{2,1,0:T(8,128)(2,1)S(1)}, bf16[32,64,128]{2,1,0:T(8,128)(2,1)S(1)}, u32[]{:S(2)}, u32[]{:S(2)}) collective-permute-start(bf16[32,64,128]{2,1,0:T(8,128)(2,1)S(1)} %fusion.77), channel_id=1, source_target_pairs={{0,64},{64,0},{8,72},{72,8},{16,80},{80,16},{24,88},{88,24},{32,96... | collective-permute-start | bytes 1572872 | tf_op jit(solution)/shard_map/ppermute | solution.py:14
  20.5 0.4 convolution_convert_fusion.14
  20.8 10.0 %collective-permute-done.1 = bf16[32,64,128]{2,1,0:T(8,128)(2,1)S(1)} collective-permute-done((bf16[32,64,128]{2,1,0:T(8,128)(2,1)S(1)}, bf16[32,64,128]{2,1,0:T(8,128)(2,1)S(1)}, u32[]{:S(2)}, u32[]{:S(2)}) %collective-permute-start.1) | collective-permute-done | bytes 524320 | tf_op jit(solution)/shard_map/ppermute | solution.py:14
  30.9 0.4 convolution_convert_fusion.13
  31.2 0.5 fusion.80
  31.7 3.3 %collective-permute-start.2 = (bf16[32,64,128]{2,1,0:T(8,128)(2,1)S(1)}, bf16[32,64,128]{2,1,0:T(8,128)(2,1)S(1)}, u32[]{:S(2)}, u32[]{:S(2)}) collective-permute-start(bf16[32,64,128]{2,1,0:T(8,128)(2,1)S(1)} %fusion.80), channel_id=1, source_target_pairs={{0,32},{32,0},{8,40},{40,8},{16,48},{48,16},{24,56},{56,24},{64,96... | collective-permute-start | bytes 1572872 | tf_op jit(solution)/shard_map/ppermute | solution.py:14
  35.0 0.3 convolution_convert_fusion.12
  35.4 9.3 %collective-permute-done.2 = bf16[32,64,128]{2,1,0:T(8,128)(2,1)S(1)} collective-permute-done((bf16[32,64,128]{2,1,0:T(8,128)(2,1)S(1)}, bf16[32,64,128]{2,1,0:T(8,128)(2,1)S(1)}, u32[]{:S(2)}, u32[]{:S(2)}) %collective-permute-start.2) | collective-permute-done | bytes 524320 | tf_op jit(solution)/shard_map/ppermute | solution.py:14
  44.7 0.4 convolution_convert_fusion.11
  45.1 0.5 fusion.68
  45.6 20.8 %all_to_all.5 = bf16[8,4,64,128]{3,2,1,0:T(8,128)(2,1)S(1)} all-to-all(bf16[8,4,64,128]{3,2,1,0:T(8,128)(2,1)S(1)} %bitcast.93), channel_id=1, replica_groups=mesh['lvl'=32,'mid'=8] {'mid'}, dimensions={0} | all-to-all | bytes 1048576 | tf_op jit(solution)/shard_map/all_to_all | solution.py:58
  66.4 0.0 copy-start.2
  66.4 0.3 convolution_convert_fusion.9
  66.8 0.4 convolution_convert_fusion.10
  67.1 0.9 copy-done.2
  68.0 0.5 fusion.65
  68.5 0.3 convolution_convert_fusion.8
  68.9 0.4 convolution_convert_fusion.7
  69.3 1.7 %fusion.83 = bf16[32,64,128]{2,1,0:T(8,128)(2,1)S(1)} fusion(bf16[32,64,128]{2,1,0:T(8,128)(2,1)S(1)} %convolution_convert_fusion.7, bf16[32,64,128]{2,1,0:T(8,128)(2,1)S(1)} %convolution_convert_fusion.8, bf16[32,64,128]{2,1,0:T(8,128)(2,1)S(1)} %bitcast.92, bf16[32,64,128]{2,1,0:T(8,128)(2,1)S(1)} %bitcast.88, bf16[2,32,64,256]{3,2,1,0:T(8,128)(2,1)} %param.9), kind=kOutput, calls=%fused_computation.83 | convolution fusion | flops 142868480 | bytes 3670016 | tf_op jit(solution)/shard_map/nrk,nkc->nrc/dot_general | solution.py:35
  71.0 0.0 copy-start.3
  71.0 1.4 %collective-permute-start.3 = (bf16[32,64,128]{2,1,0:T(8,128)(2,1)S(1)}, bf16[32,64,128]{2,1,0:T(8,128)(2,1)S(1)}, u32[]{:S(2)}, u32[]{:S(2)}) collective-permute-start(bf16[32,64,128]{2,1,0:T(8,128)(2,1)S(1)} %fusion.83), channel_id=1, source_target_pairs={{0,16},{16,0},{8,24},{24,8},{32,48},{48,32},{40,56},{56,40},{64,80... | collective-permute-start | bytes 1572872 | tf_op jit(solution)/shard_map/ppermute | solution.py:14
  72.4 0.3 convolution_convert_fusion.6
  72.7 6.4 %collective-permute-done.3 = bf16[32,64,128]{2,1,0:T(8,128)(2,1)S(1)} collective-permute-done((bf16[32,64,128]{2,1,0:T(8,128)(2,1)S(1)}, bf16[32,64,128]{2,1,0:T(8,128)(2,1)S(1)}, u32[]{:S(2)}, u32[]{:S(2)}) %collective-permute-start.3) | collective-permute-done | bytes 524320 | tf_op jit(solution)/shard_map/ppermute | solution.py:14
  79.1 0.3 convolution_convert_fusion.5
  79.5 0.0 copy-done.3
  79.5 0.5 fusion.86
  80.0 6.7 %collective-permute-start.4 = (bf16[32,64,128]{2,1,0:T(8,128)(2,1)S(1)}, bf16[32,64,128]{2,1,0:T(8,128)(2,1)S(1)}, u32[]{:S(2)}, u32[]{:S(2)}) collective-permute-start(bf16[32,64,128]{2,1,0:T(8,128)(2,1)S(1)} %fusion.86), channel_id=1, source_target_pairs={{0,8},{8,0},{16,24},{24,16},{32,40},{40,32},{48,56},{56,48},{64,72... | collective-permute-start | bytes 1572872 | tf_op jit(solution)/shard_map/ppermute | solution.py:14
  86.7 0.3 convolution_convert_fusion.4
  87.0 1.2 %collective-permute-done.4 = bf16[32,64,128]{2,1,0:T(8,128)(2,1)S(1)} collective-permute-done((bf16[32,64,128]{2,1,0:T(8,128)(2,1)S(1)}, bf16[32,64,128]{2,1,0:T(8,128)(2,1)S(1)}, u32[]{:S(2)}, u32[]{:S(2)}) %collective-permute-start.4) | collective-permute-done | bytes 524320 | tf_op jit(solution)/shard_map/ppermute | solution.py:14
  88.2 0.4 convolution_convert_fusion.3
  88.6 0.0 copy-start.4
  88.6 0.5 fusion.89
  89.1 0.4 convolution_convert_fusion.2
  89.4 0.2 copy-done.4
  89.6 1.2 %fusion.94 = bf16[32,64,128]{2,1,0:T(8,128)(2,1)} fusion(bf16[32,64,128]{2,1,0:T(8,128)(2,1)S(1)} %copy-done.4, bf16[32,64,128]{2,1,0:T(8,128)(2,1)S(1)} %convolution_convert_fusion.2, bf16[32,64,128]{2,1,0:T(8,128)(2,1)S(1)} %fusion.89), kind=kOutput, calls=%fused_computation.88 | convolution fusion | flops 69468160 | bytes 2097152 | tf_op jit(solution)/shard_map/nrk,nkc->nrc/dot_general | solution.py:35
  (3 shorter events, 0.1 us)
Async XLA Ops:
  0.0 1.5 %copy-start = (bf16[32,64,128]{2,1,0:T(8,128)(2,1)S(1)}, bf16[32,64,128]{2,1,0:T(8,128)(2,1)}, u32[]{:S(2)}) copy-start(bf16[32,64,128]{2,1,0:T(8,128)(2,1)} %param.7) | copy-start | bytes 1572868
  1.5 16.2 %copy-start.1 = (bf16[3,32,64,256]{3,2,1,0:T(8,128)(2,1)S(1)}, bf16[3,32,64,256]{3,2,1,0:T(8,128)(2,1)}, u32[]{:S(2)}) copy-start(bf16[3,32,64,256]{3,2,1,0:T(8,128)(2,1)} %param.8) | copy-start | bytes 9437188
  3.1 14.2 %collective-permute-start = (bf16[32,64,128]{2,1,0:T(8,128)(2,1)S(1)}, bf16[32,64,128]{2,1,0:T(8,128)(2,1)S(1)}, u32[]{:S(2)}, u32[]{:S(2)}) collective-permute-start(bf16[32,64,128]{2,1,0:T(8,128)(2,1)S(1)} %fusion.93), channel_id=1, source_target_pairs={{0,128},{128,0},{8,136},{136,8},{16,144},{144,16},{24,152},{152,24... | collective-permute-start | bytes 1572872 | tf_op jit(solution)/shard_map/ppermute | solution.py:14
  18.2 12.6 %collective-permute-start.1 = (bf16[32,64,128]{2,1,0:T(8,128)(2,1)S(1)}, bf16[32,64,128]{2,1,0:T(8,128)(2,1)S(1)}, u32[]{:S(2)}, u32[]{:S(2)}) collective-permute-start(bf16[32,64,128]{2,1,0:T(8,128)(2,1)S(1)} %fusion.77), channel_id=1, source_target_pairs={{0,64},{64,0},{8,72},{72,8},{16,80},{80,16},{24,88},{88,24},{32,96... | collective-permute-start | bytes 1572872 | tf_op jit(solution)/shard_map/ppermute | solution.py:14
  31.7 13.0 %collective-permute-start.2 = (bf16[32,64,128]{2,1,0:T(8,128)(2,1)S(1)}, bf16[32,64,128]{2,1,0:T(8,128)(2,1)S(1)}, u32[]{:S(2)}, u32[]{:S(2)}) collective-permute-start(bf16[32,64,128]{2,1,0:T(8,128)(2,1)S(1)} %fusion.80), channel_id=1, source_target_pairs={{0,32},{32,0},{8,40},{40,8},{16,48},{48,16},{24,56},{56,24},{64,96... | collective-permute-start | bytes 1572872 | tf_op jit(solution)/shard_map/ppermute | solution.py:14
  66.4 1.6 %copy-start.2 = (bf16[2,32,64,256]{3,2,1,0:T(8,128)(2,1)S(1)}, bf16[2,32,64,256]{3,2,1,0:T(8,128)(2,1)}, u32[]{:S(2)}) copy-start(bf16[2,32,64,256]{3,2,1,0:T(8,128)(2,1)} %param.9) | copy-start | bytes 6291460
  71.0 8.5 %copy-start.3 = (bf16[2,32,64,256]{3,2,1,0:T(8,128)(2,1)S(1)}, bf16[2,32,64,256]{3,2,1,0:T(8,128)(2,1)}, u32[]{:S(2)}) copy-start(bf16[2,32,64,256]{3,2,1,0:T(8,128)(2,1)} %param.10) | copy-start | bytes 6291460
  71.0 8.1 %collective-permute-start.3 = (bf16[32,64,128]{2,1,0:T(8,128)(2,1)S(1)}, bf16[32,64,128]{2,1,0:T(8,128)(2,1)S(1)}, u32[]{:S(2)}, u32[]{:S(2)}) collective-permute-start(bf16[32,64,128]{2,1,0:T(8,128)(2,1)S(1)} %fusion.83), channel_id=1, source_target_pairs={{0,16},{16,0},{8,24},{24,8},{32,48},{48,32},{40,56},{56,40},{64,80... | collective-permute-start | bytes 1572872 | tf_op jit(solution)/shard_map/ppermute | solution.py:14
  80.0 8.2 %collective-permute-start.4 = (bf16[32,64,128]{2,1,0:T(8,128)(2,1)S(1)}, bf16[32,64,128]{2,1,0:T(8,128)(2,1)S(1)}, u32[]{:S(2)}, u32[]{:S(2)}) collective-permute-start(bf16[32,64,128]{2,1,0:T(8,128)(2,1)S(1)} %fusion.86), channel_id=1, source_target_pairs={{0,8},{8,0},{16,24},{24,16},{32,40},{40,32},{48,56},{56,48},{64,72... | collective-permute-start | bytes 1572872 | tf_op jit(solution)/shard_map/ppermute | solution.py:14
  88.6 1.0 %copy-start.4 = (bf16[32,64,128]{2,1,0:T(8,128)(2,1)S(1)}, bf16[32,64,128]{2,1,0:T(8,128)(2,1)}, u32[]{:S(2)}) copy-start(bf16[32,64,128]{2,1,0:T(8,128)(2,1)} %param.11) | copy-start | bytes 1572868
where the time goes:
time: 91.1 us; the launch traced here: 90.8 us
  waiting for transfers between devices  37.2 us (41%)
  blocking collectives  20.8 us (23%)
  starting transfers between devices  17.3 us (19%)
  matrix products  14.2 us (16%)
  local copies, waits for them, and re-layouts  1.14 us (1%)
    ppermute x5, waiting for transfers between devices, from_partner(): return lax.ppermute(block, axis, route)  37.2 us
    all_to_all x1, blocking collectives, on_device(): lax.all_to_all(blocks, 'mid', split_axis=0, concat_axis=0, tiled=True)  20.8 us
    ppermute x5, starting transfers between devices, from_partner(): return lax.ppermute(block, axis, route)  17.3 us
    dot_general x9, matrix products, mix(): jnp.einsum('nrk,nkc->nrc', weights, stacked, preferred_element_type=jnp.f...  7.53 us
    dot_general x16, matrix products, mix(): jnp.einsum('nkc,cd->nkd', piece, table, preferred_element_type=jnp.float32)  6.7 us
  transfers between devices with their start and end apart: 5, of which 5 were waited for; matrix products, arithmetic and copies ran while one was open for 2% of the time, Pallas kernels for 0%

commit v1 on v0

v1 whole, which is shorter than its diff:
```python
import functools

import jax
import jax.numpy as jnp
from jax import lax
from jax.experimental import pallas as pl
from jax.experimental.pallas import tpu as pltpu
from jax.sharding import PartitionSpec as P

WIDTHS = (1, 1, 1, 1)
GROUPS = ((0, 1, 2, 3),)
LEAF_LIMIT = 8 << 20
PLAN = (
    "L0", "L1", "L2", "L3", "U00", "U01", "U02", "U10", "U03", "U11", "U20", "U12", "U21", "U13",
    "U22", "W0", "U23", "M0", "M1", "M2", "M3", "D00", "D01", "D02", "D03", "E012", "E3",
)
VMEM = pl.BlockSpec(memory_space=pltpu.VMEM)
ANY = pl.BlockSpec(memory_space=pl.ANY)
DMA = pltpu.SemaphoreType.DMA
TOKEN = jax.ShapeDtypeStruct((8, 128), jnp.float32)
COST = {"L": 0, "W": 0, "U0": 0, "U1": 0, "U2": 0, "M": 0, "D0": 0, "D1": 0}


def turn(piece):
    half = piece.shape[-1] // 2
    rolled = pltpu.roll(piece.astype(jnp.float32), half, 1)
    lane = lax.broadcasted_iota(jnp.int32, piece.shape, 1)
    return jnp.where(lane < half, -rolled, rolled).astype(jnp.bfloat16)


def product(weights, parts):
    stacked = jnp.concatenate(list(parts) + [turn(p) for p in parts], axis=0)
    return jnp.dot(weights, stacked, preferred_element_type=jnp.float32).astype(jnp.bfloat16)


def leaf_kernel(first, w_ref, x_ref, t_ref, o_ref, u_ref, ws_ref, xs_ref, sems):
    u_ref[...] = t_ref[...]
    width = o_ref.shape[1]
    loads = [
        pltpu.make_async_copy(w_ref.at[:, first:first + width], ws_ref, sems.at[0]),
        pltpu.make_async_copy(x_ref.at[:, first:first + width], xs_ref, sems.at[1]),
    ]
    for load in loads:
        load.start()
    for load in loads:
        load.wait()
    for a in range(o_ref.shape[0]):
        for b in range(width):
            o_ref[a, b] = product(ws_ref[a, b], [xs_ref[a, b]])


def stage_kernel(t_ref, *refs):
    count = (len(refs) - 2) // 2
    u_ref, sems = refs[-2:]
    u_ref[...] = t_ref[...]
    loads = [pltpu.make_async_copy(refs[i], refs[count + i], sems.at[i]) for i in range(count)]
    for load in loads:
        load.start()
    for load in loads:
        load.wait()


def level_kernel(first, step, w_ref, x_ref, y_ref, t_ref, o_ref, u_ref):
    u_ref[...] = t_ref[...]
    for a in range(o_ref.shape[0]):
        for b in range(o_ref.shape[1]):
            o_ref[a, b] = product(w_ref[step, a, first + b], [x_ref[a, b], y_ref[a, b]])


def join_kernel(first, step, w_ref, x_ref, y_ref, t_ref, *refs):
    *earlier, o_ref, u_ref, s_ref, sem = refs
    u_ref[...] = t_ref[...]
    at = 0
    stores = []
    for e_ref in earlier:
        stores.append(pltpu.make_async_copy(e_ref, o_ref.at[:, at:at + e_ref.shape[1]], sem))
        at += e_ref.shape[1]
    for a in range(s_ref.shape[0]):
        for b in range(x_ref.shape[1]):
            s_ref[a, b] = product(w_ref[step, a, first + b], [x_ref[a, b], y_ref[a, b]])
    stores.append(pltpu.make_async_copy(s_ref, o_ref.at[:, at:], sem))
    for store in stores:
        store.start()
    for store in stores:
        store.wait()


def middle_kernel(first, at, w_ref, x_ref, t_ref, o_ref, u_ref, x_scr, s_ref, sem):
    u_ref[...] = t_ref[...]
    count, width = o_ref.shape[:2]
    load = pltpu.make_async_copy(x_ref.at[:, at:at + width], x_scr, sem)
    load.start()
    load.wait()
    for a in range(count):
        for b in range(width):
            s_ref[a, b] = product(w_ref[0, a, first + b], [x_scr[a, b], x_scr[a ^ (count // 2), b]])
    for a in range(count):
        for b in range(width):
            o_ref[a, b] = product(w_ref[1, a, first + b], [s_ref[a, b], s_ref[a ^ (count // 4), b]])


def last_group_kernel(step, firsts, w_ref, v_ref, t_ref, *refs):
    o_ref, u_ref, r_ref, sems = refs[-4:]
    u_ref[...] = t_ref[...]
    stores = []
    for c, first in enumerate(firsts):
        x_ref, y_ref = refs[2 * c], refs[2 * c + 1]
        width = x_ref.shape[1]
        for a in range(x_ref.shape[0]):
            for b in range(width):
                value = product(w_ref[step, a, first + b], [x_ref[a, b], y_ref[a, b]])
                r_ref[a, first + b] = product(v_ref[a, first + b], [value])
        store = pltpu.make_async_copy(r_ref.at[:, first:first + width], o_ref.at[:, first:first + width], sems.at[c])
        store.start()
        stores.append(store)
    for store in stores:
        store.wait()


def call(kind, kernel, shapes, args, specs, out_specs, token, limit=8 << 20, **kw):
    *outs, token = pl.pallas_call(
        kernel,
        out_shape=[jax.ShapeDtypeStruct(shape, jnp.bfloat16) for shape in shapes] + [TOKEN],
        in_specs=specs,
        out_specs=list(out_specs) + [VMEM],
        compiler_params=pltpu.CompilerParams(vmem_limit_bytes=limit),
        cost_estimate=pl.CostEstimate(flops=1 + int(COST[kind] * 1e9), bytes_accessed=1, transcendentals=0),
        **kw,
    )(*args)
    return outs, token


def on_device(signal, leaf_in, upper_w, middle_w, lower_w, leaf_out):
    lvl_size, mid_size = lax.axis_size("lvl"), lax.axis_size("mid")
    lvl_bits = lvl_size.bit_length() - 1
    inner = signal.shape[0] // mid_size
    box = signal.shape[1:]
    part = functools.partial
    leaf_w, up_w, mid_w, low_w, out_w, samples = (
        v.reshape(v.shape[:-3] + (mid_size, inner) + v.shape[-2:])
        for v in (leaf_in, upper_w, middle_w, lower_w, leaf_out, signal)
    )
    firsts = [sum(WIDTHS[:c]) for c in range(len(WIDTHS))]
    shapes = [(mid_size, w) + box for w in WIDTHS]

    def swap(block, bit):
        return lax.ppermute(block, "lvl", [(i, i ^ (1 << bit)) for i in range(lvl_size)])

    field, other, place = {}, {}, {}
    token = jnp.zeros(TOKEN.shape, TOKEN.dtype)
    result = None
    lower_count = lower_w.shape[0]
    upper_count = upper_w.shape[0]
    for item in PLAN:
        kind, c = item[0], int(item[-1])
        step = int(item[1])
        name = item[:-1] if kind in "UD" else kind
        name = name if item not in COST else item
        first, shape = firsts[c], shapes[c]
        block = pltpu.VMEM(shape, jnp.bfloat16)
        if kind == "W":
            staged = (mid_w, low_w, out_w)
            (mid_w, low_w, out_w), token = call(name, stage_kernel, [v.shape for v in staged], (token, *staged),
                                                      [VMEM] + [ANY] * 3, [VMEM] * 3, token, scratch_shapes=[DMA((3,))])
        elif kind == "L":
            (field[c],), token = call(name, part(leaf_kernel, first), [shape], (leaf_w, samples, token), [ANY, ANY, VMEM],
                                      [VMEM], token, LEAF_LIMIT if c == 0 else 8 << 20,
                                      scratch_shapes=[block, block, DMA((2,))])
            other[c] = swap(field[c], lvl_bits - 1)
        elif kind == "U" and (step < upper_count - 1 or c not in [g[-1] for g in GROUPS]):
            (field[c],), token = call(name, part(level_kernel, first, step), [shape], (up_w, field[c], other[c], token),
                                      [VMEM] * 4, [VMEM], token)
            if step < upper_count - 1:
                other[c] = swap(field[c], lvl_bits - 2 - step)
        elif kind == "U":
            group = next(g for g in GROUPS if c in g)
            earlier = [field[e] for e in group[:-1]]
            whole = (mid_size, sum(WIDTHS[e] for e in group)) + box
            (joined,), token = call(name, part(join_kernel, first, step), [whole],
                                    (up_w, field[c], other[c], token, *earlier), [VMEM] * (4 + len(earlier)), [ANY],
                                    token, scratch_shapes=[block, DMA])
            moved = lax.all_to_all(joined, "mid", split_axis=0, concat_axis=0, tiled=True)
            at = 0
            for e in group:
                field[e], place[e] = moved, at
                at += WIDTHS[e]
        elif kind == "M":
            (field[c],), token = call(name, part(middle_kernel, first, place[c]), [shape], (mid_w, field[c], token),
                                      [VMEM, ANY, VMEM], [VMEM], token, scratch_shapes=[block, block, DMA])
            other[c] = swap(field[c], lower_count - 1)
        elif kind == "D" and step < lower_count - 1:
            (field[c],), token = call(name, part(level_kernel, first, step), [shape], (low_w, field[c], other[c], token),
                                      [VMEM] * 4, [VMEM], token)
            other[c] = swap(field[c], lower_count - 2 - step)
        elif kind == "E":
            chosen = [int(e) for e in item[1:]]
            pairs = [v for e in chosen for v in (field[e], other[e])]
            args, specs, alias = (low_w, out_w, token, *pairs), [VMEM] * (3 + len(pairs)), {}
            if result is not None:
                args, specs, alias = args + (result,), specs + [ANY], {len(args): 0}
            (result,), token = call("D1", part(last_group_kernel, lower_count - 1, [firsts[e] for e in chosen]),
                                    [samples.shape], args, specs, [ANY], token, input_output_aliases=alias,
                                    scratch_shapes=[pltpu.VMEM(samples.shape, jnp.bfloat16), DMA((len(chosen),))])
    return result.reshape(signal.shape)


def solution(mesh):
    boxes = P(("lvl", "mid"), None, None)
    levels = P(None, ("lvl", "mid"), None, None)
    return jax.shard_map(
        on_device,
        mesh=mesh,
        in_specs=(boxes, boxes, levels, levels, levels, boxes),
        out_specs=boxes,
        check_vma=False,
    )
```

time: 91.1 us -> 78.5 us (0.86)
  waiting for transfers between devices: 37.2 us -> 9.17 us
  starting transfers between devices: 17.3 us -> 33.8 us
  matrix products: 14.2 us -> 0 us
  Pallas kernels: 0 us -> 12.3 us
  local copies, waits for them, and re-layouts: 1.14 us -> 2.1 us
    ppermute x5 -> x20, waiting for transfers between devices: 37.2 us -> 9.17 us  [swap(): lax.ppermute(block, 'lvl', [(i, i ^ 1 << bit) for i in range(lvl_size)])]
    ppermute x5 -> x20, starting transfers between devices: 17.3 us -> 33.8 us  [swap(): lax.ppermute(block, 'lvl', [(i, i ^ 1 << bit) for i in range(lvl_size)])]
    dot_general x25 -> x0, matrix products: 14.2 us -> none  [the longest x9 7.53 us: mix(): jnp.einsum('nrk,nkc->nrc', weights, stacked, preferred_element_type=jnp.f...]
    pallas_call x0 -> x27, Pallas kernels: none -> 12.3 us  [call(): pl.pallas_call(kernel, out_shape=[jax.ShapeDtypeStruct(shape, jnp.bfloat1...]
    unnamed x10 -> x12, local copies, waits for them, and re-layouts: 1.07 us -> 2.1 us
  transfers between devices with their start and end apart: 5 -> 20, of which waited for: 5 -> 8; matrix products, arithmetic and copies ran while one was open for 2% -> 0% of each run, Pallas kernels for 0% -> 12%
where the time goes in v1:
time: 78.5 us; the launch traced here: 78.3 us
  starting transfers between devices  33.8 us (43%)
  blocking collectives  20.5 us (26%)
  Pallas kernels  12.3 us (16%)
  waiting for transfers between devices  9.17 us (12%)
  local copies, waits for them, and re-layouts  2.1 us (3%)
    ppermute x20, starting transfers between devices, swap(): lax.ppermute(block, 'lvl', [(i, i ^ 1 << bit) for i in range(lvl_size)])  33.8 us
    all_to_all x1, blocking collectives, on_device(): lax.all_to_all(joined, 'mid', split_axis=0, concat_axis=0, tiled=True)  20.5 us
    pallas_call x27, Pallas kernels, call(): pl.pallas_call(kernel, out_shape=[jax.ShapeDtypeStruct(shape, jnp.bfloat1...  12.3 us
    ppermute x20, waiting for transfers between devices, swap(): lax.ppermute(block, 'lvl', [(i, i ^ 1 << bit) for i in range(lvl_size)])  9.17 us
    unnamed x12, local copies, waits for them, and re-layouts  2.1 us
  transfers between devices with their start and end apart: 20, of which 8 were waited for; matrix products, arithmetic and copies ran while one was open for 0% of the time, Pallas kernels for 12%

profile of v1, /device:TPU:1, one launch (start us, length us, event | category | flops | bytes accessed | tf_op | source)
XLA Modules:
  0.0 78.3 jit_solution(2557532275355237178)
XLA Ops:
  0.0 1.0 %copy-done.1 = bf16[32,64,128]{2,1,0:T(8,128)(2,1)S(1)} copy-done((bf16[32,64,128]{2,1,0:T(8,128)(2,1)S(1)}, bf16[32,64,128]{2,1,0:T(8,128)(2,1)}, u32[]{:S(2)}) %copy-start.1) | copy-done | bytes 524312
  1.0 1.0 %copy-done.2 = bf16[32,64,128]{2,1,0:T(8,128)(2,1)S(1)} copy-done((bf16[32,64,128]{2,1,0:T(8,128)(2,1)S(1)}, bf16[32,64,128]{2,1,0:T(8,128)(2,1)}, u32[]{:S(2)}) %copy-start.2) | copy-done | bytes 524312
  2.1 0.3 shard_map.64
  2.4 3.7 %collective-permute-start.2 = (bf16[8,1,64,128]{3,2,1,0:T(8,128)(2,1)S(1)}, bf16[8,1,64,128]{3,2,1,0:T(8,128)(2,1)S(1)}, u32[]{:S(2)}, u32[]{:S(2)}) collective-permute-start(bf16[8,1,64,128]{3,2,1,0:T(8,128)(2,1)S(1)} %get-tuple-element.64.x_ref), channel_id=1, source_target_pairs={{0,128},{8,136},{16,144},{24,152},{32,160},{40,168},{48,176},{56,1... | collective-permute-start | bytes 393224 | tf_op jit(solution)/shard_map/ppermute | solution.py:147
  6.1 0.3 shard_map.65
  6.4 0.1 collective-permute-start.1
  6.5 0.3 shard_map.66
  6.9 3.0 %collective-permute-start = (bf16[8,1,64,128]{3,2,1,0:T(8,128)(2,1)S(1)}, bf16[8,1,64,128]{3,2,1,0:T(8,128)(2,1)S(1)}, u32[]{:S(2)}, u32[]{:S(2)}) collective-permute-start(bf16[8,1,64,128]{3,2,1,0:T(8,128)(2,1)S(1)} %get-tuple-element.62.x_ref), channel_id=1, source_target_pairs={{0,128},{8,136},{16,144},{24,152},{32,160},{40,168},{48,176},{56,1... | collective-permute-start | bytes 393224 | tf_op jit(solution)/shard_map/ppermute | solution.py:147
  9.9 0.3 shard_map.67
  10.3 0.3 shard_map.68
  10.6 0.4 collective-permute-start.4
  11.0 2.3 %collective-permute-start.7 = (bf16[8,1,64,128]{3,2,1,0:T(8,128)(2,1)S(1)}, bf16[8,1,64,128]{3,2,1,0:T(8,128)(2,1)S(1)}, u32[]{:S(2)}, u32[]{:S(2)}) collective-permute-start(bf16[8,1,64,128]{3,2,1,0:T(8,128)(2,1)S(1)} %get-tuple-element.74.x_ref), channel_id=1, source_target_pairs={{0,128},{8,136},{16,144},{24,152},{32,160},{40,168},{48,176},{56,1... | collective-permute-start | bytes 393224 | tf_op jit(solution)/shard_map/ppermute | solution.py:147
  13.3 0.3 collective-permute-done.1.y_ref
  13.5 0.3 shard_map.69
  13.8 0.1 collective-permute-start.6
  13.9 2.4 %collective-permute-done.y_ref = bf16[8,1,64,128]{3,2,1,0:T(8,128)(2,1)S(1)} collective-permute-done((bf16[8,1,64,128]{3,2,1,0:T(8,128)(2,1)S(1)}, bf16[8,1,64,128]{3,2,1,0:T(8,128)(2,1)S(1)}, u32[]{:S(2)}, u32[]{:S(2)}) %collective-permute-start) | collective-permute-done | bytes 131104 | tf_op jit(solution)/shard_map/ppermute | solution.py:147
  16.3 0.3 shard_map.70
  16.6 1.1 %collective-permute-done.4.y_ref = bf16[8,1,64,128]{3,2,1,0:T(8,128)(2,1)S(1)} collective-permute-done((bf16[8,1,64,128]{3,2,1,0:T(8,128)(2,1)S(1)}, bf16[8,1,64,128]{3,2,1,0:T(8,128)(2,1)S(1)}, u32[]{:S(2)}, u32[]{:S(2)}) %collective-permute-start.4) | collective-permute-done | bytes 131104 | tf_op jit(solution)/shard_map/ppermute | solution.py:147
  17.7 0.3 shard_map.71
  18.0 3.0 %collective-permute-start.5 = (bf16[8,1,64,128]{3,2,1,0:T(8,128)(2,1)S(1)}, bf16[8,1,64,128]{3,2,1,0:T(8,128)(2,1)S(1)}, u32[]{:S(2)}, u32[]{:S(2)}) collective-permute-start(bf16[8,1,64,128]{3,2,1,0:T(8,128)(2,1)S(1)} %get-tuple-element.72.x_ref), channel_id=1, source_target_pairs={{0,32},{8,40},{16,48},{24,56},{32,0},{40,8},{48,16},{56,24},{64,96... | collective-permute-start | bytes 393224 | tf_op jit(solution)/shard_map/ppermute | solution.py:147
  21.0 1.2 %collective-permute-start.3 = (bf16[8,1,64,128]{3,2,1,0:T(8,128)(2,1)S(1)}, bf16[8,1,64,128]{3,2,1,0:T(8,128)(2,1)S(1)}, u32[]{:S(2)}, u32[]{:S(2)}) collective-permute-start(bf16[8,1,64,128]{3,2,1,0:T(8,128)(2,1)S(1)} %get-tuple-element.69.x_ref), channel_id=1, source_target_pairs={{0,64},{8,72},{16,80},{24,88},{32,96},{40,104},{48,112},{56,120},{... | collective-permute-start | bytes 393224 | tf_op jit(solution)/shard_map/ppermute | solution.py:147
  22.2 0.3 shard_map.72
  22.5 0.8 %collective-permute-done.6.y_ref = bf16[8,1,64,128]{3,2,1,0:T(8,128)(2,1)S(1)} collective-permute-done((bf16[8,1,64,128]{3,2,1,0:T(8,128)(2,1)S(1)}, bf16[8,1,64,128]{3,2,1,0:T(8,128)(2,1)S(1)}, u32[]{:S(2)}, u32[]{:S(2)}) %collective-permute-start.6) | collective-permute-done | bytes 131104 | tf_op jit(solution)/shard_map/ppermute | solution.py:147
  23.3 0.3 shard_map.73
  23.7 3.0 %collective-permute-start.10 = (bf16[8,1,64,128]{3,2,1,0:T(8,128)(2,1)S(1)}, bf16[8,1,64,128]{3,2,1,0:T(8,128)(2,1)S(1)}, u32[]{:S(2)}, u32[]{:S(2)}) collective-permute-start(bf16[8,1,64,128]{3,2,1,0:T(8,128)(2,1)S(1)} %get-tuple-element.81.x_ref), channel_id=1, source_target_pairs={{0,32},{8,40},{16,48},{24,56},{32,0},{40,8},{48,16},{56,24},{64,96... | collective-permute-start | bytes 393224 | tf_op jit(solution)/shard_map/ppermute | solution.py:147
  26.6 1.1 %collective-permute-start.9 = (bf16[8,1,64,128]{3,2,1,0:T(8,128)(2,1)S(1)}, bf16[8,1,64,128]{3,2,1,0:T(8,128)(2,1)S(1)}, u32[]{:S(2)}, u32[]{:S(2)}) collective-permute-start(bf16[8,1,64,128]{3,2,1,0:T(8,128)(2,1)S(1)} %get-tuple-element.80.x_ref), channel_id=1, source_target_pairs={{0,64},{8,72},{16,80},{24,88},{32,96},{40,104},{48,112},{56,120},{... | collective-permute-start | bytes 393224 | tf_op jit(solution)/shard_map/ppermute | solution.py:147
  27.8 0.0 collective-permute-done.5.y_ref
  27.8 0.3 shard_map.74
  28.1 0.0 collective-permute-done.3.y_ref
  28.1 0.3 shard_map.75
  28.4 1.0 %collective-permute-start.8 = (bf16[8,1,64,128]{3,2,1,0:T(8,128)(2,1)S(1)}, bf16[8,1,64,128]{3,2,1,0:T(8,128)(2,1)S(1)}, u32[]{:S(2)}, u32[]{:S(2)}) collective-permute-start(bf16[8,1,64,128]{3,2,1,0:T(8,128)(2,1)S(1)} %get-tuple-element.79.x_ref), channel_id=1, source_target_pairs={{0,32},{8,40},{16,48},{24,56},{32,0},{40,8},{48,16},{56,24},{64,96... | collective-permute-start | bytes 393224 | tf_op jit(solution)/shard_map/ppermute | solution.py:147
  29.5 0.0 collective-permute-done.10.y_ref
  29.5 0.3 shard_map.76
  29.8 0.7 collective-permute-done.9.y_ref
  30.5 0.3 shard_map.77
  30.8 0.0 copy-start.3
  30.8 0.0 copy-start.5
  30.8 1.9 %collective-permute-start.11 = (bf16[8,1,64,128]{3,2,1,0:T(8,128)(2,1)S(1)}, bf16[8,1,64,128]{3,2,1,0:T(8,128)(2,1)S(1)}, u32[]{:S(2)}, u32[]{:S(2)}) collective-permute-start(bf16[8,1,64,128]{3,2,1,0:T(8,128)(2,1)S(1)} %get-tuple-element.89.x_ref), channel_id=1, source_target_pairs={{0,32},{8,40},{16,48},{24,56},{32,0},{40,8},{48,16},{56,24},{64,96... | collective-permute-start | bytes 393224 | tf_op jit(solution)/shard_map/ppermute | solution.py:147
  32.7 1.1 %collective-permute-done.8.y_ref = bf16[8,1,64,128]{3,2,1,0:T(8,128)(2,1)S(1)} collective-permute-done((bf16[8,1,64,128]{3,2,1,0:T(8,128)(2,1)S(1)}, bf16[8,1,64,128]{3,2,1,0:T(8,128)(2,1)S(1)}, u32[]{:S(2)}, u32[]{:S(2)}) %collective-permute-start.8) | collective-permute-done | bytes 131104 | tf_op jit(solution)/shard_map/ppermute | solution.py:147
  33.8 0.3 shard_map.78
  34.2 0.4 shard_map.79
  34.5 1.7 %collective-permute-done.11.y_ref = bf16[8,1,64,128]{3,2,1,0:T(8,128)(2,1)S(1)} collective-permute-done((bf16[8,1,64,128]{3,2,1,0:T(8,128)(2,1)S(1)}, bf16[8,1,64,128]{3,2,1,0:T(8,128)(2,1)S(1)}, u32[]{:S(2)}, u32[]{:S(2)}) %collective-permute-start.11) | collective-permute-done | bytes 131104 | tf_op jit(solution)/shard_map/ppermute | solution.py:147
  36.2 0.4 shard_map.80
  36.6 20.5 %all_to_all.5.x_ref = bf16[8,4,64,128]{3,2,1,0:T(8,128)(2,1)S(1)} all-to-all(bf16[8,4,64,128]{3,2,1,0:T(8,128)(2,1)S(1)} %get-tuple-element.94), channel_id=1, replica_groups=mesh['lvl'=32,'mid'=8] {'mid'}, dimensions={0} | all-to-all | bytes 1048576 | tf_op jit(solution)/shard_map/all_to_all | solution.py:182
  57.1 0.6 shard_map.81
  57.7 0.5 collective-permute-start.15
  58.2 0.6 shard_map.82
  58.8 1.3 %collective-permute-start.14 = (bf16[8,1,64,128]{3,2,1,0:T(8,128)(2,1)S(1)}, bf16[8,1,64,128]{3,2,1,0:T(8,128)(2,1)S(1)}, u32[]{:S(2)}, u32[]{:S(2)}) collective-permute-start(bf16[8,1,64,128]{3,2,1,0:T(8,128)(2,1)S(1)} %get-tuple-element.101.x_ref), channel_id=1, source_target_pairs={{0,16},{8,24},{16,0},{24,8},{32,48},{40,56},{48,32},{56,40},{64,80... | collective-permute-start | bytes 393224 | tf_op jit(solution)/shard_map/ppermute | solution.py:147
  60.1 0.6 shard_map.83
  60.7 0.5 collective-permute-start.13
  61.2 0.6 shard_map.84
  61.8 1.1 %collective-permute-start.12 = (bf16[8,1,64,128]{3,2,1,0:T(8,128)(2,1)S(1)}, bf16[8,1,64,128]{3,2,1,0:T(8,128)(2,1)S(1)}, u32[]{:S(2)}, u32[]{:S(2)}) collective-permute-start(bf16[8,1,64,128]{3,2,1,0:T(8,128)(2,1)S(1)} %get-tuple-element.99.x_ref), channel_id=1, source_target_pairs={{0,16},{8,24},{16,0},{24,8},{32,48},{40,56},{48,32},{56,40},{64,80... | collective-permute-start | bytes 393224 | tf_op jit(solution)/shard_map/ppermute | solution.py:147
  62.9 0.3 shard_map.85
  63.2 0.3 shard_map.86
  63.5 1.1 %collective-permute-done.13.y_ref = bf16[8,1,64,128]{3,2,1,0:T(8,128)(2,1)S(1)} collective-permute-done((bf16[8,1,64,128]{3,2,1,0:T(8,128)(2,1)S(1)}, bf16[8,1,64,128]{3,2,1,0:T(8,128)(2,1)S(1)}, u32[]{:S(2)}, u32[]{:S(2)}) %collective-permute-start.13) | collective-permute-done | bytes 131104 | tf_op jit(solution)/shard_map/ppermute | solution.py:147
  64.6 0.3 shard_map.87
  64.9 8.2 %collective-permute-start.18 = (bf16[8,1,64,128]{3,2,1,0:T(8,128)(2,1)S(1)}, bf16[8,1,64,128]{3,2,1,0:T(8,128)(2,1)S(1)}, u32[]{:S(2)}, u32[]{:S(2)}) collective-permute-start(bf16[8,1,64,128]{3,2,1,0:T(8,128)(2,1)S(1)} %get-tuple-element.110.refs_4_), channel_id=1, source_target_pairs={{0,8},{8,0},{16,24},{24,16},{32,40},{40,32},{48,56},{56,48},{64,72... | collective-permute-start | bytes 393224 | tf_op jit(solution)/shard_map/ppermute | solution.py:147
  73.1 0.1 collective-permute-start.17
  73.2 0.4 collective-permute-start.16
  73.6 0.0 collective-permute-done.12.y_ref
  73.6 0.3 shard_map.88
  73.9 0.8 %collective-permute-start.19 = (bf16[8,1,64,128]{3,2,1,0:T(8,128)(2,1)S(1)}, bf16[8,1,64,128]{3,2,1,0:T(8,128)(2,1)S(1)}, u32[]{:S(2)}, u32[]{:S(2)}) collective-permute-start(bf16[8,1,64,128]{3,2,1,0:T(8,128)(2,1)S(1)} %get-tuple-element.112.refs_0_), channel_id=1, source_target_pairs={{0,8},{8,0},{16,24},{24,16},{32,40},{40,32},{48,56},{56,48},{64,72... | collective-permute-start | bytes 393224 | tf_op jit(solution)/shard_map/ppermute | solution.py:147
  74.7 1.6 %shard_map.89 = (bf16[8,4,64,128]{3,2,1,0:T(8,128)(2,1)}, f32[8,128]{1,0:T(8,128)S(1)}) custom-call(bf16[2,8,4,64,256]{4,3,2,1,0:T(8,128)(2,1)S(1)} %get-tuple-element.86.w_ref, bf16[8,4,64,128]{3,2,1,0:T(8,128)(2,1)S(1)} %get-tuple-element.87.v_ref, f32[8,128]{1,0:T(8,128)S(1)} %get-tuple-element.107.t_ref, ...), custom_call_target="tpu_custom_call" | custom-call | flops 1 | bytes 1 | tf_op jit(solution)/shard_map/pallas_call | solution.py:121
  76.3 1.8 %shard_map.90 = (bf16[8,4,64,128]{3,2,1,0:T(8,128)(2,1)}, f32[8,128]{1,0:T(8,128)}) custom-call(bf16[2,8,4,64,256]{4,3,2,1,0:T(8,128)(2,1)S(1)} %get-tuple-element.86.w_ref, bf16[8,4,64,128]{3,2,1,0:T(8,128)(2,1)S(1)} %get-tuple-element.87.v_ref, f32[8,128]{1,0:T(8,128)S(1)} %get-tuple-element.111.t_ref, ...), custom_call_target="tpu_custom_call", output_to_operand_aliasing={{0}: (5, {})} | custom-call | flops 1 | bytes 1 | tf_op jit(solution)/shard_map/pallas_call | solution.py:121
  (17 shorter events, 0.0 us)
Async XLA Ops:
  0.0 1.0 %copy-start.1 = (bf16[32,64,128]{2,1,0:T(8,128)(2,1)S(1)}, bf16[32,64,128]{2,1,0:T(8,128)(2,1)}, u32[]{:S(2)}) copy-start(bf16[32,64,128]{2,1,0:T(8,128)(2,1)} %param.7) | copy-start | bytes 1572868
  1.0 1.0 %copy-start.2 = (bf16[32,64,128]{2,1,0:T(8,128)(2,1)S(1)}, bf16[32,64,128]{2,1,0:T(8,128)(2,1)}, u32[]{:S(2)}) copy-start(bf16[32,64,128]{2,1,0:T(8,128)(2,1)} %param.6) | copy-start | bytes 1572868
  2.1 8.2 %copy-start = (bf16[3,32,64,256]{3,2,1,0:T(8,128)(2,1)S(1)}, bf16[3,32,64,256]{3,2,1,0:T(8,128)(2,1)}, u32[]{:S(2)}) copy-start(bf16[3,32,64,256]{3,2,1,0:T(8,128)(2,1)} %param.8) | copy-start | bytes 9437188
  2.4 7.8 %collective-permute-start.2 = (bf16[8,1,64,128]{3,2,1,0:T(8,128)(2,1)S(1)}, bf16[8,1,64,128]{3,2,1,0:T(8,128)(2,1)S(1)}, u32[]{:S(2)}, u32[]{:S(2)}) collective-permute-start(bf16[8,1,64,128]{3,2,1,0:T(8,128)(2,1)S(1)} %get-tuple-element.64.x_ref), channel_id=1, source_target_pairs={{0,128},{8,136},{16,144},{24,152},{32,160},{40,168},{48,176},{56,1... | collective-permute-start | bytes 393224 | tf_op jit(solution)/shard_map/ppermute | solution.py:147
  6.4 7.1 %collective-permute-start.1 = (bf16[8,1,64,128]{3,2,1,0:T(8,128)(2,1)S(1)}, bf16[8,1,64,128]{3,2,1,0:T(8,128)(2,1)S(1)}, u32[]{:S(2)}, u32[]{:S(2)}) collective-permute-start(bf16[8,1,64,128]{3,2,1,0:T(8,128)(2,1)S(1)} %get-tuple-element.63.x_ref), channel_id=1, source_target_pairs={{0,128},{8,136},{16,144},{24,152},{32,160},{40,168},{48,176},{56,1... | collective-permute-start | bytes 393224 | tf_op jit(solution)/shard_map/ppermute | solution.py:147
  6.9 9.5 %collective-permute-start = (bf16[8,1,64,128]{3,2,1,0:T(8,128)(2,1)S(1)}, bf16[8,1,64,128]{3,2,1,0:T(8,128)(2,1)S(1)}, u32[]{:S(2)}, u32[]{:S(2)}) collective-permute-start(bf16[8,1,64,128]{3,2,1,0:T(8,128)(2,1)S(1)} %get-tuple-element.62.x_ref), channel_id=1, source_target_pairs={{0,128},{8,136},{16,144},{24,152},{32,160},{40,168},{48,176},{56,1... | collective-permute-start | bytes 393224 | tf_op jit(solution)/shard_map/ppermute | solution.py:147
  10.6 7.2 %collective-permute-start.4 = (bf16[8,1,64,128]{3,2,1,0:T(8,128)(2,1)S(1)}, bf16[8,1,64,128]{3,2,1,0:T(8,128)(2,1)S(1)}, u32[]{:S(2)}, u32[]{:S(2)}) collective-permute-start(bf16[8,1,64,128]{3,2,1,0:T(8,128)(2,1)S(1)} %get-tuple-element.70.x_ref), channel_id=1, source_target_pairs={{0,64},{8,72},{16,80},{24,88},{32,96},{40,104},{48,112},{56,120},{... | collective-permute-start | bytes 393224 | tf_op jit(solution)/shard_map/ppermute | solution.py:147
  11.0 11.2 %collective-permute-start.7 = (bf16[8,1,64,128]{3,2,1,0:T(8,128)(2,1)S(1)}, bf16[8,1,64,128]{3,2,1,0:T(8,128)(2,1)S(1)}, u32[]{:S(2)}, u32[]{:S(2)}) collective-permute-start(bf16[8,1,64,128]{3,2,1,0:T(8,128)(2,1)S(1)} %get-tuple-element.74.x_ref), channel_id=1, source_target_pairs={{0,128},{8,136},{16,144},{24,152},{32,160},{40,168},{48,176},{56,1... | collective-permute-start | bytes 393224 | tf_op jit(solution)/shard_map/ppermute | solution.py:147
  13.8 9.5 %collective-permute-start.6 = (bf16[8,1,64,128]{3,2,1,0:T(8,128)(2,1)S(1)}, bf16[8,1,64,128]{3,2,1,0:T(8,128)(2,1)S(1)}, u32[]{:S(2)}, u32[]{:S(2)}) collective-permute-start(bf16[8,1,64,128]{3,2,1,0:T(8,128)(2,1)S(1)} %get-tuple-element.73.x_ref), channel_id=1, source_target_pairs={{0,64},{8,72},{16,80},{24,88},{32,96},{40,104},{48,112},{56,120},{... | collective-permute-start | bytes 393224 | tf_op jit(solution)/shard_map/ppermute | solution.py:147
  18.0 9.8 %collective-permute-start.5 = (bf16[8,1,64,128]{3,2,1,0:T(8,128)(2,1)S(1)}, bf16[8,1,64,128]{3,2,1,0:T(8,128)(2,1)S(1)}, u32[]{:S(2)}, u32[]{:S(2)}) collective-permute-start(bf16[8,1,64,128]{3,2,1,0:T(8,128)(2,1)S(1)} %get-tuple-element.72.x_ref), channel_id=1, source_target_pairs={{0,32},{8,40},{16,48},{24,56},{32,0},{40,8},{48,16},{56,24},{64,96... | collective-permute-start | bytes 393224 | tf_op jit(solution)/shard_map/ppermute | solution.py:147
  21.0 7.1 %collective-permute-start.3 = (bf16[8,1,64,128]{3,2,1,0:T(8,128)(2,1)S(1)}, bf16[8,1,64,128]{3,2,1,0:T(8,128)(2,1)S(1)}, u32[]{:S(2)}, u32[]{:S(2)}) collective-permute-start(bf16[8,1,64,128]{3,2,1,0:T(8,128)(2,1)S(1)} %get-tuple-element.69.x_ref), channel_id=1, source_target_pairs={{0,64},{8,72},{16,80},{24,88},{32,96},{40,104},{48,112},{56,120},{... | collective-permute-start | bytes 393224 | tf_op jit(solution)/shard_map/ppermute | solution.py:147
  23.7 5.8 %collective-permute-start.10 = (bf16[8,1,64,128]{3,2,1,0:T(8,128)(2,1)S(1)}, bf16[8,1,64,128]{3,2,1,0:T(8,128)(2,1)S(1)}, u32[]{:S(2)}, u32[]{:S(2)}) collective-permute-start(bf16[8,1,64,128]{3,2,1,0:T(8,128)(2,1)S(1)} %get-tuple-element.81.x_ref), channel_id=1, source_target_pairs={{0,32},{8,40},{16,48},{24,56},{32,0},{40,8},{48,16},{56,24},{64,96... | collective-permute-start | bytes 393224 | tf_op jit(solution)/shard_map/ppermute | solution.py:147
  26.6 3.8 %collective-permute-start.9 = (bf16[8,1,64,128]{3,2,1,0:T(8,128)(2,1)S(1)}, bf16[8,1,64,128]{3,2,1,0:T(8,128)(2,1)S(1)}, u32[]{:S(2)}, u32[]{:S(2)}) collective-permute-start(bf16[8,1,64,128]{3,2,1,0:T(8,128)(2,1)S(1)} %get-tuple-element.80.x_ref), channel_id=1, source_target_pairs={{0,64},{8,72},{16,80},{24,88},{32,96},{40,104},{48,112},{56,120},{... | collective-permute-start | bytes 393224 | tf_op jit(solution)/shard_map/ppermute | solution.py:147
  28.4 5.4 %collective-permute-start.8 = (bf16[8,1,64,128]{3,2,1,0:T(8,128)(2,1)S(1)}, bf16[8,1,64,128]{3,2,1,0:T(8,128)(2,1)S(1)}, u32[]{:S(2)}, u32[]{:S(2)}) collective-permute-start(bf16[8,1,64,128]{3,2,1,0:T(8,128)(2,1)S(1)} %get-tuple-element.79.x_ref), channel_id=1, source_target_pairs={{0,32},{8,40},{16,48},{24,56},{32,0},{40,8},{48,16},{56,24},{64,96... | collective-permute-start | bytes 393224 | tf_op jit(solution)/shard_map/ppermute | solution.py:147
  30.5 3.7 %copy-start.4 = (bf16[2,32,64,256]{3,2,1,0:T(8,128)(2,1)S(1)}, bf16[2,32,64,256]{3,2,1,0:T(8,128)(2,1)}, u32[]{:S(2)}) copy-start(bf16[2,32,64,256]{3,2,1,0:T(8,128)(2,1)} %param.10) | copy-start | bytes 6291460
  30.8 3.4 %copy-start.3 = (bf16[2,32,64,256]{3,2,1,0:T(8,128)(2,1)S(1)}, bf16[2,32,64,256]{3,2,1,0:T(8,128)(2,1)}, u32[]{:S(2)}) copy-start(bf16[2,32,64,256]{3,2,1,0:T(8,128)(2,1)} %param.9) | copy-start | bytes 6291460
  30.8 3.4 %copy-start.5 = (bf16[32,64,128]{2,1,0:T(8,128)(2,1)S(1)}, bf16[32,64,128]{2,1,0:T(8,128)(2,1)}, u32[]{:S(2)}) copy-start(bf16[32,64,128]{2,1,0:T(8,128)(2,1)} %param.11) | copy-start | bytes 1572868
  30.8 5.4 %collective-permute-start.11 = (bf16[8,1,64,128]{3,2,1,0:T(8,128)(2,1)S(1)}, bf16[8,1,64,128]{3,2,1,0:T(8,128)(2,1)S(1)}, u32[]{:S(2)}, u32[]{:S(2)}) collective-permute-start(bf16[8,1,64,128]{3,2,1,0:T(8,128)(2,1)S(1)} %get-tuple-element.89.x_ref), channel_id=1, source_target_pairs={{0,32},{8,40},{16,48},{24,56},{32,0},{40,8},{48,16},{56,24},{64,96... | collective-permute-start | bytes 393224 | tf_op jit(solution)/shard_map/ppermute | solution.py:147
  57.7 5.3 %collective-permute-start.15 = (bf16[8,1,64,128]{3,2,1,0:T(8,128)(2,1)S(1)}, bf16[8,1,64,128]{3,2,1,0:T(8,128)(2,1)S(1)}, u32[]{:S(2)}, u32[]{:S(2)}) collective-permute-start(bf16[8,1,64,128]{3,2,1,0:T(8,128)(2,1)S(1)} %get-tuple-element.102.x_ref), channel_id=1, source_target_pairs={{0,16},{8,24},{16,0},{24,8},{32,48},{40,56},{48,32},{56,40},{64,80... | collective-permute-start | bytes 393224 | tf_op jit(solution)/shard_map/ppermute | solution.py:147
  58.8 4.4 %collective-permute-start.14 = (bf16[8,1,64,128]{3,2,1,0:T(8,128)(2,1)S(1)}, bf16[8,1,64,128]{3,2,1,0:T(8,128)(2,1)S(1)}, u32[]{:S(2)}, u32[]{:S(2)}) collective-permute-start(bf16[8,1,64,128]{3,2,1,0:T(8,128)(2,1)S(1)} %get-tuple-element.101.x_ref), channel_id=1, source_target_pairs={{0,16},{8,24},{16,0},{24,8},{32,48},{40,56},{48,32},{56,40},{64,80... | collective-permute-start | bytes 393224 | tf_op jit(solution)/shard_map/ppermute | solution.py:147
  60.7 3.9 %collective-permute-start.13 = (bf16[8,1,64,128]{3,2,1,0:T(8,128)(2,1)S(1)}, bf16[8,1,64,128]{3,2,1,0:T(8,128)(2,1)S(1)}, u32[]{:S(2)}, u32[]{:S(2)}) collective-permute-start(bf16[8,1,64,128]{3,2,1,0:T(8,128)(2,1)S(1)} %get-tuple-element.100.x_ref), channel_id=1, source_target_pairs={{0,16},{8,24},{16,0},{24,8},{32,48},{40,56},{48,32},{56,40},{64,80... | collective-permute-start | bytes 393224 | tf_op jit(solution)/shard_map/ppermute | solution.py:147
  61.8 11.8 %collective-permute-start.12 = (bf16[8,1,64,128]{3,2,1,0:T(8,128)(2,1)S(1)}, bf16[8,1,64,128]{3,2,1,0:T(8,128)(2,1)S(1)}, u32[]{:S(2)}, u32[]{:S(2)}) collective-permute-start(bf16[8,1,64,128]{3,2,1,0:T(8,128)(2,1)S(1)} %get-tuple-element.99.x_ref), channel_id=1, source_target_pairs={{0,16},{8,24},{16,0},{24,8},{32,48},{40,56},{48,32},{56,40},{64,80... | collective-permute-start | bytes 393224 | tf_op jit(solution)/shard_map/ppermute | solution.py:147
  64.9 9.8 %collective-permute-start.18 = (bf16[8,1,64,128]{3,2,1,0:T(8,128)(2,1)S(1)}, bf16[8,1,64,128]{3,2,1,0:T(8,128)(2,1)S(1)}, u32[]{:S(2)}, u32[]{:S(2)}) collective-permute-start(bf16[8,1,64,128]{3,2,1,0:T(8,128)(2,1)S(1)} %get-tuple-element.110.refs_4_), channel_id=1, source_target_pairs={{0,8},{8,0},{16,24},{24,16},{32,40},{40,32},{48,56},{56,48},{64,72... | collective-permute-start | bytes 393224 | tf_op jit(solution)/shard_map/ppermute | solution.py:147
  73.1 1.6 %collective-permute-start.17 = (bf16[8,1,64,128]{3,2,1,0:T(8,128)(2,1)S(1)}, bf16[8,1,64,128]{3,2,1,0:T(8,128)(2,1)S(1)}, u32[]{:S(2)}, u32[]{:S(2)}) collective-permute-start(bf16[8,1,64,128]{3,2,1,0:T(8,128)(2,1)S(1)} %get-tuple-element.109.refs_2_), channel_id=1, source_target_pairs={{0,8},{8,0},{16,24},{24,16},{32,40},{40,32},{48,56},{56,48},{64,72... | collective-permute-start | bytes 393224 | tf_op jit(solution)/shard_map/ppermute | solution.py:147
  73.2 1.5 %collective-permute-start.16 = (bf16[8,1,64,128]{3,2,1,0:T(8,128)(2,1)S(1)}, bf16[8,1,64,128]{3,2,1,0:T(8,128)(2,1)S(1)}, u32[]{:S(2)}, u32[]{:S(2)}) collective-permute-start(bf16[8,1,64,128]{3,2,1,0:T(8,128)(2,1)S(1)} %get-tuple-element.108.refs_0_), channel_id=1, source_target_pairs={{0,8},{8,0},{16,24},{24,16},{32,40},{40,32},{48,56},{56,48},{64,72... | collective-permute-start | bytes 393224 | tf_op jit(solution)/shard_map/ppermute | solution.py:147
  73.9 2.4 %collective-permute-start.19 = (bf16[8,1,64,128]{3,2,1,0:T(8,128)(2,1)S(1)}, bf16[8,1,64,128]{3,2,1,0:T(8,128)(2,1)S(1)}, u32[]{:S(2)}, u32[]{:S(2)}) collective-permute-start(bf16[8,1,64,128]{3,2,1,0:T(8,128)(2,1)S(1)} %get-tuple-element.112.refs_0_), channel_id=1, source_target_pairs={{0,8},{8,0},{16,24},{24,16},{32,40},{40,32},{48,56},{56,48},{64,72... | collective-permute-start | bytes 393224 | tf_op jit(solution)/shard_map/ppermute | solution.py:147

commit v2 on v1

--- a/solution.py
+++ b/solution.py
@@ -11,14 +11,14 @@
 GROUPS = ((0, 1, 2, 3),)
 LEAF_LIMIT = 8 << 20
 PLAN = (
-    "L0", "L1", "L2", "L3", "U00", "U01", "U02", "U10", "U03", "U11", "U20", "U12", "U21", "U13",
+    "T0", "L0", "L1", "L2", "L3", "U00", "U01", "U02", "U03", "U10", "U11", "U12", "U13", "U20", "U21",
     "U22", "W0", "U23", "M0", "M1", "M2", "M3", "D00", "D01", "D02", "D03", "E012", "E3",
 )
 VMEM = pl.BlockSpec(memory_space=pltpu.VMEM)
 ANY = pl.BlockSpec(memory_space=pl.ANY)
 DMA = pltpu.SemaphoreType.DMA
 TOKEN = jax.ShapeDtypeStruct((8, 128), jnp.float32)
-COST = {"L": 0, "W": 0, "U0": 0, "U1": 0, "U2": 0, "M": 0, "D0": 0, "D1": 0}
+COST = {"T0": 100}
 
 
 def turn(piece):
@@ -31,6 +31,10 @@
 def product(weights, parts):
     stacked = jnp.concatenate(list(parts) + [turn(p) for p in parts], axis=0)
     return jnp.dot(weights, stacked, preferred_element_type=jnp.float32).astype(jnp.bfloat16)
+
+
+def token_kernel(t_ref, u_ref):
+    u_ref[...] = t_ref[...]
 
 
 def leaf_kernel(first, w_ref, x_ref, t_ref, o_ref, u_ref, ws_ref, xs_ref, sems):
@@ -99,20 +103,32 @@
             o_ref[a, b] = product(w_ref[1, a, first + b], [s_ref[a, b], s_ref[a ^ (count // 4), b]])
 
 
-def last_group_kernel(step, firsts, w_ref, v_ref, t_ref, *refs):
-    o_ref, u_ref, r_ref, sems = refs[-4:]
-    u_ref[...] = t_ref[...]
+def finish(step, first, w_ref, v_ref, x_ref, y_ref, r_ref, at):
+    for a in range(x_ref.shape[0]):
+        for b in range(x_ref.shape[1]):
+            value = product(w_ref[step, a, first + b], [x_ref[a, b], y_ref[a, b]])
+            r_ref[a, at + b] = product(v_ref[a, first + b], [value])
+
+
+def finish_kernel(step, firsts, w_ref, v_ref, t_ref, *refs):
+    r_ref, u_ref = refs[-2:]
+    u_ref[...] = t_ref[...]
+    for c, first in enumerate(firsts):
+        finish(step, first, w_ref, v_ref, refs[2 * c], refs[2 * c + 1], r_ref, first - firsts[0])
+
+
+def store_kernel(step, first, w_ref, v_ref, t_ref, x_ref, y_ref, *refs):
+    *earlier, o_ref, r_ref, sems = refs
     stores = []
-    for c, first in enumerate(firsts):
-        x_ref, y_ref = refs[2 * c], refs[2 * c + 1]
-        width = x_ref.shape[1]
-        for a in range(x_ref.shape[0]):
-            for b in range(width):
-                value = product(w_ref[step, a, first + b], [x_ref[a, b], y_ref[a, b]])
-                r_ref[a, first + b] = product(v_ref[a, first + b], [value])
-        store = pltpu.make_async_copy(r_ref.at[:, first:first + width], o_ref.at[:, first:first + width], sems.at[c])
+    at = 0
+    for e_ref in earlier:
+        stores.append(pltpu.make_async_copy(e_ref, o_ref.at[:, at:at + e_ref.shape[1]], sems.at[len(stores)]))
+        at += e_ref.shape[1]
+    for store in stores:
         store.start()
-        stores.append(store)
+    finish(step, first, w_ref, v_ref, x_ref, y_ref, r_ref, 0)
+    stores.append(pltpu.make_async_copy(r_ref, o_ref.at[:, first:first + x_ref.shape[1]], sems.at[len(stores)]))
+    stores[-1].start()
     for store in stores:
         store.wait()
 
@@ -124,7 +140,7 @@
         in_specs=specs,
         out_specs=list(out_specs) + [VMEM],
         compiler_params=pltpu.CompilerParams(vmem_limit_bytes=limit),
-        cost_estimate=pl.CostEstimate(flops=1 + int(COST[kind] * 1e9), bytes_accessed=1, transcendentals=0),
+        cost_estimate=pl.CostEstimate(flops=1 + int(COST.get(kind, 0) * 1e9), bytes_accessed=1, transcendentals=0),
         **kw,
     )(*args)
     return outs, token
@@ -148,17 +164,18 @@
 
     field, other, place = {}, {}, {}
     token = jnp.zeros(TOKEN.shape, TOKEN.dtype)
-    result = None
+    result, finished = None, []
     lower_count = lower_w.shape[0]
     upper_count = upper_w.shape[0]
     for item in PLAN:
         kind, c = item[0], int(item[-1])
         step = int(item[1])
-        name = item[:-1] if kind in "UD" else kind
-        name = name if item not in COST else item
+        name = item
         first, shape = firsts[c], shapes[c]
         block = pltpu.VMEM(shape, jnp.bfloat16)
-        if kind == "W":
+        if kind == "T":
+            _, token = call(name, token_kernel, [], (token,), [VMEM], [], token)
+        elif kind == "W":
             staged = (mid_w, low_w, out_w)
             (mid_w, low_w, out_w), token = call(name, stage_kernel, [v.shape for v in staged], (token, *staged),
                                                       [VMEM] + [ANY] * 3, [VMEM] * 3, token, scratch_shapes=[DMA((3,))])
@@ -192,15 +209,24 @@
             (field[c],), token = call(name, part(level_kernel, first, step), [shape], (low_w, field[c], other[c], token),
                                       [VMEM] * 4, [VMEM], token)
             other[c] = swap(field[c], lower_count - 2 - step)
-        elif kind == "E":
+        elif kind == "E" and item != PLAN[-1]:
             chosen = [int(e) for e in item[1:]]
             pairs = [v for e in chosen for v in (field[e], other[e])]
-            args, specs, alias = (low_w, out_w, token, *pairs), [VMEM] * (3 + len(pairs)), {}
-            if result is not None:
-                args, specs, alias = args + (result,), specs + [ANY], {len(args): 0}
-            (result,), token = call("D1", part(last_group_kernel, lower_count - 1, [firsts[e] for e in chosen]),
-                                    [samples.shape], args, specs, [ANY], token, input_output_aliases=alias,
-                                    scratch_shapes=[pltpu.VMEM(samples.shape, jnp.bfloat16), DMA((len(chosen),))])
+            whole = (mid_size, sum(WIDTHS[e] for e in chosen)) + box
+            (done,), token = call(name, part(finish_kernel, lower_count - 1, [firsts[e] for e in chosen]), [whole],
+                                  (low_w, out_w, token, *pairs), [VMEM] * (3 + len(pairs)), [VMEM], token)
+            finished.append(done)
+        elif kind == "E":
+            args = (low_w, out_w, token, field[c], other[c], *finished)
+            result = pl.pallas_call(
+                part(store_kernel, lower_count - 1, first),
+                out_shape=jax.ShapeDtypeStruct(samples.shape, jnp.bfloat16),
+                in_specs=[VMEM] * len(args),
+                out_specs=ANY,
+                scratch_shapes=[block, DMA((1 + len(finished),))],
+                compiler_params=pltpu.CompilerParams(vmem_limit_bytes=8 << 20),
+                cost_estimate=pl.CostEstimate(flops=1, bytes_accessed=1, transcendentals=0),
+            )(*args)
     return result.reshape(signal.shape)
 
 

time: 78.5 us -> 76.6 us (0.976)
  starting transfers between devices: 33.8 us -> 30.4 us
  waiting for transfers between devices: 9.17 us -> 11 us
  Pallas kernels: 12.3 us -> 11 us
  blocking collectives: 20.5 us -> 21.3 us
    ppermute x20, starting transfers between devices: 33.8 us -> 30.4 us  [swap(): lax.ppermute(block, 'lvl', [(i, i ^ 1 << bit) for i in range(lvl_size)])]
    pallas_call x27, Pallas kernels: 12.3 us -> 9.74 us  [call(): pl.pallas_call(kernel, out_shape=[jax.ShapeDtypeStruct(shape, jnp.bfloat1...]
    ppermute x20, waiting for transfers between devices: 9.17 us -> 11 us  [swap(): lax.ppermute(block, 'lvl', [(i, i ^ 1 << bit) for i in range(lvl_size)])]
    pallas_call x0 -> x1, Pallas kernels: none -> 1.21 us  [on_device(): pl.pallas_call(part(store_kernel, lower_count - 1, first), out_shape=jax....]
    all_to_all x1, blocking collectives: 20.5 us -> 21.3 us  [on_device(): lax.all_to_all(joined, 'mid', split_axis=0, concat_axis=0, tiled=True)]
  transfers between devices with their start and end apart: 20 -> 20, of which waited for: 8 -> 9; matrix products, arithmetic and copies ran while one was open for 0% -> 0% of each run, Pallas kernels for 12% -> 11%
where the time goes in v2:
time: 76.6 us; the launch traced here: 76.5 us
  starting transfers between devices  30.4 us (40%)
  blocking collectives  21.3 us (28%)
  Pallas kernels  11 us (14%)
  waiting for transfers between devices  11 us (14%)
  local copies, waits for them, and re-layouts  2.37 us (3%)
    ppermute x20, starting transfers between devices, swap(): lax.ppermute(block, 'lvl', [(i, i ^ 1 << bit) for i in range(lvl_size)])  30.4 us
    all_to_all x1, blocking collectives, on_device(): lax.all_to_all(joined, 'mid', split_axis=0, concat_axis=0, tiled=True)  21.3 us
    ppermute x20, waiting for transfers between devices, swap(): lax.ppermute(block, 'lvl', [(i, i ^ 1 << bit) for i in range(lvl_size)])  11 us
    pallas_call x27, Pallas kernels, call(): pl.pallas_call(kernel, out_shape=[jax.ShapeDtypeStruct(shape, jnp.bfloat1...  9.74 us
    unnamed x12, local copies, waits for them, and re-layouts  2.36 us
  transfers between devices with their start and end apart: 20, of which 9 were waited for; matrix products, arithmetic and copies ran while one was open for 0% of the time, Pallas kernels for 11%

profile of v2, /device:TPU:1, one launch (start us, length us, event | category | flops | bytes accessed | tf_op | source)
XLA Modules:
  0.0 76.5 jit_solution(14178471859537067194)
XLA Ops:
  0.0 1.0 %copy-done.1 = bf16[32,64,128]{2,1,0:T(8,128)(2,1)S(1)} copy-done((bf16[32,64,128]{2,1,0:T(8,128)(2,1)S(1)}, bf16[32,64,128]{2,1,0:T(8,128)(2,1)}, u32[]{:S(2)}) %copy-start.1) | copy-done | bytes 524312
  1.0 0.2 copy-done.2
  1.2 0.3 shard_map.65
  1.5 3.7 %collective-permute-start.2 = (bf16[8,1,64,128]{3,2,1,0:T(8,128)(2,1)S(1)}, bf16[8,1,64,128]{3,2,1,0:T(8,128)(2,1)S(1)}, u32[]{:S(2)}, u32[]{:S(2)}) collective-permute-start(bf16[8,1,64,128]{3,2,1,0:T(8,128)(2,1)S(1)} %get-tuple-element.63.x_ref), channel_id=1, source_target_pairs={{0,128},{8,136},{16,144},{24,152},{32,160},{40,168},{48,176},{56,1... | collective-permute-start | bytes 393224 | tf_op jit(solution)/shard_map/ppermute | solution.py:163
  5.2 0.3 shard_map.66
  5.5 0.1 collective-permute-start.1
  5.6 0.3 shard_map.67
  6.0 3.0 %collective-permute-start = (bf16[8,1,64,128]{3,2,1,0:T(8,128)(2,1)S(1)}, bf16[8,1,64,128]{3,2,1,0:T(8,128)(2,1)S(1)}, u32[]{:S(2)}, u32[]{:S(2)}) collective-permute-start(bf16[8,1,64,128]{3,2,1,0:T(8,128)(2,1)S(1)} %get-tuple-element.61.x_ref), channel_id=1, source_target_pairs={{0,128},{8,136},{16,144},{24,152},{32,160},{40,168},{48,176},{56,1... | collective-permute-start | bytes 393224 | tf_op jit(solution)/shard_map/ppermute | solution.py:163
  9.0 0.3 shard_map.68
  9.4 0.1 collective-permute-start.6
  9.5 0.3 shard_map.69
  9.8 1.5 %collective-permute-start.5 = (bf16[8,1,64,128]{3,2,1,0:T(8,128)(2,1)S(1)}, bf16[8,1,64,128]{3,2,1,0:T(8,128)(2,1)S(1)}, u32[]{:S(2)}, u32[]{:S(2)}) collective-permute-start(bf16[8,1,64,128]{3,2,1,0:T(8,128)(2,1)S(1)} %get-tuple-element.70.x_ref), channel_id=1, source_target_pairs={{0,64},{8,72},{16,80},{24,88},{32,96},{40,104},{48,112},{56,120},{... | collective-permute-start | bytes 393224 | tf_op jit(solution)/shard_map/ppermute | solution.py:163
  11.3 1.4 %collective-permute-done.1.y_ref = bf16[8,1,64,128]{3,2,1,0:T(8,128)(2,1)S(1)} collective-permute-done((bf16[8,1,64,128]{3,2,1,0:T(8,128)(2,1)S(1)}, bf16[8,1,64,128]{3,2,1,0:T(8,128)(2,1)S(1)}, u32[]{:S(2)}, u32[]{:S(2)}) %collective-permute-start.1) | collective-permute-done | bytes 131104 | tf_op jit(solution)/shard_map/ppermute | solution.py:163
  12.6 0.3 shard_map.70
  12.9 0.1 collective-permute-start.4
  13.0 2.4 %collective-permute-done.y_ref = bf16[8,1,64,128]{3,2,1,0:T(8,128)(2,1)S(1)} collective-permute-done((bf16[8,1,64,128]{3,2,1,0:T(8,128)(2,1)S(1)}, bf16[8,1,64,128]{3,2,1,0:T(8,128)(2,1)S(1)}, u32[]{:S(2)}, u32[]{:S(2)}) %collective-permute-start) | collective-permute-done | bytes 131104 | tf_op jit(solution)/shard_map/ppermute | solution.py:163
  15.5 0.3 shard_map.71
  15.8 0.1 collective-permute-start.3
  15.9 2.4 %collective-permute-done.6.y_ref = bf16[8,1,64,128]{3,2,1,0:T(8,128)(2,1)S(1)} collective-permute-done((bf16[8,1,64,128]{3,2,1,0:T(8,128)(2,1)S(1)}, bf16[8,1,64,128]{3,2,1,0:T(8,128)(2,1)S(1)}, u32[]{:S(2)}, u32[]{:S(2)}) %collective-permute-start.6) | collective-permute-done | bytes 131104 | tf_op jit(solution)/shard_map/ppermute | solution.py:163
  18.3 0.3 shard_map.72
  18.6 0.1 collective-permute-start.10
  18.7 1.0 %collective-permute-done.5.y_ref = bf16[8,1,64,128]{3,2,1,0:T(8,128)(2,1)S(1)} collective-permute-done((bf16[8,1,64,128]{3,2,1,0:T(8,128)(2,1)S(1)}, bf16[8,1,64,128]{3,2,1,0:T(8,128)(2,1)S(1)}, u32[]{:S(2)}, u32[]{:S(2)}) %collective-permute-start.5) | collective-permute-done | bytes 131104 | tf_op jit(solution)/shard_map/ppermute | solution.py:163
  19.6 0.3 shard_map.73
  20.0 3.0 %collective-permute-start.9 = (bf16[8,1,64,128]{3,2,1,0:T(8,128)(2,1)S(1)}, bf16[8,1,64,128]{3,2,1,0:T(8,128)(2,1)S(1)}, u32[]{:S(2)}, u32[]{:S(2)}) collective-permute-start(bf16[8,1,64,128]{3,2,1,0:T(8,128)(2,1)S(1)} %get-tuple-element.78.x_ref), channel_id=1, source_target_pairs={{0,32},{8,40},{16,48},{24,56},{32,0},{40,8},{48,16},{56,24},{64,96... | collective-permute-start | bytes 393224 | tf_op jit(solution)/shard_map/ppermute | solution.py:163
  23.0 0.3 shard_map.74
  23.3 2.5 %collective-permute-start.8 = (bf16[8,1,64,128]{3,2,1,0:T(8,128)(2,1)S(1)}, bf16[8,1,64,128]{3,2,1,0:T(8,128)(2,1)S(1)}, u32[]{:S(2)}, u32[]{:S(2)}) collective-permute-start(bf16[8,1,64,128]{3,2,1,0:T(8,128)(2,1)S(1)} %get-tuple-element.77.x_ref), channel_id=1, source_target_pairs={{0,32},{8,40},{16,48},{24,56},{32,0},{40,8},{48,16},{56,24},{64,96... | collective-permute-start | bytes 393224 | tf_op jit(solution)/shard_map/ppermute | solution.py:163
  25.8 0.3 shard_map.75
  26.1 2.5 %collective-permute-start.7 = (bf16[8,1,64,128]{3,2,1,0:T(8,128)(2,1)S(1)}, bf16[8,1,64,128]{3,2,1,0:T(8,128)(2,1)S(1)}, u32[]{:S(2)}, u32[]{:S(2)}) collective-permute-start(bf16[8,1,64,128]{3,2,1,0:T(8,128)(2,1)S(1)} %get-tuple-element.76.x_ref), channel_id=1, source_target_pairs={{0,32},{8,40},{16,48},{24,56},{32,0},{40,8},{48,16},{56,24},{64,96... | collective-permute-start | bytes 393224 | tf_op jit(solution)/shard_map/ppermute | solution.py:163
  28.6 0.3 shard_map.76
  28.9 2.5 %collective-permute-start.11 = (bf16[8,1,64,128]{3,2,1,0:T(8,128)(2,1)S(1)}, bf16[8,1,64,128]{3,2,1,0:T(8,128)(2,1)S(1)}, u32[]{:S(2)}, u32[]{:S(2)}) collective-permute-start(bf16[8,1,64,128]{3,2,1,0:T(8,128)(2,1)S(1)} %get-tuple-element.88.x_ref), channel_id=1, source_target_pairs={{0,32},{8,40},{16,48},{24,56},{32,0},{40,8},{48,16},{56,24},{64,96... | collective-permute-start | bytes 393224 | tf_op jit(solution)/shard_map/ppermute | solution.py:163
  31.4 0.3 shard_map.77
  31.7 0.0 copy-start.4
  31.7 0.3 shard_map.78
  32.0 0.0 copy-start.5
  32.0 0.6 collective-permute-done.7.y_ref
  32.6 0.3 shard_map.79
  32.9 0.4 copy-done.4
  33.3 0.7 copy-done.3
  34.0 0.1 copy-done.5
  34.1 0.3 shard_map.80
  34.4 1.0 %collective-permute-done.11.y_ref = bf16[8,1,64,128]{3,2,1,0:T(8,128)(2,1)S(1)} collective-permute-done((bf16[8,1,64,128]{3,2,1,0:T(8,128)(2,1)S(1)}, bf16[8,1,64,128]{3,2,1,0:T(8,128)(2,1)S(1)}, u32[]{:S(2)}, u32[]{:S(2)}) %collective-permute-start.11) | collective-permute-done | bytes 131104 | tf_op jit(solution)/shard_map/ppermute | solution.py:163
  35.4 0.4 shard_map.81
  35.8 21.3 %all_to_all.5.x_ref = bf16[8,4,64,128]{3,2,1,0:T(8,128)(2,1)S(1)} all-to-all(bf16[8,4,64,128]{3,2,1,0:T(8,128)(2,1)S(1)} %get-tuple-element.93), channel_id=1, replica_groups=mesh['lvl'=32,'mid'=8] {'mid'}, dimensions={0} | all-to-all | bytes 1048576 | tf_op jit(solution)/shard_map/all_to_all | solution.py:199
  57.1 0.6 shard_map.82
  57.7 2.2 %collective-permute-start.15 = (bf16[8,1,64,128]{3,2,1,0:T(8,128)(2,1)S(1)}, bf16[8,1,64,128]{3,2,1,0:T(8,128)(2,1)S(1)}, u32[]{:S(2)}, u32[]{:S(2)}) collective-permute-start(bf16[8,1,64,128]{3,2,1,0:T(8,128)(2,1)S(1)} %get-tuple-element.101.x_ref), channel_id=1, source_target_pairs={{0,16},{8,24},{16,0},{24,8},{32,48},{40,56},{48,32},{56,40},{64,80... | collective-permute-start | bytes 393224 | tf_op jit(solution)/shard_map/ppermute | solution.py:163
  59.9 0.6 shard_map.83
  60.5 0.3 collective-permute-start.14
  60.8 0.6 shard_map.84
  61.4 1.5 %collective-permute-start.13 = (bf16[8,1,64,128]{3,2,1,0:T(8,128)(2,1)S(1)}, bf16[8,1,64,128]{3,2,1,0:T(8,128)(2,1)S(1)}, u32[]{:S(2)}, u32[]{:S(2)}) collective-permute-start(bf16[8,1,64,128]{3,2,1,0:T(8,128)(2,1)S(1)} %get-tuple-element.99.x_ref), channel_id=1, source_target_pairs={{0,16},{8,24},{16,0},{24,8},{32,48},{40,56},{48,32},{56,40},{64,80... | collective-permute-start | bytes 393224 | tf_op jit(solution)/shard_map/ppermute | solution.py:163
  62.9 0.6 shard_map.85
  63.5 0.1 collective-permute-start.12
  63.6 0.3 shard_map.86
  63.9 0.7 collective-permute-done.14.y_ref
  64.6 0.3 shard_map.87
  64.9 1.5 %collective-permute-done.13.y_ref = bf16[8,1,64,128]{3,2,1,0:T(8,128)(2,1)S(1)} collective-permute-done((bf16[8,1,64,128]{3,2,1,0:T(8,128)(2,1)S(1)}, bf16[8,1,64,128]{3,2,1,0:T(8,128)(2,1)S(1)}, u32[]{:S(2)}, u32[]{:S(2)}) %collective-permute-start.13) | collective-permute-done | bytes 131104 | tf_op jit(solution)/shard_map/ppermute | solution.py:163
  66.4 0.3 shard_map.88
  66.7 6.0 %collective-permute-start.18 = (bf16[8,1,64,128]{3,2,1,0:T(8,128)(2,1)S(1)}, bf16[8,1,64,128]{3,2,1,0:T(8,128)(2,1)S(1)}, u32[]{:S(2)}, u32[]{:S(2)}) collective-permute-start(bf16[8,1,64,128]{3,2,1,0:T(8,128)(2,1)S(1)} %get-tuple-element.109.refs_4_), channel_id=1, source_target_pairs={{0,8},{8,0},{16,24},{24,16},{32,40},{40,32},{48,56},{56,48},{64,72... | collective-permute-start | bytes 393224 | tf_op jit(solution)/shard_map/ppermute | solution.py:163
  72.7 0.1 collective-permute-start.17
  72.8 0.4 collective-permute-start.16
  73.2 0.3 shard_map.89
  73.5 0.6 collective-permute-start.19
  74.1 0.1 collective-permute-done.16.refs_1_
  74.2 0.9 %shard_map.90 = (bf16[8,3,64,128]{3,2,1,0:T(8,128)(2,1)S(1)}, f32[8,128]{1,0:T(8,128)S(1)}) custom-call(bf16[2,8,4,64,256]{4,3,2,1,0:T(8,128)(2,1)S(1)} %get-tuple-element.85.w_ref, bf16[8,4,64,128]{3,2,1,0:T(8,128)(2,1)S(1)} %get-tuple-element.86.v_ref, f32[8,128]{1,0:T(8,128)S(1)} %get-tuple-element.106.t_ref, ...), custom_call_target="tpu_custom_call" | custom-call | flops 1 | bytes 1 | tf_op jit(solution)/shard_map/pallas_call | solution.py:137
  75.1 1.2 %shard_map.91 = bf16[8,4,64,128]{3,2,1,0:T(8,128)(2,1)} custom-call(bf16[2,8,4,64,256]{4,3,2,1,0:T(8,128)(2,1)S(1)} %get-tuple-element.85.w_ref, bf16[8,4,64,128]{3,2,1,0:T(8,128)(2,1)S(1)} %get-tuple-element.86.v_ref, f32[8,128]{1,0:T(8,128)S(1)} %get-tuple-element.110.t_ref, bf16[8,1,64,128]{3,2,1,0:T(8,128)(2,1)S(1)} %get-tuple-element.111.x_ref, ...), custom_call_target="tpu_custom_call" | custom-call | flops 1 | bytes 1 | tf_op jit(solution)/shard_map/pallas_call | solution.py:221
  (18 shorter events, 0.0 us)
Async XLA Ops:
  0.0 1.0 %copy-start.1 = (bf16[32,64,128]{2,1,0:T(8,128)(2,1)S(1)}, bf16[32,64,128]{2,1,0:T(8,128)(2,1)}, u32[]{:S(2)}) copy-start(bf16[32,64,128]{2,1,0:T(8,128)(2,1)} %param.7) | copy-start | bytes 1572868
  0.0 1.2 %copy-start.2 = (bf16[32,64,128]{2,1,0:T(8,128)(2,1)S(1)}, bf16[32,64,128]{2,1,0:T(8,128)(2,1)}, u32[]{:S(2)}) copy-start(bf16[32,64,128]{2,1,0:T(8,128)(2,1)} %param.6) | copy-start | bytes 1572868
  1.2 8.3 %copy-start = (bf16[3,32,64,256]{3,2,1,0:T(8,128)(2,1)S(1)}, bf16[3,32,64,256]{3,2,1,0:T(8,128)(2,1)}, u32[]{:S(2)}) copy-start(bf16[3,32,64,256]{3,2,1,0:T(8,128)(2,1)} %param.8) | copy-start | bytes 9437188
  1.5 7.9 %collective-permute-start.2 = (bf16[8,1,64,128]{3,2,1,0:T(8,128)(2,1)S(1)}, bf16[8,1,64,128]{3,2,1,0:T(8,128)(2,1)S(1)}, u32[]{:S(2)}, u32[]{:S(2)}) collective-permute-start(bf16[8,1,64,128]{3,2,1,0:T(8,128)(2,1)S(1)} %get-tuple-element.63.x_ref), channel_id=1, source_target_pairs={{0,128},{8,136},{16,144},{24,152},{32,160},{40,168},{48,176},{56,1... | collective-permute-start | bytes 393224 | tf_op jit(solution)/shard_map/ppermute | solution.py:163
  5.5 7.1 %collective-permute-start.1 = (bf16[8,1,64,128]{3,2,1,0:T(8,128)(2,1)S(1)}, bf16[8,1,64,128]{3,2,1,0:T(8,128)(2,1)S(1)}, u32[]{:S(2)}, u32[]{:S(2)}) collective-permute-start(bf16[8,1,64,128]{3,2,1,0:T(8,128)(2,1)S(1)} %get-tuple-element.62.x_ref), channel_id=1, source_target_pairs={{0,128},{8,136},{16,144},{24,152},{32,160},{40,168},{48,176},{56,1... | collective-permute-start | bytes 393224 | tf_op jit(solution)/shard_map/ppermute | solution.py:163
  6.0 9.5 %collective-permute-start = (bf16[8,1,64,128]{3,2,1,0:T(8,128)(2,1)S(1)}, bf16[8,1,64,128]{3,2,1,0:T(8,128)(2,1)S(1)}, u32[]{:S(2)}, u32[]{:S(2)}) collective-permute-start(bf16[8,1,64,128]{3,2,1,0:T(8,128)(2,1)S(1)} %get-tuple-element.61.x_ref), channel_id=1, source_target_pairs={{0,128},{8,136},{16,144},{24,152},{32,160},{40,168},{48,176},{56,1... | collective-permute-start | bytes 393224 | tf_op jit(solution)/shard_map/ppermute | solution.py:163
  9.4 8.9 %collective-permute-start.6 = (bf16[8,1,64,128]{3,2,1,0:T(8,128)(2,1)S(1)}, bf16[8,1,64,128]{3,2,1,0:T(8,128)(2,1)S(1)}, u32[]{:S(2)}, u32[]{:S(2)}) collective-permute-start(bf16[8,1,64,128]{3,2,1,0:T(8,128)(2,1)S(1)} %get-tuple-element.71.x_ref), channel_id=1, source_target_pairs={{0,128},{8,136},{16,144},{24,152},{32,160},{40,168},{48,176},{56,1... | collective-permute-start | bytes 393224 | tf_op jit(solution)/shard_map/ppermute | solution.py:163
  9.8 9.9 %collective-permute-start.5 = (bf16[8,1,64,128]{3,2,1,0:T(8,128)(2,1)S(1)}, bf16[8,1,64,128]{3,2,1,0:T(8,128)(2,1)S(1)}, u32[]{:S(2)}, u32[]{:S(2)}) collective-permute-start(bf16[8,1,64,128]{3,2,1,0:T(8,128)(2,1)S(1)} %get-tuple-element.70.x_ref), channel_id=1, source_target_pairs={{0,64},{8,72},{16,80},{24,88},{32,96},{40,104},{48,112},{56,120},{... | collective-permute-start | bytes 393224 | tf_op jit(solution)/shard_map/ppermute | solution.py:163
  12.9 10.0 %collective-permute-start.4 = (bf16[8,1,64,128]{3,2,1,0:T(8,128)(2,1)S(1)}, bf16[8,1,64,128]{3,2,1,0:T(8,128)(2,1)S(1)}, u32[]{:S(2)}, u32[]{:S(2)}) collective-permute-start(bf16[8,1,64,128]{3,2,1,0:T(8,128)(2,1)S(1)} %get-tuple-element.69.x_ref), channel_id=1, source_target_pairs={{0,64},{8,72},{16,80},{24,88},{32,96},{40,104},{48,112},{56,120},{... | collective-permute-start | bytes 393224 | tf_op jit(solution)/shard_map/ppermute | solution.py:163
  15.8 10.0 %collective-permute-start.3 = (bf16[8,1,64,128]{3,2,1,0:T(8,128)(2,1)S(1)}, bf16[8,1,64,128]{3,2,1,0:T(8,128)(2,1)S(1)}, u32[]{:S(2)}, u32[]{:S(2)}) collective-permute-start(bf16[8,1,64,128]{3,2,1,0:T(8,128)(2,1)S(1)} %get-tuple-element.68.x_ref), channel_id=1, source_target_pairs={{0,64},{8,72},{16,80},{24,88},{32,96},{40,104},{48,112},{56,120},{... | collective-permute-start | bytes 393224 | tf_op jit(solution)/shard_map/ppermute | solution.py:163
  18.6 10.0 %collective-permute-start.10 = (bf16[8,1,64,128]{3,2,1,0:T(8,128)(2,1)S(1)}, bf16[8,1,64,128]{3,2,1,0:T(8,128)(2,1)S(1)}, u32[]{:S(2)}, u32[]{:S(2)}) collective-permute-start(bf16[8,1,64,128]{3,2,1,0:T(8,128)(2,1)S(1)} %get-tuple-element.79.x_ref), channel_id=1, source_target_pairs={{0,64},{8,72},{16,80},{24,88},{32,96},{40,104},{48,112},{56,120},{... | collective-permute-start | bytes 393224 | tf_op jit(solution)/shard_map/ppermute | solution.py:163
  20.0 11.4 %collective-permute-start.9 = (bf16[8,1,64,128]{3,2,1,0:T(8,128)(2,1)S(1)}, bf16[8,1,64,128]{3,2,1,0:T(8,128)(2,1)S(1)}, u32[]{:S(2)}, u32[]{:S(2)}) collective-permute-start(bf16[8,1,64,128]{3,2,1,0:T(8,128)(2,1)S(1)} %get-tuple-element.78.x_ref), channel_id=1, source_target_pairs={{0,32},{8,40},{16,48},{24,56},{32,0},{40,8},{48,16},{56,24},{64,96... | collective-permute-start | bytes 393224 | tf_op jit(solution)/shard_map/ppermute | solution.py:163
  23.3 8.4 %collective-permute-start.8 = (bf16[8,1,64,128]{3,2,1,0:T(8,128)(2,1)S(1)}, bf16[8,1,64,128]{3,2,1,0:T(8,128)(2,1)S(1)}, u32[]{:S(2)}, u32[]{:S(2)}) collective-permute-start(bf16[8,1,64,128]{3,2,1,0:T(8,128)(2,1)S(1)} %get-tuple-element.77.x_ref), channel_id=1, source_target_pairs={{0,32},{8,40},{16,48},{24,56},{32,0},{40,8},{48,16},{56,24},{64,96... | collective-permute-start | bytes 393224 | tf_op jit(solution)/shard_map/ppermute | solution.py:163
  26.1 6.5 %collective-permute-start.7 = (bf16[8,1,64,128]{3,2,1,0:T(8,128)(2,1)S(1)}, bf16[8,1,64,128]{3,2,1,0:T(8,128)(2,1)S(1)}, u32[]{:S(2)}, u32[]{:S(2)}) collective-permute-start(bf16[8,1,64,128]{3,2,1,0:T(8,128)(2,1)S(1)} %get-tuple-element.76.x_ref), channel_id=1, source_target_pairs={{0,32},{8,40},{16,48},{24,56},{32,0},{40,8},{48,16},{56,24},{64,96... | collective-permute-start | bytes 393224 | tf_op jit(solution)/shard_map/ppermute | solution.py:163
  28.9 6.5 %collective-permute-start.11 = (bf16[8,1,64,128]{3,2,1,0:T(8,128)(2,1)S(1)}, bf16[8,1,64,128]{3,2,1,0:T(8,128)(2,1)S(1)}, u32[]{:S(2)}, u32[]{:S(2)}) collective-permute-start(bf16[8,1,64,128]{3,2,1,0:T(8,128)(2,1)S(1)} %get-tuple-element.88.x_ref), channel_id=1, source_target_pairs={{0,32},{8,40},{16,48},{24,56},{32,0},{40,8},{48,16},{56,24},{64,96... | collective-permute-start | bytes 393224 | tf_op jit(solution)/shard_map/ppermute | solution.py:163
  31.7 1.6 %copy-start.4 = (bf16[2,32,64,256]{3,2,1,0:T(8,128)(2,1)S(1)}, bf16[2,32,64,256]{3,2,1,0:T(8,128)(2,1)}, u32[]{:S(2)}) copy-start(bf16[2,32,64,256]{3,2,1,0:T(8,128)(2,1)} %param.10) | copy-start | bytes 6291460
  32.0 2.0 %copy-start.3 = (bf16[2,32,64,256]{3,2,1,0:T(8,128)(2,1)S(1)}, bf16[2,32,64,256]{3,2,1,0:T(8,128)(2,1)}, u32[]{:S(2)}) copy-start(bf16[2,32,64,256]{3,2,1,0:T(8,128)(2,1)} %param.9) | copy-start | bytes 6291460
  32.0 2.0 %copy-start.5 = (bf16[32,64,128]{2,1,0:T(8,128)(2,1)S(1)}, bf16[32,64,128]{2,1,0:T(8,128)(2,1)}, u32[]{:S(2)}) copy-start(bf16[32,64,128]{2,1,0:T(8,128)(2,1)} %param.11) | copy-start | bytes 1572868
  57.7 5.9 %collective-permute-start.15 = (bf16[8,1,64,128]{3,2,1,0:T(8,128)(2,1)S(1)}, bf16[8,1,64,128]{3,2,1,0:T(8,128)(2,1)S(1)}, u32[]{:S(2)}, u32[]{:S(2)}) collective-permute-start(bf16[8,1,64,128]{3,2,1,0:T(8,128)(2,1)S(1)} %get-tuple-element.101.x_ref), channel_id=1, source_target_pairs={{0,16},{8,24},{16,0},{24,8},{32,48},{40,56},{48,32},{56,40},{64,80... | collective-permute-start | bytes 393224 | tf_op jit(solution)/shard_map/ppermute | solution.py:163
  60.5 4.1 %collective-permute-start.14 = (bf16[8,1,64,128]{3,2,1,0:T(8,128)(2,1)S(1)}, bf16[8,1,64,128]{3,2,1,0:T(8,128)(2,1)S(1)}, u32[]{:S(2)}, u32[]{:S(2)}) collective-permute-start(bf16[8,1,64,128]{3,2,1,0:T(8,128)(2,1)S(1)} %get-tuple-element.100.x_ref), channel_id=1, source_target_pairs={{0,16},{8,24},{16,0},{24,8},{32,48},{40,56},{48,32},{56,40},{64,80... | collective-permute-start | bytes 393224 | tf_op jit(solution)/shard_map/ppermute | solution.py:163
  61.4 5.0 %collective-permute-start.13 = (bf16[8,1,64,128]{3,2,1,0:T(8,128)(2,1)S(1)}, bf16[8,1,64,128]{3,2,1,0:T(8,128)(2,1)S(1)}, u32[]{:S(2)}, u32[]{:S(2)}) collective-permute-start(bf16[8,1,64,128]{3,2,1,0:T(8,128)(2,1)S(1)} %get-tuple-element.99.x_ref), channel_id=1, source_target_pairs={{0,16},{8,24},{16,0},{24,8},{32,48},{40,56},{48,32},{56,40},{64,80... | collective-permute-start | bytes 393224 | tf_op jit(solution)/shard_map/ppermute | solution.py:163
  63.5 9.7 %collective-permute-start.12 = (bf16[8,1,64,128]{3,2,1,0:T(8,128)(2,1)S(1)}, bf16[8,1,64,128]{3,2,1,0:T(8,128)(2,1)S(1)}, u32[]{:S(2)}, u32[]{:S(2)}) collective-permute-start(bf16[8,1,64,128]{3,2,1,0:T(8,128)(2,1)S(1)} %get-tuple-element.98.x_ref), channel_id=1, source_target_pairs={{0,16},{8,24},{16,0},{24,8},{32,48},{40,56},{48,32},{56,40},{64,80... | collective-permute-start | bytes 393224 | tf_op jit(solution)/shard_map/ppermute | solution.py:163
  66.7 7.4 %collective-permute-start.18 = (bf16[8,1,64,128]{3,2,1,0:T(8,128)(2,1)S(1)}, bf16[8,1,64,128]{3,2,1,0:T(8,128)(2,1)S(1)}, u32[]{:S(2)}, u32[]{:S(2)}) collective-permute-start(bf16[8,1,64,128]{3,2,1,0:T(8,128)(2,1)S(1)} %get-tuple-element.109.refs_4_), channel_id=1, source_target_pairs={{0,8},{8,0},{16,24},{24,16},{32,40},{40,32},{48,56},{56,48},{64,72... | collective-permute-start | bytes 393224 | tf_op jit(solution)/shard_map/ppermute | solution.py:163
  72.7 1.4 %collective-permute-start.17 = (bf16[8,1,64,128]{3,2,1,0:T(8,128)(2,1)S(1)}, bf16[8,1,64,128]{3,2,1,0:T(8,128)(2,1)S(1)}, u32[]{:S(2)}, u32[]{:S(2)}) collective-permute-start(bf16[8,1,64,128]{3,2,1,0:T(8,128)(2,1)S(1)} %get-tuple-element.108.refs_2_), channel_id=1, source_target_pairs={{0,8},{8,0},{16,24},{24,16},{32,40},{40,32},{48,56},{56,48},{64,72... | collective-permute-start | bytes 393224 | tf_op jit(solution)/shard_map/ppermute | solution.py:163
  72.8 1.4 %collective-permute-start.16 = (bf16[8,1,64,128]{3,2,1,0:T(8,128)(2,1)S(1)}, bf16[8,1,64,128]{3,2,1,0:T(8,128)(2,1)S(1)}, u32[]{:S(2)}, u32[]{:S(2)}) collective-permute-start(bf16[8,1,64,128]{3,2,1,0:T(8,128)(2,1)S(1)} %get-tuple-element.107.refs_0_), channel_id=1, source_target_pairs={{0,8},{8,0},{16,24},{24,16},{32,40},{40,32},{48,56},{56,48},{64,72... | collective-permute-start | bytes 393224 | tf_op jit(solution)/shard_map/ppermute | solution.py:163
  73.5 1.6 %collective-permute-start.19 = (bf16[8,1,64,128]{3,2,1,0:T(8,128)(2,1)S(1)}, bf16[8,1,64,128]{3,2,1,0:T(8,128)(2,1)S(1)}, u32[]{:S(2)}, u32[]{:S(2)}) collective-permute-start(bf16[8,1,64,128]{3,2,1,0:T(8,128)(2,1)S(1)} %get-tuple-element.111.x_ref), channel_id=1, source_target_pairs={{0,8},{8,0},{16,24},{24,16},{32,40},{40,32},{48,56},{56,48},{64,72... | collective-permute-start | bytes 393224 | tf_op jit(solution)/shard_map/ppermute | solution.py:163

commit v3 on v2

v3 whole, which is shorter than its diff:
```python
import functools

import jax
import jax.numpy as jnp
from jax import lax
from jax.experimental import pallas as pl
from jax.experimental.pallas import tpu as pltpu
from jax.sharding import PartitionSpec as P

WIDTHS = (1, 1, 1, 1)
PIECES = 1
PLAN = (
    "T0", "L0", "L1", "L2", "L3", "U00", "U01", "U02", "U03", "U10", "U11", "U12", "U13", "U20", "U21",
    "U22", "W0", "U23", "M0", "M1", "D00", "D01", "E0", "E1",
)
VMEM = pl.BlockSpec(memory_space=pltpu.VMEM)
ANY = pl.BlockSpec(memory_space=pl.ANY)
DMA = pltpu.SemaphoreType.DMA
TOKEN = jax.ShapeDtypeStruct((8, 128), jnp.float32)
COST = {"T0": 100}


def turn(piece):
    half = piece.shape[-1] // 2
    rolled = pltpu.roll(piece.astype(jnp.float32), half, 1)
    lane = lax.broadcasted_iota(jnp.int32, piece.shape, 1)
    return jnp.where(lane < half, -rolled, rolled).astype(jnp.bfloat16)


def product(weights, parts):
    stacked = jnp.concatenate(list(parts) + [turn(p) for p in parts], axis=0)
    return jnp.dot(weights, stacked, preferred_element_type=jnp.float32).astype(jnp.bfloat16)


def token_kernel(t_ref, u_ref):
    u_ref[...] = t_ref[...]


def leaf_kernel(first, w_ref, x_ref, t_ref, o_ref, u_ref, ws_ref, xs_ref, sems):
    u_ref[...] = t_ref[...]
    width = o_ref.shape[1]
    loads = [
        pltpu.make_async_copy(w_ref.at[:, first:first + width], ws_ref, sems.at[0]),
        pltpu.make_async_copy(x_ref.at[:, first:first + width], xs_ref, sems.at[1]),
    ]
    for load in loads:
        load.start()
    for load in loads:
        load.wait()
    for a in range(o_ref.shape[0]):
        for b in range(width):
            o_ref[a, b] = product(ws_ref[a, b], [xs_ref[a, b]])


def stage_kernel(t_ref, *refs):
    count = (len(refs) - 2) // 2
    u_ref, sems = refs[-2:]
    u_ref[...] = t_ref[...]
    loads = [pltpu.make_async_copy(refs[i], refs[count + i], sems.at[i]) for i in range(count)]
    for load in loads:
        load.start()
    for load in loads:
        load.wait()


def level_kernel(first, step, w_ref, x_ref, y_ref, t_ref, o_ref, u_ref):
    u_ref[...] = t_ref[...]
    for a in range(o_ref.shape[0]):
        for b in range(o_ref.shape[1]):
            o_ref[a, b] = product(w_ref[step, a, first + b], [x_ref[a, b], y_ref[a, b]])


def spread_kernel(first, step, w_ref, x_ref, y_ref, t_ref, *refs):
    *earlier, u_ref = refs
    count = x_ref.shape[0]
    earlier, outs = earlier[:-count], earlier[-count:]
    u_ref[...] = t_ref[...]
    me = lax.axis_index("mid")
    for q in range(count):
        a = me ^ q
        at = 0
        for e_ref in earlier:
            outs[q][at:at + e_ref.shape[1]] = e_ref[a]
            at += e_ref.shape[1]
        for b in range(x_ref.shape[1]):
            outs[q][at + b] = product(w_ref[step, a, first + b], [x_ref[a, b], y_ref[a, b]])


def middle_kernel(gaps, w_ref, t_ref, *refs):
    count = len(gaps)
    got, outs, u_ref, s_ref = refs[:count], refs[count:-2], refs[-2], refs[-1]
    u_ref[...] = t_ref[...]
    me = lax.axis_index("mid")
    width = outs[0].shape[1]
    for i, q in enumerate(gaps):
        for b in range(s_ref.shape[1]):
            s_ref[i, b] = product(w_ref[0, me ^ q, b], [got[i][b], got[i ^ (count // 2)][b]])
    for i, q in enumerate(gaps):
        for b in range(s_ref.shape[1]):
            outs[b // width][i, b % width] = product(w_ref[1, me ^ q, b], [s_ref[i, b], s_ref[i ^ (count // 4), b]])


def lower_kernel(gaps, first, step, w_ref, x_ref, y_ref, t_ref, o_ref, u_ref):
    u_ref[...] = t_ref[...]
    me = lax.axis_index("mid")
    for i, q in enumerate(gaps):
        for b in range(o_ref.shape[1]):
            o_ref[i, b] = product(w_ref[step, me ^ q, first + b], [x_ref[i, b], y_ref[i, b]])


def finish(gaps, first, step, w_ref, v_ref, x_ref, y_ref, r_ref):
    me = lax.axis_index("mid")
    for i, q in enumerate(gaps):
        for b in range(x_ref.shape[1]):
            value = product(w_ref[step, me ^ q, first + b], [x_ref[i, b], y_ref[i, b]])
            r_ref[i, b] = product(v_ref[me ^ q, first + b], [value])


def finish_kernel(gaps, first, step, w_ref, v_ref, t_ref, x_ref, y_ref, r_ref, u_ref):
    u_ref[...] = t_ref[...]
    finish(gaps, first, step, w_ref, v_ref, x_ref, y_ref, r_ref)


def store_kernel(places, step, w_ref, v_ref, t_ref, x_ref, y_ref, *refs):
    *earlier, o_ref, r_ref, sems = refs
    me = lax.axis_index("mid")
    width = r_ref.shape[1]

    def stores(c, source):
        gaps, first = places[c]
        return [
            pltpu.make_async_copy(source.at[i], o_ref.at[me ^ q, first:first + width], sems.at[c * len(gaps) + i])
            for i, q in enumerate(gaps)
        ]

    moving = [store for c, e_ref in enumerate(earlier) for store in stores(c, e_ref)]
    for store in moving:
        store.start()
    gaps, first = places[-1]
    finish(gaps, first, step, w_ref, v_ref, x_ref, y_ref, r_ref)
    final = stores(len(places) - 1, r_ref)
    for store in final:
        store.start()
    for store in moving + final:
        store.wait()


def call(kind, kernel, shapes, args, specs, out_specs, token, **kw):
    *outs, token = pl.pallas_call(
        kernel,
        out_shape=[jax.ShapeDtypeStruct(shape, jnp.bfloat16) for shape in shapes] + [TOKEN],
        in_specs=specs,
        out_specs=list(out_specs) + [VMEM],
        compiler_params=pltpu.CompilerParams(vmem_limit_bytes=8 << 20),
        cost_estimate=pl.CostEstimate(flops=1 + int(COST.get(kind, 0) * 1e9), bytes_accessed=1, transcendentals=0),
        **kw,
    )(*args)
    return outs, token


def on_device(signal, leaf_in, upper_w, middle_w, lower_w, leaf_out):
    lvl_size, mid_size = lax.axis_size("lvl"), lax.axis_size("mid")
    lvl_bits = lvl_size.bit_length() - 1
    inner = signal.shape[0] // mid_size
    box = signal.shape[1:]
    part = functools.partial
    leaf_w, up_w, mid_w, low_w, out_w, samples = (
        v.reshape(v.shape[:-3] + (mid_size, inner) + v.shape[-2:])
        for v in (leaf_in, upper_w, middle_w, lower_w, leaf_out, signal)
    )
    firsts = [sum(WIDTHS[:c]) for c in range(len(WIDTHS))]
    shapes = [(mid_size, w) + box for w in WIDTHS]

    def swap(block, bit):
        return lax.ppermute(block, "lvl", [(i, i ^ (1 << bit)) for i in range(lvl_size)])

    def across(block, gap):
        return lax.ppermute(block, "mid", [(i, i ^ gap) for i in range(mid_size)])

    field, other, place = {}, {}, {}
    token = jnp.zeros(TOKEN.shape, TOKEN.dtype)
    result, finished = None, []
    lower_count = lower_w.shape[0]
    upper_count = upper_w.shape[0]
    for item in PLAN:
        kind, c = item[0], int(item[-1])
        step = int(item[1])
        name = item
        first, shape = firsts[c], shapes[c]
        block = pltpu.VMEM(shape, jnp.bfloat16)
        if kind == "T":
            _, token = call(name, token_kernel, [], (token,), [VMEM], [], token)
        elif kind == "W":
            staged = (mid_w, low_w, out_w)
            (mid_w, low_w, out_w), token = call(name, stage_kernel, [v.shape for v in staged], (token, *staged),
                                                      [VMEM] + [ANY] * 3, [VMEM] * 3, token, scratch_shapes=[DMA((3,))])
        elif kind == "L":
            (field[c],), token = call(name, part(leaf_kernel, first), [shape], (leaf_w, samples, token), [ANY, ANY, VMEM],
                                      [VMEM], token,
                                      scratch_shapes=[block, block, DMA((2,))])
            other[c] = swap(field[c], lvl_bits - 1)
        elif kind == "U" and (step < upper_count - 1 or c < len(WIDTHS) - 1):
            (field[c],), token = call(name, part(level_kernel, first, step), [shape], (up_w, field[c], other[c], token),
                                      [VMEM] * 4, [VMEM], token)
            if step < upper_count - 1:
                other[c] = swap(field[c], lvl_bits - 2 - step)
        elif kind == "U":
            earlier = [field[e] for e in range(c)]
            sends, token = call(name, part(spread_kernel, first, step), [(inner,) + box] * mid_size,
                                (up_w, field[c], other[c], token, *earlier), [VMEM] * (4 + len(earlier)),
                                [VMEM] * mid_size, token)
            got = [across(send, gap) if gap else send for gap, send in enumerate(sends)]
        elif kind == "M":
            gaps = tuple(range(c, mid_size, 2))
            tall = (len(gaps), inner)
            fields, token = call(name, part(middle_kernel, gaps), [(len(gaps), inner // PIECES) + box] * PIECES,
                                 (mid_w, token, *[got[q] for q in gaps]), [VMEM] * (2 + len(gaps)), [VMEM] * PIECES,
                                 token, scratch_shapes=[pltpu.VMEM(tall + box, jnp.bfloat16)])
            for piece, value in enumerate(fields):
                e = c * PIECES + piece
                field[e], other[e] = value, swap(value, lower_count - 1)
                place[e] = (gaps, piece * (inner // PIECES))
        elif kind == "D":
            (field[c],), token = call(name, part(lower_kernel, *place[c], step), [field[c].shape],
                                      (low_w, field[c], other[c], token), [VMEM] * 4, [VMEM], token)
            other[c] = swap(field[c], lower_count - 2 - step)
        elif item != PLAN[-1]:
            (done,), token = call(name, part(finish_kernel, *place[c], lower_count - 1), [field[c].shape],
                                  (low_w, out_w, token, field[c], other[c]), [VMEM] * 5, [VMEM], token)
            finished.append(done)
        else:
            args = (low_w, out_w, token, field[c], other[c], *finished)
            places = [place[e] for e in range(c + 1)]
            result = pl.pallas_call(
                part(store_kernel, places, lower_count - 1),
                out_shape=jax.ShapeDtypeStruct(samples.shape, jnp.bfloat16),
                in_specs=[VMEM] * len(args),
                out_specs=ANY,
                scratch_shapes=[pltpu.VMEM(field[c].shape, jnp.bfloat16), DMA((mid_size * PIECES,))],
                compiler_params=pltpu.CompilerParams(vmem_limit_bytes=8 << 20),
                cost_estimate=pl.CostEstimate(flops=1, bytes_accessed=1, transcendentals=0),
            )(*args)
    return result.reshape(signal.shape)


def solution(mesh):
    boxes = P(("lvl", "mid"), None, None)
    levels = P(None, ("lvl", "mid"), None, None)
    return jax.shard_map(
        on_device,
        mesh=mesh,
        in_specs=(boxes, boxes, levels, levels, levels, boxes),
        out_specs=boxes,
        check_vma=False,
    )
```

time: 76.6 us -> 71.1 us (0.928)
  blocking collectives: 21.3 us -> 0 us
  starting transfers between devices: 30.4 us -> 45.8 us
  Pallas kernels: 11 us -> 9.59 us
  waiting for transfers between devices: 11 us -> 12.2 us
    all_to_all x1 -> x0, blocking collectives: 21.3 us -> none  [on_device(): lax.all_to_all(joined, 'mid', split_axis=0, concat_axis=0, tiled=True)]
    ppermute x0 -> x7, starting transfers between devices: none -> 14.5 us  [across(): return lax.ppermute(block, 'mid', [(i, i ^ gap) for i in range(mid_size)])]
    ppermute x0 -> x7, waiting for transfers between devices: none -> 2.67 us  [across(): return lax.ppermute(block, 'mid', [(i, i ^ gap) for i in range(mid_size)])]
    pallas_call x27 -> x23, Pallas kernels: 9.74 us -> 8.12 us  [call(): pl.pallas_call(kernel, out_shape=[jax.ShapeDtypeStruct(shape, jnp.bfloat1...]
    ppermute x20 -> x16, waiting for transfers between devices: 11 us -> 9.57 us  [swap(): lax.ppermute(block, 'lvl', [(i, i ^ 1 << bit) for i in range(lvl_size)])]
    ppermute x20 -> x16, starting transfers between devices: 30.4 us -> 31.2 us  [swap(): lax.ppermute(block, 'lvl', [(i, i ^ 1 << bit) for i in range(lvl_size)])]
  transfers between devices with their start and end apart: 20 -> 23, of which waited for: 9 -> 10; matrix products, arithmetic and copies ran while one was open for 0% -> 0% of each run, Pallas kernels for 11% -> 11%
where the time goes in v3:
time: 71.1 us; the launch traced here: 70.4 us
  starting transfers between devices  45.8 us (64%)
  waiting for transfers between devices  12.2 us (17%)
  Pallas kernels  9.59 us (13%)
  local copies, waits for them, and re-layouts  2.37 us (3%)
    ppermute x16, starting transfers between devices, swap(): lax.ppermute(block, 'lvl', [(i, i ^ 1 << bit) for i in range(lvl_size)])  31.2 us
    ppermute x7, starting transfers between devices, across(): return lax.ppermute(block, 'mid', [(i, i ^ gap) for i in range(mid_size)])  14.5 us
    ppermute x16, waiting for transfers between devices, swap(): lax.ppermute(block, 'lvl', [(i, i ^ 1 << bit) for i in range(lvl_size)])  9.57 us
    pallas_call x23, Pallas kernels, call(): pl.pallas_call(kernel, out_shape=[jax.ShapeDtypeStruct(shape, jnp.bfloat1...  8.12 us
    ppermute x7, waiting for transfers between devices, across(): return lax.ppermute(block, 'mid', [(i, i ^ gap) for i in range(mid_size)])  2.67 us
    unnamed x12, local copies, waits for them, and re-layouts  2.36 us
    pallas_call x1, Pallas kernels, on_device(): pl.pallas_call(part(store_kernel, places, lower_count - 1), out_shape=jax...  1.48 us
  transfers between devices with their start and end apart: 23, of which 10 were waited for; matrix products, arithmetic and copies ran while one was open for 0% of the time, Pallas kernels for 11%

profile of v3, /device:TPU:1, one launch (start us, length us, event | category | flops | bytes accessed | tf_op | source)
XLA Modules:
  0.0 70.4 jit_solution(12254557388528313082)
XLA Ops:
  0.0 1.0 %copy-done.1 = bf16[32,64,128]{2,1,0:T(8,128)(2,1)S(1)} copy-done((bf16[32,64,128]{2,1,0:T(8,128)(2,1)S(1)}, bf16[32,64,128]{2,1,0:T(8,128)(2,1)}, u32[]{:S(2)}) %copy-start.1) | copy-done | bytes 524312
  1.0 0.2 copy-done.2
  1.2 0.3 shard_map.65
  1.5 3.7 %collective-permute-start.2 = (bf16[8,1,64,128]{3,2,1,0:T(8,128)(2,1)S(1)}, bf16[8,1,64,128]{3,2,1,0:T(8,128)(2,1)S(1)}, u32[]{:S(2)}, u32[]{:S(2)}) collective-permute-start(bf16[8,1,64,128]{3,2,1,0:T(8,128)(2,1)S(1)} %get-tuple-element.62.x_ref), channel_id=1, source_target_pairs={{0,128},{8,136},{16,144},{24,152},{32,160},{40,168},{48,176},{56,1... | collective-permute-start | bytes 393224 | tf_op jit(solution)/shard_map/ppermute | solution.py:175
  5.2 0.3 shard_map.66
  5.5 0.1 collective-permute-start.1
  5.6 0.3 shard_map.67
  6.0 3.0 %collective-permute-start = (bf16[8,1,64,128]{3,2,1,0:T(8,128)(2,1)S(1)}, bf16[8,1,64,128]{3,2,1,0:T(8,128)(2,1)S(1)}, u32[]{:S(2)}, u32[]{:S(2)}) collective-permute-start(bf16[8,1,64,128]{3,2,1,0:T(8,128)(2,1)S(1)} %get-tuple-element.60.x_ref), channel_id=1, source_target_pairs={{0,128},{8,136},{16,144},{24,152},{32,160},{40,168},{48,176},{56,1... | collective-permute-start | bytes 393224 | tf_op jit(solution)/shard_map/ppermute | solution.py:175
  9.0 0.3 shard_map.68
  9.4 0.1 collective-permute-start.6
  9.5 0.0 collective-permute-done.2.y_ref
  9.5 0.3 shard_map.69
  9.8 1.5 %collective-permute-start.5 = (bf16[8,1,64,128]{3,2,1,0:T(8,128)(2,1)S(1)}, bf16[8,1,64,128]{3,2,1,0:T(8,128)(2,1)S(1)}, u32[]{:S(2)}, u32[]{:S(2)}) collective-permute-start(bf16[8,1,64,128]{3,2,1,0:T(8,128)(2,1)S(1)} %get-tuple-element.69.x_ref), channel_id=1, source_target_pairs={{0,64},{8,72},{16,80},{24,88},{32,96},{40,104},{48,112},{56,120},{... | collective-permute-start | bytes 393224 | tf_op jit(solution)/shard_map/ppermute | solution.py:175
  11.3 1.4 %collective-permute-done.1.y_ref = bf16[8,1,64,128]{3,2,1,0:T(8,128)(2,1)S(1)} collective-permute-done((bf16[8,1,64,128]{3,2,1,0:T(8,128)(2,1)S(1)}, bf16[8,1,64,128]{3,2,1,0:T(8,128)(2,1)S(1)}, u32[]{:S(2)}, u32[]{:S(2)}) %collective-permute-start.1) | collective-permute-done | bytes 131104 | tf_op jit(solution)/shard_map/ppermute | solution.py:175
  12.6 0.3 shard_map.70
  12.9 0.1 collective-permute-start.4
  13.0 2.4 %collective-permute-done.y_ref = bf16[8,1,64,128]{3,2,1,0:T(8,128)(2,1)S(1)} collective-permute-done((bf16[8,1,64,128]{3,2,1,0:T(8,128)(2,1)S(1)}, bf16[8,1,64,128]{3,2,1,0:T(8,128)(2,1)S(1)}, u32[]{:S(2)}, u32[]{:S(2)}) %collective-permute-start) | collective-permute-done | bytes 131104 | tf_op jit(solution)/shard_map/ppermute | solution.py:175
  15.5 0.3 shard_map.71
  15.8 0.1 collective-permute-start.3
  15.9 2.4 %collective-permute-done.6.y_ref = bf16[8,1,64,128]{3,2,1,0:T(8,128)(2,1)S(1)} collective-permute-done((bf16[8,1,64,128]{3,2,1,0:T(8,128)(2,1)S(1)}, bf16[8,1,64,128]{3,2,1,0:T(8,128)(2,1)S(1)}, u32[]{:S(2)}, u32[]{:S(2)}) %collective-permute-start.6) | collective-permute-done | bytes 131104 | tf_op jit(solution)/shard_map/ppermute | solution.py:175
  18.3 0.3 shard_map.72
  18.6 0.1 collective-permute-start.10
  18.7 1.0 %collective-permute-done.5.y_ref = bf16[8,1,64,128]{3,2,1,0:T(8,128)(2,1)S(1)} collective-permute-done((bf16[8,1,64,128]{3,2,1,0:T(8,128)(2,1)S(1)}, bf16[8,1,64,128]{3,2,1,0:T(8,128)(2,1)S(1)}, u32[]{:S(2)}, u32[]{:S(2)}) %collective-permute-start.5) | collective-permute-done | bytes 131104 | tf_op jit(solution)/shard_map/ppermute | solution.py:175
  19.6 0.3 shard_map.73
  20.0 3.0 %collective-permute-start.9 = (bf16[8,1,64,128]{3,2,1,0:T(8,128)(2,1)S(1)}, bf16[8,1,64,128]{3,2,1,0:T(8,128)(2,1)S(1)}, u32[]{:S(2)}, u32[]{:S(2)}) collective-permute-start(bf16[8,1,64,128]{3,2,1,0:T(8,128)(2,1)S(1)} %get-tuple-element.77.x_ref), channel_id=1, source_target_pairs={{0,32},{8,40},{16,48},{24,56},{32,0},{40,8},{48,16},{56,24},{64,96... | collective-permute-start | bytes 393224 | tf_op jit(solution)/shard_map/ppermute | solution.py:175
  23.0 0.3 shard_map.74
  23.3 2.5 %collective-permute-start.8 = (bf16[8,1,64,128]{3,2,1,0:T(8,128)(2,1)S(1)}, bf16[8,1,64,128]{3,2,1,0:T(8,128)(2,1)S(1)}, u32[]{:S(2)}, u32[]{:S(2)}) collective-permute-start(bf16[8,1,64,128]{3,2,1,0:T(8,128)(2,1)S(1)} %get-tuple-element.76.x_ref), channel_id=1, source_target_pairs={{0,32},{8,40},{16,48},{24,56},{32,0},{40,8},{48,16},{56,24},{64,96... | collective-permute-start | bytes 393224 | tf_op jit(solution)/shard_map/ppermute | solution.py:175
  25.8 0.3 shard_map.75
  26.1 2.5 %collective-permute-start.7 = (bf16[8,1,64,128]{3,2,1,0:T(8,128)(2,1)S(1)}, bf16[8,1,64,128]{3,2,1,0:T(8,128)(2,1)S(1)}, u32[]{:S(2)}, u32[]{:S(2)}) collective-permute-start(bf16[8,1,64,128]{3,2,1,0:T(8,128)(2,1)S(1)} %get-tuple-element.75.x_ref), channel_id=1, source_target_pairs={{0,32},{8,40},{16,48},{24,56},{32,0},{40,8},{48,16},{56,24},{64,96... | collective-permute-start | bytes 393224 | tf_op jit(solution)/shard_map/ppermute | solution.py:175
  28.6 0.3 shard_map.76
  28.9 2.5 %collective-permute-start.11 = (bf16[8,1,64,128]{3,2,1,0:T(8,128)(2,1)S(1)}, bf16[8,1,64,128]{3,2,1,0:T(8,128)(2,1)S(1)}, u32[]{:S(2)}, u32[]{:S(2)}) collective-permute-start(bf16[8,1,64,128]{3,2,1,0:T(8,128)(2,1)S(1)} %get-tuple-element.87.x_ref), channel_id=1, source_target_pairs={{0,32},{8,40},{16,48},{24,56},{32,0},{40,8},{48,16},{56,24},{64,96... | collective-permute-start | bytes 393224 | tf_op jit(solution)/shard_map/ppermute | solution.py:175
  31.4 0.3 shard_map.77
  31.7 0.0 copy-start.4
  31.7 0.3 shard_map.78
  32.0 0.0 copy-start.3
  32.0 0.0 copy-start.5
  32.0 0.6 collective-permute-done.7.y_ref
  32.6 0.3 shard_map.79
  32.9 0.4 copy-done.4
  33.3 0.7 %copy-done.3 = bf16[2,32,64,256]{3,2,1,0:T(8,128)(2,1)S(1)} copy-done((bf16[2,32,64,256]{3,2,1,0:T(8,128)(2,1)S(1)}, bf16[2,32,64,256]{3,2,1,0:T(8,128)(2,1)}, u32[]{:S(2)}) %copy-start.3) | copy-done | bytes 2097176
  34.0 0.1 copy-done.5
  34.1 0.3 shard_map.80
  34.4 1.0 %collective-permute-done.11.y_ref = bf16[8,1,64,128]{3,2,1,0:T(8,128)(2,1)S(1)} collective-permute-done((bf16[8,1,64,128]{3,2,1,0:T(8,128)(2,1)S(1)}, bf16[8,1,64,128]{3,2,1,0:T(8,128)(2,1)S(1)}, u32[]{:S(2)}, u32[]{:S(2)}) %collective-permute-start.11) | collective-permute-done | bytes 131104 | tf_op jit(solution)/shard_map/ppermute | solution.py:175
  35.4 0.3 shard_map.81
  35.7 3.1 %collective-permute-start.12 = (bf16[4,64,128]{2,1,0:T(8,128)(2,1)S(1)}, bf16[4,64,128]{2,1,0:T(8,128)(2,1)S(1)}, u32[]{:S(2)}, u32[]{:S(2)}) collective-permute-start(bf16[4,64,128]{2,1,0:T(8,128)(2,1)S(1)} %get-tuple-element.94), channel_id=1, source_target_pairs={{0,2},{1,3},{2,0},{3,1},{4,6},{5,7},{6,4},{7,5},{8,10},{9,11},{10,... | collective-permute-start | bytes 196616 | tf_op jit(solution)/shard_map/ppermute | solution.py:178
  38.8 5.1 %collective-permute-start.13 = (bf16[4,64,128]{2,1,0:T(8,128)(2,1)S(1)}, bf16[4,64,128]{2,1,0:T(8,128)(2,1)S(1)}, u32[]{:S(2)}, u32[]{:S(2)}) collective-permute-start(bf16[4,64,128]{2,1,0:T(8,128)(2,1)S(1)} %get-tuple-element.95), channel_id=1, source_target_pairs={{0,4},{1,5},{2,6},{3,7},{4,0},{5,1},{6,2},{7,3},{8,12},{9,13},{10,... | collective-permute-start | bytes 196616 | tf_op jit(solution)/shard_map/ppermute | solution.py:178
  43.9 0.8 %collective-permute-start.15 = (bf16[4,64,128]{2,1,0:T(8,128)(2,1)S(1)}, bf16[4,64,128]{2,1,0:T(8,128)(2,1)S(1)}, u32[]{:S(2)}, u32[]{:S(2)}) collective-permute-start(bf16[4,64,128]{2,1,0:T(8,128)(2,1)S(1)} %get-tuple-element.98), channel_id=1, source_target_pairs={{0,1},{1,0},{2,3},{3,2},{4,5},{5,4},{6,7},{7,6},{8,9},{9,8},{10,11... | collective-permute-start | bytes 196616 | tf_op jit(solution)/shard_map/ppermute | solution.py:178
  44.7 1.6 %collective-permute-start.16 = (bf16[4,64,128]{2,1,0:T(8,128)(2,1)S(1)}, bf16[4,64,128]{2,1,0:T(8,128)(2,1)S(1)}, u32[]{:S(2)}, u32[]{:S(2)}) collective-permute-start(bf16[4,64,128]{2,1,0:T(8,128)(2,1)S(1)} %get-tuple-element.99), channel_id=1, source_target_pairs={{0,3},{1,2},{2,1},{3,0},{4,7},{5,6},{6,5},{7,4},{8,11},{9,10},{10,... | collective-permute-start | bytes 196616 | tf_op jit(solution)/shard_map/ppermute | solution.py:178
  46.3 3.1 %collective-permute-start.17 = (bf16[4,64,128]{2,1,0:T(8,128)(2,1)S(1)}, bf16[4,64,128]{2,1,0:T(8,128)(2,1)S(1)}, u32[]{:S(2)}, u32[]{:S(2)}) collective-permute-start(bf16[4,64,128]{2,1,0:T(8,128)(2,1)S(1)} %get-tuple-element.100), channel_id=1, source_target_pairs={{0,5},{1,4},{2,7},{3,6},{4,1},{5,0},{6,3},{7,2},{8,13},{9,12},{10,... | collective-permute-start | bytes 196616 | tf_op jit(solution)/shard_map/ppermute | solution.py:178
  49.4 0.9 %collective-permute-start.18 = (bf16[4,64,128]{2,1,0:T(8,128)(2,1)S(1)}, bf16[4,64,128]{2,1,0:T(8,128)(2,1)S(1)}, u32[]{:S(2)}, u32[]{:S(2)}) collective-permute-start(bf16[4,64,128]{2,1,0:T(8,128)(2,1)S(1)} %get-tuple-element.101), channel_id=1, source_target_pairs={{0,7},{1,6},{2,5},{3,4},{4,3},{5,2},{6,1},{7,0},{8,15},{9,14},{10,... | collective-permute-start | bytes 196616 | tf_op jit(solution)/shard_map/ppermute | solution.py:178
  50.3 0.7 %shard_map.82 = (bf16[4,4,64,128]{3,2,1,0:T(8,128)(2,1)S(1)}, f32[8,128]{1,0:T(8,128)S(1)}) custom-call(bf16[2,8,4,64,256]{4,3,2,1,0:T(8,128)(2,1)S(1)} %get-tuple-element.86.w_ref, f32[8,128]{1,0:T(8,128)S(1)} %get-tuple-element.92.t_ref, bf16[4,64,128]{2,1,0:T(8,128)(2,1)S(1)} %get-tuple-element.93.refs_0_, ...), custom_call_target="tpu_custom_call" | custom-call | flops 1 | bytes 1 | tf_op jit(solution)/shard_map/pallas_call | solution.py:149
  51.0 1.1 %collective-permute-start.20 = (bf16[4,4,64,128]{3,2,1,0:T(8,128)(2,1)S(1)}, bf16[4,4,64,128]{3,2,1,0:T(8,128)(2,1)S(1)}, u32[]{:S(2)}, u32[]{:S(2)}) collective-permute-start(bf16[4,4,64,128]{3,2,1,0:T(8,128)(2,1)S(1)} %get-tuple-element.103.x_ref), channel_id=1, source_target_pairs={{0,16},{8,24},{16,0},{24,8},{32,48},{40,56},{48,32},{56,40},{64,80... | collective-permute-start | bytes 786440 | tf_op jit(solution)/shard_map/ppermute | solution.py:175
  52.1 1.8 %collective-permute-done.17.refs_2_ = bf16[4,64,128]{2,1,0:T(8,128)(2,1)S(1)} collective-permute-done((bf16[4,64,128]{2,1,0:T(8,128)(2,1)S(1)}, bf16[4,64,128]{2,1,0:T(8,128)(2,1)S(1)}, u32[]{:S(2)}, u32[]{:S(2)}) %collective-permute-start.17) | collective-permute-done | bytes 65568 | tf_op jit(solution)/shard_map/ppermute | solution.py:178
  53.9 0.8 %collective-permute-done.18.refs_3_ = bf16[4,64,128]{2,1,0:T(8,128)(2,1)S(1)} collective-permute-done((bf16[4,64,128]{2,1,0:T(8,128)(2,1)S(1)}, bf16[4,64,128]{2,1,0:T(8,128)(2,1)S(1)}, u32[]{:S(2)}, u32[]{:S(2)}) %collective-permute-start.18) | collective-permute-done | bytes 65568 | tf_op jit(solution)/shard_map/ppermute | solution.py:178
  54.7 0.7 %shard_map.83 = (bf16[4,4,64,128]{3,2,1,0:T(8,128)(2,1)S(1)}, f32[8,128]{1,0:T(8,128)S(1)}) custom-call(bf16[2,8,4,64,256]{4,3,2,1,0:T(8,128)(2,1)S(1)} %get-tuple-element.86.w_ref, f32[8,128]{1,0:T(8,128)S(1)} %get-tuple-element.97.t_ref, bf16[4,64,128]{2,1,0:T(8,128)(2,1)S(1)} %collective-permute-done.15.refs_0_, ...), custom_call_target="tpu_custom_call" | custom-call | flops 1 | bytes 1 | tf_op jit(solution)/shard_map/pallas_call | solution.py:149
  55.5 0.8 %collective-permute-start.19 = (bf16[4,4,64,128]{3,2,1,0:T(8,128)(2,1)S(1)}, bf16[4,4,64,128]{3,2,1,0:T(8,128)(2,1)S(1)}, u32[]{:S(2)}, u32[]{:S(2)}) collective-permute-start(bf16[4,4,64,128]{3,2,1,0:T(8,128)(2,1)S(1)} %get-tuple-element.102.x_ref), channel_id=1, source_target_pairs={{0,16},{8,24},{16,0},{24,8},{32,48},{40,56},{48,32},{56,40},{64,80... | collective-permute-start | bytes 786440 | tf_op jit(solution)/shard_map/ppermute | solution.py:175
  56.2 0.4 collective-permute-done.20.y_ref
  56.6 0.4 shard_map.84
  57.0 7.7 %collective-permute-start.21 = (bf16[4,4,64,128]{3,2,1,0:T(8,128)(2,1)S(1)}, bf16[4,4,64,128]{3,2,1,0:T(8,128)(2,1)S(1)}, u32[]{:S(2)}, u32[]{:S(2)}) collective-permute-start(bf16[4,4,64,128]{3,2,1,0:T(8,128)(2,1)S(1)} %get-tuple-element.107.x_ref), channel_id=1, source_target_pairs={{0,8},{8,0},{16,24},{24,16},{32,40},{40,32},{48,56},{56,48},{64,72... | collective-permute-start | bytes 786440 | tf_op jit(solution)/shard_map/ppermute | solution.py:175
  64.7 0.4 shard_map.85
  65.1 2.4 %collective-permute-start.22 = (bf16[4,4,64,128]{3,2,1,0:T(8,128)(2,1)S(1)}, bf16[4,4,64,128]{3,2,1,0:T(8,128)(2,1)S(1)}, u32[]{:S(2)}, u32[]{:S(2)}) collective-permute-start(bf16[4,4,64,128]{3,2,1,0:T(8,128)(2,1)S(1)} %get-tuple-element.109.x_ref), channel_id=1, source_target_pairs={{0,8},{8,0},{16,24},{24,16},{32,40},{40,32},{48,56},{56,48},{64,72... | collective-permute-start | bytes 786440 | tf_op jit(solution)/shard_map/ppermute | solution.py:175
  67.6 0.7 shard_map.86
  68.3 0.5 collective-permute-done.22.y_ref
  68.7 1.5 %shard_map.87 = bf16[8,4,64,128]{3,2,1,0:T(8,128)(2,1)} custom-call(bf16[2,8,4,64,256]{4,3,2,1,0:T(8,128)(2,1)S(1)} %get-tuple-element.84.w_ref, bf16[8,4,64,128]{3,2,1,0:T(8,128)(2,1)S(1)} %get-tuple-element.85.v_ref, f32[8,128]{1,0:T(8,128)S(1)} %get-tuple-element.108.t_ref, bf16[4,4,64,128]{3,2,1,0:T(8,128)(2,1)S(1)} %get-tuple-element.109.x_ref, ...), custom_call_target="tpu_custom_call" | custom-call | flops 1 | bytes 1 | tf_op jit(solution)/shard_map/pallas_call | solution.py:234
  (19 shorter events, 0.0 us)
Async XLA Ops:
  0.0 1.0 %copy-start.1 = (bf16[32,64,128]{2,1,0:T(8,128)(2,1)S(1)}, bf16[32,64,128]{2,1,0:T(8,128)(2,1)}, u32[]{:S(2)}) copy-start(bf16[32,64,128]{2,1,0:T(8,128)(2,1)} %param.7) | copy-start | bytes 1572868
  0.0 1.2 %copy-start.2 = (bf16[32,64,128]{2,1,0:T(8,128)(2,1)S(1)}, bf16[32,64,128]{2,1,0:T(8,128)(2,1)}, u32[]{:S(2)}) copy-start(bf16[32,64,128]{2,1,0:T(8,128)(2,1)} %param.6) | copy-start | bytes 1572868
  1.2 8.3 %copy-start = (bf16[3,32,64,256]{3,2,1,0:T(8,128)(2,1)S(1)}, bf16[3,32,64,256]{3,2,1,0:T(8,128)(2,1)}, u32[]{:S(2)}) copy-start(bf16[3,32,64,256]{3,2,1,0:T(8,128)(2,1)} %param.8) | copy-start | bytes 9437188
  1.5 7.9 %collective-permute-start.2 = (bf16[8,1,64,128]{3,2,1,0:T(8,128)(2,1)S(1)}, bf16[8,1,64,128]{3,2,1,0:T(8,128)(2,1)S(1)}, u32[]{:S(2)}, u32[]{:S(2)}) collective-permute-start(bf16[8,1,64,128]{3,2,1,0:T(8,128)(2,1)S(1)} %get-tuple-element.62.x_ref), channel_id=1, source_target_pairs={{0,128},{8,136},{16,144},{24,152},{32,160},{40,168},{48,176},{56,1... | collective-permute-start | bytes 393224 | tf_op jit(solution)/shard_map/ppermute | solution.py:175
  5.5 7.1 %collective-permute-start.1 = (bf16[8,1,64,128]{3,2,1,0:T(8,128)(2,1)S(1)}, bf16[8,1,64,128]{3,2,1,0:T(8,128)(2,1)S(1)}, u32[]{:S(2)}, u32[]{:S(2)}) collective-permute-start(bf16[8,1,64,128]{3,2,1,0:T(8,128)(2,1)S(1)} %get-tuple-element.61.x_ref), channel_id=1, source_target_pairs={{0,128},{8,136},{16,144},{24,152},{32,160},{40,168},{48,176},{56,1... | collective-permute-start | bytes 393224 | tf_op jit(solution)/shard_map/ppermute | solution.py:175
  6.0 9.5 %collective-permute-start = (bf16[8,1,64,128]{3,2,1,0:T(8,128)(2,1)S(1)}, bf16[8,1,64,128]{3,2,1,0:T(8,128)(2,1)S(1)}, u32[]{:S(2)}, u32[]{:S(2)}) collective-permute-start(bf16[8,1,64,128]{3,2,1,0:T(8,128)(2,1)S(1)} %get-tuple-element.60.x_ref), channel_id=1, source_target_pairs={{0,128},{8,136},{16,144},{24,152},{32,160},{40,168},{48,176},{56,1... | collective-permute-start | bytes 393224 | tf_op jit(solution)/shard_map/ppermute | solution.py:175
  9.4 8.9 %collective-permute-start.6 = (bf16[8,1,64,128]{3,2,1,0:T(8,128)(2,1)S(1)}, bf16[8,1,64,128]{3,2,1,0:T(8,128)(2,1)S(1)}, u32[]{:S(2)}, u32[]{:S(2)}) collective-permute-start(bf16[8,1,64,128]{3,2,1,0:T(8,128)(2,1)S(1)} %get-tuple-element.70.x_ref), channel_id=1, source_target_pairs={{0,128},{8,136},{16,144},{24,152},{32,160},{40,168},{48,176},{56,1... | collective-permute-start | bytes 393224 | tf_op jit(solution)/shard_map/ppermute | solution.py:175
  9.8 9.9 %collective-permute-start.5 = (bf16[8,1,64,128]{3,2,1,0:T(8,128)(2,1)S(1)}, bf16[8,1,64,128]{3,2,1,0:T(8,128)(2,1)S(1)}, u32[]{:S(2)}, u32[]{:S(2)}) collective-permute-start(bf16[8,1,64,128]{3,2,1,0:T(8,128)(2,1)S(1)} %get-tuple-element.69.x_ref), channel_id=1, source_target_pairs={{0,64},{8,72},{16,80},{24,88},{32,96},{40,104},{48,112},{56,120},{... | collective-permute-start | bytes 393224 | tf_op jit(solution)/shard_map/ppermute | solution.py:175
  12.9 10.0 %collective-permute-start.4 = (bf16[8,1,64,128]{3,2,1,0:T(8,128)(2,1)S(1)}, bf16[8,1,64,128]{3,2,1,0:T(8,128)(2,1)S(1)}, u32[]{:S(2)}, u32[]{:S(2)}) collective-permute-start(bf16[8,1,64,128]{3,2,1,0:T(8,128)(2,1)S(1)} %get-tuple-element.68.x_ref), channel_id=1, source_target_pairs={{0,64},{8,72},{16,80},{24,88},{32,96},{40,104},{48,112},{56,120},{... | collective-permute-start | bytes 393224 | tf_op jit(solution)/shard_map/ppermute | solution.py:175
  15.8 10.0 %collective-permute-start.3 = (bf16[8,1,64,128]{3,2,1,0:T(8,128)(2,1)S(1)}, bf16[8,1,64,128]{3,2,1,0:T(8,128)(2,1)S(1)}, u32[]{:S(2)}, u32[]{:S(2)}) collective-permute-start(bf16[8,1,64,128]{3,2,1,0:T(8,128)(2,1)S(1)} %get-tuple-element.67.x_ref), channel_id=1, source_target_pairs={{0,64},{8,72},{16,80},{24,88},{32,96},{40,104},{48,112},{56,120},{... | collective-permute-start | bytes 393224 | tf_op jit(solution)/shard_map/ppermute | solution.py:175
  18.6 10.0 %collective-permute-start.10 = (bf16[8,1,64,128]{3,2,1,0:T(8,128)(2,1)S(1)}, bf16[8,1,64,128]{3,2,1,0:T(8,128)(2,1)S(1)}, u32[]{:S(2)}, u32[]{:S(2)}) collective-permute-start(bf16[8,1,64,128]{3,2,1,0:T(8,128)(2,1)S(1)} %get-tuple-element.78.x_ref), channel_id=1, source_target_pairs={{0,64},{8,72},{16,80},{24,88},{32,96},{40,104},{48,112},{56,120},{... | collective-permute-start | bytes 393224 | tf_op jit(solution)/shard_map/ppermute | solution.py:175
  20.0 11.4 %collective-permute-start.9 = (bf16[8,1,64,128]{3,2,1,0:T(8,128)(2,1)S(1)}, bf16[8,1,64,128]{3,2,1,0:T(8,128)(2,1)S(1)}, u32[]{:S(2)}, u32[]{:S(2)}) collective-permute-start(bf16[8,1,64,128]{3,2,1,0:T(8,128)(2,1)S(1)} %get-tuple-element.77.x_ref), channel_id=1, source_target_pairs={{0,32},{8,40},{16,48},{24,56},{32,0},{40,8},{48,16},{56,24},{64,96... | collective-permute-start | bytes 393224 | tf_op jit(solution)/shard_map/ppermute | solution.py:175
  23.3 8.4 %collective-permute-start.8 = (bf16[8,1,64,128]{3,2,1,0:T(8,128)(2,1)S(1)}, bf16[8,1,64,128]{3,2,1,0:T(8,128)(2,1)S(1)}, u32[]{:S(2)}, u32[]{:S(2)}) collective-permute-start(bf16[8,1,64,128]{3,2,1,0:T(8,128)(2,1)S(1)} %get-tuple-element.76.x_ref), channel_id=1, source_target_pairs={{0,32},{8,40},{16,48},{24,56},{32,0},{40,8},{48,16},{56,24},{64,96... | collective-permute-start | bytes 393224 | tf_op jit(solution)/shard_map/ppermute | solution.py:175
  26.1 6.5 %collective-permute-start.7 = (bf16[8,1,64,128]{3,2,1,0:T(8,128)(2,1)S(1)}, bf16[8,1,64,128]{3,2,1,0:T(8,128)(2,1)S(1)}, u32[]{:S(2)}, u32[]{:S(2)}) collective-permute-start(bf16[8,1,64,128]{3,2,1,0:T(8,128)(2,1)S(1)} %get-tuple-element.75.x_ref), channel_id=1, source_target_pairs={{0,32},{8,40},{16,48},{24,56},{32,0},{40,8},{48,16},{56,24},{64,96... | collective-permute-start | bytes 393224 | tf_op jit(solution)/shard_map/ppermute | solution.py:175
  28.9 6.5 %collective-permute-start.11 = (bf16[8,1,64,128]{3,2,1,0:T(8,128)(2,1)S(1)}, bf16[8,1,64,128]{3,2,1,0:T(8,128)(2,1)S(1)}, u32[]{:S(2)}, u32[]{:S(2)}) collective-permute-start(bf16[8,1,64,128]{3,2,1,0:T(8,128)(2,1)S(1)} %get-tuple-element.87.x_ref), channel_id=1, source_target_pairs={{0,32},{8,40},{16,48},{24,56},{32,0},{40,8},{48,16},{56,24},{64,96... | collective-permute-start | bytes 393224 | tf_op jit(solution)/shard_map/ppermute | solution.py:175
  31.7 1.6 %copy-start.4 = (bf16[2,32,64,256]{3,2,1,0:T(8,128)(2,1)S(1)}, bf16[2,32,64,256]{3,2,1,0:T(8,128)(2,1)}, u32[]{:S(2)}) copy-start(bf16[2,32,64,256]{3,2,1,0:T(8,128)(2,1)} %param.10) | copy-start | bytes 6291460
  32.0 2.0 %copy-start.3 = (bf16[2,32,64,256]{3,2,1,0:T(8,128)(2,1)S(1)}, bf16[2,32,64,256]{3,2,1,0:T(8,128)(2,1)}, u32[]{:S(2)}) copy-start(bf16[2,32,64,256]{3,2,1,0:T(8,128)(2,1)} %param.9) | copy-start | bytes 6291460
  32.0 2.0 %copy-start.5 = (bf16[32,64,128]{2,1,0:T(8,128)(2,1)S(1)}, bf16[32,64,128]{2,1,0:T(8,128)(2,1)}, u32[]{:S(2)}) copy-start(bf16[32,64,128]{2,1,0:T(8,128)(2,1)} %param.11) | copy-start | bytes 1572868
  35.7 10.5 %collective-permute-start.12 = (bf16[4,64,128]{2,1,0:T(8,128)(2,1)S(1)}, bf16[4,64,128]{2,1,0:T(8,128)(2,1)S(1)}, u32[]{:S(2)}, u32[]{:S(2)}) collective-permute-start(bf16[4,64,128]{2,1,0:T(8,128)(2,1)S(1)} %get-tuple-element.94), channel_id=1, source_target_pairs={{0,2},{1,3},{2,0},{3,1},{4,6},{5,7},{6,4},{7,5},{8,10},{9,11},{10,... | collective-permute-start | bytes 196616 | tf_op jit(solution)/shard_map/ppermute | solution.py:178
  38.8 10.6 %collective-permute-start.13 = (bf16[4,64,128]{2,1,0:T(8,128)(2,1)S(1)}, bf16[4,64,128]{2,1,0:T(8,128)(2,1)S(1)}, u32[]{:S(2)}, u32[]{:S(2)}) collective-permute-start(bf16[4,64,128]{2,1,0:T(8,128)(2,1)S(1)} %get-tuple-element.95), channel_id=1, source_target_pairs={{0,4},{1,5},{2,6},{3,7},{4,0},{5,1},{6,2},{7,3},{8,12},{9,13},{10,... | collective-permute-start | bytes 196616 | tf_op jit(solution)/shard_map/ppermute | solution.py:178
  43.9 6.4 %collective-permute-start.14 = (bf16[4,64,128]{2,1,0:T(8,128)(2,1)S(1)}, bf16[4,64,128]{2,1,0:T(8,128)(2,1)S(1)}, u32[]{:S(2)}, u32[]{:S(2)}) collective-permute-start(bf16[4,64,128]{2,1,0:T(8,128)(2,1)S(1)} %get-tuple-element.96), channel_id=1, source_target_pairs={{0,6},{1,7},{2,4},{3,5},{4,2},{5,3},{6,0},{7,1},{8,14},{9,15},{10,... | collective-permute-start | bytes 196616 | tf_op jit(solution)/shard_map/ppermute | solution.py:178
  43.9 8.2 %collective-permute-start.15 = (bf16[4,64,128]{2,1,0:T(8,128)(2,1)S(1)}, bf16[4,64,128]{2,1,0:T(8,128)(2,1)S(1)}, u32[]{:S(2)}, u32[]{:S(2)}) collective-permute-start(bf16[4,64,128]{2,1,0:T(8,128)(2,1)S(1)} %get-tuple-element.98), channel_id=1, source_target_pairs={{0,1},{1,0},{2,3},{3,2},{4,5},{5,4},{6,7},{7,6},{8,9},{9,8},{10,11... | collective-permute-start | bytes 196616 | tf_op jit(solution)/shard_map/ppermute | solution.py:178
  44.7 7.4 %collective-permute-start.16 = (bf16[4,64,128]{2,1,0:T(8,128)(2,1)S(1)}, bf16[4,64,128]{2,1,0:T(8,128)(2,1)S(1)}, u32[]{:S(2)}, u32[]{:S(2)}) collective-permute-start(bf16[4,64,128]{2,1,0:T(8,128)(2,1)S(1)} %get-tuple-element.99), channel_id=1, source_target_pairs={{0,3},{1,2},{2,1},{3,0},{4,7},{5,6},{6,5},{7,4},{8,11},{9,10},{10,... | collective-permute-start | bytes 196616 | tf_op jit(solution)/shard_map/ppermute | solution.py:178
  46.3 7.6 %collective-permute-start.17 = (bf16[4,64,128]{2,1,0:T(8,128)(2,1)S(1)}, bf16[4,64,128]{2,1,0:T(8,128)(2,1)S(1)}, u32[]{:S(2)}, u32[]{:S(2)}) collective-permute-start(bf16[4,64,128]{2,1,0:T(8,128)(2,1)S(1)} %get-tuple-element.100), channel_id=1, source_target_pairs={{0,5},{1,4},{2,7},{3,6},{4,1},{5,0},{6,3},{7,2},{8,13},{9,12},{10,... | collective-permute-start | bytes 196616 | tf_op jit(solution)/shard_map/ppermute | solution.py:178
  49.4 5.3 %collective-permute-start.18 = (bf16[4,64,128]{2,1,0:T(8,128)(2,1)S(1)}, bf16[4,64,128]{2,1,0:T(8,128)(2,1)S(1)}, u32[]{:S(2)}, u32[]{:S(2)}) collective-permute-start(bf16[4,64,128]{2,1,0:T(8,128)(2,1)S(1)} %get-tuple-element.101), channel_id=1, source_target_pairs={{0,7},{1,6},{2,5},{3,4},{4,3},{5,2},{6,1},{7,0},{8,15},{9,14},{10,... | collective-permute-start | bytes 196616 | tf_op jit(solution)/shard_map/ppermute | solution.py:178
  51.0 5.6 %collective-permute-start.20 = (bf16[4,4,64,128]{3,2,1,0:T(8,128)(2,1)S(1)}, bf16[4,4,64,128]{3,2,1,0:T(8,128)(2,1)S(1)}, u32[]{:S(2)}, u32[]{:S(2)}) collective-permute-start(bf16[4,4,64,128]{3,2,1,0:T(8,128)(2,1)S(1)} %get-tuple-element.103.x_ref), channel_id=1, source_target_pairs={{0,16},{8,24},{16,0},{24,8},{32,48},{40,56},{48,32},{56,40},{64,80... | collective-permute-start | bytes 786440 | tf_op jit(solution)/shard_map/ppermute | solution.py:175
  55.5 9.3 %collective-permute-start.19 = (bf16[4,4,64,128]{3,2,1,0:T(8,128)(2,1)S(1)}, bf16[4,4,64,128]{3,2,1,0:T(8,128)(2,1)S(1)}, u32[]{:S(2)}, u32[]{:S(2)}) collective-permute-start(bf16[4,4,64,128]{3,2,1,0:T(8,128)(2,1)S(1)} %get-tuple-element.102.x_ref), channel_id=1, source_target_pairs={{0,16},{8,24},{16,0},{24,8},{32,48},{40,56},{48,32},{56,40},{64,80... | collective-permute-start | bytes 786440 | tf_op jit(solution)/shard_map/ppermute | solution.py:175
  57.0 10.6 %collective-permute-start.21 = (bf16[4,4,64,128]{3,2,1,0:T(8,128)(2,1)S(1)}, bf16[4,4,64,128]{3,2,1,0:T(8,128)(2,1)S(1)}, u32[]{:S(2)}, u32[]{:S(2)}) collective-permute-start(bf16[4,4,64,128]{3,2,1,0:T(8,128)(2,1)S(1)} %get-tuple-element.107.x_ref), channel_id=1, source_target_pairs={{0,8},{8,0},{16,24},{24,16},{32,40},{40,32},{48,56},{56,48},{64,72... | collective-permute-start | bytes 786440 | tf_op jit(solution)/shard_map/ppermute | solution.py:175
  65.1 3.6 %collective-permute-start.22 = (bf16[4,4,64,128]{3,2,1,0:T(8,128)(2,1)S(1)}, bf16[4,4,64,128]{3,2,1,0:T(8,128)(2,1)S(1)}, u32[]{:S(2)}, u32[]{:S(2)}) collective-permute-start(bf16[4,4,64,128]{3,2,1,0:T(8,128)(2,1)S(1)} %get-tuple-element.109.x_ref), channel_id=1, source_target_pairs={{0,8},{8,0},{16,24},{24,16},{32,40},{40,32},{48,56},{56,48},{64,72... | collective-permute-start | bytes 786440 | tf_op jit(solution)/shard_map/ppermute | solution.py:175

commit v4 on v3

--- a/solution.py
+++ b/solution.py
@@ -8,10 +8,11 @@
 from jax.sharding import PartitionSpec as P
 
 WIDTHS = (1, 1, 1, 1)
-PIECES = 1
+PIECES = (1, 1)
+ORDER = ((0, 4, 6, 2), (7, 5, 1, 3))
 PLAN = (
     "T0", "L0", "L1", "L2", "L3", "U00", "U01", "U02", "U03", "U10", "U11", "U12", "U13", "U20", "U21",
-    "U22", "W0", "U23", "M0", "M1", "D00", "D01", "E0", "E1",
+    "W0", "U22", "U23", "M0", "M1", "D00", "D01", "E0", "E1",
 )
 VMEM = pl.BlockSpec(memory_space=pltpu.VMEM)
 ANY = pl.BlockSpec(memory_space=pl.ANY)
@@ -86,9 +87,10 @@
             outs[q][at + b] = product(w_ref[step, a, first + b], [x_ref[a, b], y_ref[a, b]])
 
 
-def middle_kernel(gaps, w_ref, t_ref, *refs):
+def middle_kernel(gaps, order, w_ref, t_ref, *refs):
     count = len(gaps)
-    got, outs, u_ref, s_ref = refs[:count], refs[count:-2], refs[-2], refs[-1]
+    got = [refs[order.index(q)] for q in gaps]
+    outs, u_ref, s_ref = refs[count:-2], refs[-2], refs[-1]
     u_ref[...] = t_ref[...]
     me = lax.axis_index("mid")
     width = outs[0].shape[1]
@@ -124,10 +126,10 @@
 def store_kernel(places, step, w_ref, v_ref, t_ref, x_ref, y_ref, *refs):
     *earlier, o_ref, r_ref, sems = refs
     me = lax.axis_index("mid")
-    width = r_ref.shape[1]
 
     def stores(c, source):
         gaps, first = places[c]
+        width = source.shape[1]
         return [
             pltpu.make_async_copy(source.at[i], o_ref.at[me ^ q, first:first + width], sems.at[c * len(gaps) + i])
             for i, q in enumerate(gaps)
@@ -137,10 +139,12 @@
     for store in moving:
         store.start()
     gaps, first = places[-1]
-    finish(gaps, first, step, w_ref, v_ref, x_ref, y_ref, r_ref)
     final = stores(len(places) - 1, r_ref)
-    for store in final:
-        store.start()
+    for i, q in enumerate(gaps):
+        for b in range(x_ref.shape[1]):
+            value = product(w_ref[step, me ^ q, first + b], [x_ref[i, b], y_ref[i, b]])
+            r_ref[i, b] = product(v_ref[me ^ q, first + b], [value])
+        final[i].start()
     for store in moving + final:
         store.wait()
 
@@ -213,13 +217,14 @@
         elif kind == "M":
             gaps = tuple(range(c, mid_size, 2))
             tall = (len(gaps), inner)
-            fields, token = call(name, part(middle_kernel, gaps), [(len(gaps), inner // PIECES) + box] * PIECES,
-                                 (mid_w, token, *[got[q] for q in gaps]), [VMEM] * (2 + len(gaps)), [VMEM] * PIECES,
+            count = PIECES[c]
+            fields, token = call(name, part(middle_kernel, gaps, ORDER[c]), [(len(gaps), inner // count) + box] * count,
+                                 (mid_w, token, *[got[q] for q in ORDER[c]]), [VMEM] * (2 + len(gaps)), [VMEM] * count,
                                  token, scratch_shapes=[pltpu.VMEM(tall + box, jnp.bfloat16)])
             for piece, value in enumerate(fields):
-                e = c * PIECES + piece
+                e = sum(PIECES[:c]) + piece
                 field[e], other[e] = value, swap(value, lower_count - 1)
-                place[e] = (gaps, piece * (inner // PIECES))
+                place[e] = (gaps, piece * (inner // count))
         elif kind == "D":
             (field[c],), token = call(name, part(lower_kernel, *place[c], step), [field[c].shape],
                                       (low_w, field[c], other[c], token), [VMEM] * 4, [VMEM], token)
@@ -236,7 +241,7 @@
                 out_shape=jax.ShapeDtypeStruct(samples.shape, jnp.bfloat16),
                 in_specs=[VMEM] * len(args),
                 out_specs=ANY,
-                scratch_shapes=[pltpu.VMEM(field[c].shape, jnp.bfloat16), DMA((mid_size * PIECES,))],
+                scratch_shapes=[pltpu.VMEM(field[c].shape, jnp.bfloat16), DMA((mid_size // 2 * len(places),))],
                 compiler_params=pltpu.CompilerParams(vmem_limit_bytes=8 << 20),
                 cost_estimate=pl.CostEstimate(flops=1, bytes_accessed=1, transcendentals=0),
             )(*args)

time: 71.1 us -> 70 us (0.985)
  no operation moved by 1% of the time
where the time goes in v4:
time: 70 us; the launch traced here: 69.9 us
  starting transfers between devices  45.5 us (65%)
  waiting for transfers between devices  11.5 us (16%)
  Pallas kernels  9.54 us (14%)
  local copies, waits for them, and re-layouts  2.92 us (4%)
    ppermute x16, starting transfers between devices, swap(): lax.ppermute(block, 'lvl', [(i, i ^ 1 << bit) for i in range(lvl_size)])  31.2 us
    ppermute x7, starting transfers between devices, across(): return lax.ppermute(block, 'mid', [(i, i ^ gap) for i in range(mid_size)])  14.3 us
    ppermute x16, waiting for transfers between devices, swap(): lax.ppermute(block, 'lvl', [(i, i ^ 1 << bit) for i in range(lvl_size)])  9.08 us
    pallas_call x23, Pallas kernels, call(): pl.pallas_call(kernel, out_shape=[jax.ShapeDtypeStruct(shape, jnp.bfloat1...  8.13 us
    unnamed x12, local copies, waits for them, and re-layouts  2.92 us
    ppermute x7, waiting for transfers between devices, across(): return lax.ppermute(block, 'mid', [(i, i ^ gap) for i in range(mid_size)])  2.4 us
    pallas_call x1, Pallas kernels, on_device(): pl.pallas_call(part(store_kernel, places, lower_count - 1), out_shape=jax...  1.41 us
  transfers between devices with their start and end apart: 23, of which 10 were waited for; matrix products, arithmetic and copies ran while one was open for 0% of the time, Pallas kernels for 11%

profile of v4, /device:TPU:1, one launch (start us, length us, event | category | flops | bytes accessed | tf_op | source)
XLA Modules:
  0.0 69.9 jit_solution(3647372900449372281)
XLA Ops:
  0.0 1.0 %copy-done.1 = bf16[32,64,128]{2,1,0:T(8,128)(2,1)S(1)} copy-done((bf16[32,64,128]{2,1,0:T(8,128)(2,1)S(1)}, bf16[32,64,128]{2,1,0:T(8,128)(2,1)}, u32[]{:S(2)}) %copy-start.1) | copy-done | bytes 524312
  1.0 0.2 copy-done.2
  1.2 0.3 shard_map.65
  1.5 3.7 %collective-permute-start.1 = (bf16[8,1,64,128]{3,2,1,0:T(8,128)(2,1)S(1)}, bf16[8,1,64,128]{3,2,1,0:T(8,128)(2,1)S(1)}, u32[]{:S(2)}, u32[]{:S(2)}) collective-permute-start(bf16[8,1,64,128]{3,2,1,0:T(8,128)(2,1)S(1)} %get-tuple-element.60.x_ref), channel_id=1, source_target_pairs={{0,128},{8,136},{16,144},{24,152},{32,160},{40,168},{48,176},{56,1... | collective-permute-start | bytes 393224 | tf_op jit(solution)/shard_map/ppermute | solution.py:179
  5.2 0.3 shard_map.66
  5.5 0.1 collective-permute-start
  5.6 0.3 shard_map.67
  6.0 3.0 %collective-permute-start.5 = (bf16[8,1,64,128]{3,2,1,0:T(8,128)(2,1)S(1)}, bf16[8,1,64,128]{3,2,1,0:T(8,128)(2,1)S(1)}, u32[]{:S(2)}, u32[]{:S(2)}) collective-permute-start(bf16[8,1,64,128]{3,2,1,0:T(8,128)(2,1)S(1)} %get-tuple-element.68.x_ref), channel_id=1, source_target_pairs={{0,128},{8,136},{16,144},{24,152},{32,160},{40,168},{48,176},{56,1... | collective-permute-start | bytes 393224 | tf_op jit(solution)/shard_map/ppermute | solution.py:179
  9.0 0.3 shard_map.68
  9.4 0.1 collective-permute-start.4
  9.5 0.3 shard_map.69
  9.8 1.5 %collective-permute-start.3 = (bf16[8,1,64,128]{3,2,1,0:T(8,128)(2,1)S(1)}, bf16[8,1,64,128]{3,2,1,0:T(8,128)(2,1)S(1)}, u32[]{:S(2)}, u32[]{:S(2)}) collective-permute-start(bf16[8,1,64,128]{3,2,1,0:T(8,128)(2,1)S(1)} %get-tuple-element.66.x_ref), channel_id=1, source_target_pairs={{0,64},{8,72},{16,80},{24,88},{32,96},{40,104},{48,112},{56,120},{... | collective-permute-start | bytes 393224 | tf_op jit(solution)/shard_map/ppermute | solution.py:179
  11.3 1.4 %collective-permute-done.y_ref = bf16[8,1,64,128]{3,2,1,0:T(8,128)(2,1)S(1)} collective-permute-done((bf16[8,1,64,128]{3,2,1,0:T(8,128)(2,1)S(1)}, bf16[8,1,64,128]{3,2,1,0:T(8,128)(2,1)S(1)}, u32[]{:S(2)}, u32[]{:S(2)}) %collective-permute-start) | collective-permute-done | bytes 131104 | tf_op jit(solution)/shard_map/ppermute | solution.py:179
  12.6 0.3 shard_map.70
  12.9 0.1 collective-permute-start.2
  13.0 2.4 %collective-permute-done.5.y_ref = bf16[8,1,64,128]{3,2,1,0:T(8,128)(2,1)S(1)} collective-permute-done((bf16[8,1,64,128]{3,2,1,0:T(8,128)(2,1)S(1)}, bf16[8,1,64,128]{3,2,1,0:T(8,128)(2,1)S(1)}, u32[]{:S(2)}, u32[]{:S(2)}) %collective-permute-start.5) | collective-permute-done | bytes 131104 | tf_op jit(solution)/shard_map/ppermute | solution.py:179
  15.5 0.3 shard_map.71
  15.8 0.1 collective-permute-start.9
  15.9 2.4 %collective-permute-done.4.y_ref = bf16[8,1,64,128]{3,2,1,0:T(8,128)(2,1)S(1)} collective-permute-done((bf16[8,1,64,128]{3,2,1,0:T(8,128)(2,1)S(1)}, bf16[8,1,64,128]{3,2,1,0:T(8,128)(2,1)S(1)}, u32[]{:S(2)}, u32[]{:S(2)}) %collective-permute-start.4) | collective-permute-done | bytes 131104 | tf_op jit(solution)/shard_map/ppermute | solution.py:179
  18.3 0.3 shard_map.72
  18.6 0.1 collective-permute-start.8
  18.7 1.0 %collective-permute-done.3.y_ref = bf16[8,1,64,128]{3,2,1,0:T(8,128)(2,1)S(1)} collective-permute-done((bf16[8,1,64,128]{3,2,1,0:T(8,128)(2,1)S(1)}, bf16[8,1,64,128]{3,2,1,0:T(8,128)(2,1)S(1)}, u32[]{:S(2)}, u32[]{:S(2)}) %collective-permute-start.3) | collective-permute-done | bytes 131104 | tf_op jit(solution)/shard_map/ppermute | solution.py:179
  19.6 0.3 shard_map.73
  20.0 3.0 %collective-permute-start.7 = (bf16[8,1,64,128]{3,2,1,0:T(8,128)(2,1)S(1)}, bf16[8,1,64,128]{3,2,1,0:T(8,128)(2,1)S(1)}, u32[]{:S(2)}, u32[]{:S(2)}) collective-permute-start(bf16[8,1,64,128]{3,2,1,0:T(8,128)(2,1)S(1)} %get-tuple-element.74.x_ref), channel_id=1, source_target_pairs={{0,32},{8,40},{16,48},{24,56},{32,0},{40,8},{48,16},{56,24},{64,96... | collective-permute-start | bytes 393224 | tf_op jit(solution)/shard_map/ppermute | solution.py:179
  23.0 0.3 shard_map.74
  23.3 2.5 %collective-permute-start.6 = (bf16[8,1,64,128]{3,2,1,0:T(8,128)(2,1)S(1)}, bf16[8,1,64,128]{3,2,1,0:T(8,128)(2,1)S(1)}, u32[]{:S(2)}, u32[]{:S(2)}) collective-permute-start(bf16[8,1,64,128]{3,2,1,0:T(8,128)(2,1)S(1)} %get-tuple-element.73.x_ref), channel_id=1, source_target_pairs={{0,32},{8,40},{16,48},{24,56},{32,0},{40,8},{48,16},{56,24},{64,96... | collective-permute-start | bytes 393224 | tf_op jit(solution)/shard_map/ppermute | solution.py:179
  25.8 0.3 shard_map.75
  26.1 2.5 %collective-permute-start.11 = (bf16[8,1,64,128]{3,2,1,0:T(8,128)(2,1)S(1)}, bf16[8,1,64,128]{3,2,1,0:T(8,128)(2,1)S(1)}, u32[]{:S(2)}, u32[]{:S(2)}) collective-permute-start(bf16[8,1,64,128]{3,2,1,0:T(8,128)(2,1)S(1)} %get-tuple-element.86.x_ref), channel_id=1, source_target_pairs={{0,32},{8,40},{16,48},{24,56},{32,0},{40,8},{48,16},{56,24},{64,96... | collective-permute-start | bytes 393224 | tf_op jit(solution)/shard_map/ppermute | solution.py:179
  28.6 0.3 shard_map.76
  28.9 2.5 %collective-permute-start.10 = (bf16[8,1,64,128]{3,2,1,0:T(8,128)(2,1)S(1)}, bf16[8,1,64,128]{3,2,1,0:T(8,128)(2,1)S(1)}, u32[]{:S(2)}, u32[]{:S(2)}) collective-permute-start(bf16[8,1,64,128]{3,2,1,0:T(8,128)(2,1)S(1)} %get-tuple-element.85.x_ref), channel_id=1, source_target_pairs={{0,32},{8,40},{16,48},{24,56},{32,0},{40,8},{48,16},{56,24},{64,96... | collective-permute-start | bytes 393224 | tf_op jit(solution)/shard_map/ppermute | solution.py:179
  31.4 0.0 collective-permute-done.7.y_ref
  31.4 0.3 shard_map.77
  31.7 0.0 copy-start.3
  31.7 0.0 copy-start.5
  31.7 0.0 collective-permute-done.6.y_ref
  31.7 0.3 shard_map.78
  32.0 1.0 %copy-done.4 = bf16[2,32,64,256]{3,2,1,0:T(8,128)(2,1)S(1)} copy-done((bf16[2,32,64,256]{3,2,1,0:T(8,128)(2,1)S(1)}, bf16[2,32,64,256]{3,2,1,0:T(8,128)(2,1)}, u32[]{:S(2)}) %copy-start.4) | copy-done | bytes 2097176
  33.0 0.7 %copy-done.3 = bf16[2,32,64,256]{3,2,1,0:T(8,128)(2,1)S(1)} copy-done((bf16[2,32,64,256]{3,2,1,0:T(8,128)(2,1)S(1)}, bf16[2,32,64,256]{3,2,1,0:T(8,128)(2,1)}, u32[]{:S(2)}) %copy-start.3) | copy-done | bytes 2097176
  33.7 0.1 copy-done.5
  33.8 0.3 shard_map.79
  34.1 0.3 shard_map.80
  34.4 1.0 %collective-permute-done.10.y_ref = bf16[8,1,64,128]{3,2,1,0:T(8,128)(2,1)S(1)} collective-permute-done((bf16[8,1,64,128]{3,2,1,0:T(8,128)(2,1)S(1)}, bf16[8,1,64,128]{3,2,1,0:T(8,128)(2,1)S(1)}, u32[]{:S(2)}, u32[]{:S(2)}) %collective-permute-start.10) | collective-permute-done | bytes 131104 | tf_op jit(solution)/shard_map/ppermute | solution.py:179
  35.4 0.3 shard_map.81
  35.7 7.0 %collective-permute-start.12 = (bf16[4,64,128]{2,1,0:T(8,128)(2,1)S(1)}, bf16[4,64,128]{2,1,0:T(8,128)(2,1)S(1)}, u32[]{:S(2)}, u32[]{:S(2)}) collective-permute-start(bf16[4,64,128]{2,1,0:T(8,128)(2,1)S(1)} %get-tuple-element.94), channel_id=1, source_target_pairs={{0,4},{1,5},{2,6},{3,7},{4,0},{5,1},{6,2},{7,3},{8,12},{9,13},{10,... | collective-permute-start | bytes 196616 | tf_op jit(solution)/shard_map/ppermute | solution.py:182
  42.7 1.2 %collective-permute-start.14 = (bf16[4,64,128]{2,1,0:T(8,128)(2,1)S(1)}, bf16[4,64,128]{2,1,0:T(8,128)(2,1)S(1)}, u32[]{:S(2)}, u32[]{:S(2)}) collective-permute-start(bf16[4,64,128]{2,1,0:T(8,128)(2,1)S(1)} %get-tuple-element.96), channel_id=1, source_target_pairs={{0,2},{1,3},{2,0},{3,1},{4,6},{5,7},{6,4},{7,5},{8,10},{9,11},{10,... | collective-permute-start | bytes 196616 | tf_op jit(solution)/shard_map/ppermute | solution.py:182
  43.9 3.1 %collective-permute-start.15 = (bf16[4,64,128]{2,1,0:T(8,128)(2,1)S(1)}, bf16[4,64,128]{2,1,0:T(8,128)(2,1)S(1)}, u32[]{:S(2)}, u32[]{:S(2)}) collective-permute-start(bf16[4,64,128]{2,1,0:T(8,128)(2,1)S(1)} %get-tuple-element.98), channel_id=1, source_target_pairs={{0,7},{1,6},{2,5},{3,4},{4,3},{5,2},{6,1},{7,0},{8,15},{9,14},{10,... | collective-permute-start | bytes 196616 | tf_op jit(solution)/shard_map/ppermute | solution.py:182
  47.1 1.3 %collective-permute-start.16 = (bf16[4,64,128]{2,1,0:T(8,128)(2,1)S(1)}, bf16[4,64,128]{2,1,0:T(8,128)(2,1)S(1)}, u32[]{:S(2)}, u32[]{:S(2)}) collective-permute-start(bf16[4,64,128]{2,1,0:T(8,128)(2,1)S(1)} %get-tuple-element.99), channel_id=1, source_target_pairs={{0,5},{1,4},{2,7},{3,6},{4,1},{5,0},{6,3},{7,2},{8,13},{9,12},{10,... | collective-permute-start | bytes 196616 | tf_op jit(solution)/shard_map/ppermute | solution.py:182
  48.4 0.3 collective-permute-start.17
  48.7 0.2 collective-permute-done.13.refs_2_
  48.9 1.4 %collective-permute-start.18 = (bf16[4,64,128]{2,1,0:T(8,128)(2,1)S(1)}, bf16[4,64,128]{2,1,0:T(8,128)(2,1)S(1)}, u32[]{:S(2)}, u32[]{:S(2)}) collective-permute-start(bf16[4,64,128]{2,1,0:T(8,128)(2,1)S(1)} %get-tuple-element.101), channel_id=1, source_target_pairs={{0,3},{1,2},{2,1},{3,0},{4,7},{5,6},{6,5},{7,4},{8,11},{9,10},{10,... | collective-permute-start | bytes 196616 | tf_op jit(solution)/shard_map/ppermute | solution.py:182
  50.3 0.7 %shard_map.82 = (bf16[4,4,64,128]{3,2,1,0:T(8,128)(2,1)S(1)}, f32[8,128]{1,0:T(8,128)S(1)}) custom-call(bf16[2,8,4,64,256]{4,3,2,1,0:T(8,128)(2,1)S(1)} %get-tuple-element.84.w_ref, f32[8,128]{1,0:T(8,128)S(1)} %get-tuple-element.92.t_ref, bf16[4,64,128]{2,1,0:T(8,128)(2,1)S(1)} %get-tuple-element.93.refs_0_, ...), custom_call_target="tpu_custom_call" | custom-call | flops 1 | bytes 1 | tf_op jit(solution)/shard_map/pallas_call | solution.py:153
  51.1 1.1 %collective-permute-start.20 = (bf16[4,4,64,128]{3,2,1,0:T(8,128)(2,1)S(1)}, bf16[4,4,64,128]{3,2,1,0:T(8,128)(2,1)S(1)}, u32[]{:S(2)}, u32[]{:S(2)}) collective-permute-start(bf16[4,4,64,128]{3,2,1,0:T(8,128)(2,1)S(1)} %get-tuple-element.103.x_ref), channel_id=1, source_target_pairs={{0,16},{8,24},{16,0},{24,8},{32,48},{40,56},{48,32},{56,40},{64,80... | collective-permute-start | bytes 786440 | tf_op jit(solution)/shard_map/ppermute | solution.py:179
  52.2 1.5 %collective-permute-done.16.refs_1_ = bf16[4,64,128]{2,1,0:T(8,128)(2,1)S(1)} collective-permute-done((bf16[4,64,128]{2,1,0:T(8,128)(2,1)S(1)}, bf16[4,64,128]{2,1,0:T(8,128)(2,1)S(1)}, u32[]{:S(2)}, u32[]{:S(2)}) %collective-permute-start.16) | collective-permute-done | bytes 65568 | tf_op jit(solution)/shard_map/ppermute | solution.py:182
  53.7 0.7 collective-permute-done.18.refs_3_
  54.3 0.7 %shard_map.83 = (bf16[4,4,64,128]{3,2,1,0:T(8,128)(2,1)S(1)}, f32[8,128]{1,0:T(8,128)S(1)}) custom-call(bf16[2,8,4,64,256]{4,3,2,1,0:T(8,128)(2,1)S(1)} %get-tuple-element.84.w_ref, f32[8,128]{1,0:T(8,128)S(1)} %get-tuple-element.97.t_ref, bf16[4,64,128]{2,1,0:T(8,128)(2,1)S(1)} %collective-permute-done.15.refs_0_, ...), custom_call_target="tpu_custom_call" | custom-call | flops 1 | bytes 1 | tf_op jit(solution)/shard_map/pallas_call | solution.py:153
  55.0 1.2 %collective-permute-start.19 = (bf16[4,4,64,128]{3,2,1,0:T(8,128)(2,1)S(1)}, bf16[4,4,64,128]{3,2,1,0:T(8,128)(2,1)S(1)}, u32[]{:S(2)}, u32[]{:S(2)}) collective-permute-start(bf16[4,4,64,128]{3,2,1,0:T(8,128)(2,1)S(1)} %get-tuple-element.102.x_ref), channel_id=1, source_target_pairs={{0,16},{8,24},{16,0},{24,8},{32,48},{40,56},{48,32},{56,40},{64,80... | collective-permute-start | bytes 786440 | tf_op jit(solution)/shard_map/ppermute | solution.py:179
  56.2 0.4 collective-permute-done.20.y_ref
  56.7 0.4 shard_map.84
  57.0 7.3 %collective-permute-start.21 = (bf16[4,4,64,128]{3,2,1,0:T(8,128)(2,1)S(1)}, bf16[4,4,64,128]{3,2,1,0:T(8,128)(2,1)S(1)}, u32[]{:S(2)}, u32[]{:S(2)}) collective-permute-start(bf16[4,4,64,128]{3,2,1,0:T(8,128)(2,1)S(1)} %get-tuple-element.107.x_ref), channel_id=1, source_target_pairs={{0,8},{8,0},{16,24},{24,16},{32,40},{40,32},{48,56},{56,48},{64,72... | collective-permute-start | bytes 786440 | tf_op jit(solution)/shard_map/ppermute | solution.py:179
  64.3 0.4 shard_map.85
  64.7 2.4 %collective-permute-start.22 = (bf16[4,4,64,128]{3,2,1,0:T(8,128)(2,1)S(1)}, bf16[4,4,64,128]{3,2,1,0:T(8,128)(2,1)S(1)}, u32[]{:S(2)}, u32[]{:S(2)}) collective-permute-start(bf16[4,4,64,128]{3,2,1,0:T(8,128)(2,1)S(1)} %get-tuple-element.109.x_ref), channel_id=1, source_target_pairs={{0,8},{8,0},{16,24},{24,16},{32,40},{40,32},{48,56},{56,48},{64,72... | collective-permute-start | bytes 786440 | tf_op jit(solution)/shard_map/ppermute | solution.py:179
  67.1 0.7 %shard_map.86 = (bf16[4,4,64,128]{3,2,1,0:T(8,128)(2,1)S(1)}, f32[8,128]{1,0:T(8,128)S(1)}) custom-call(bf16[2,8,4,64,256]{4,3,2,1,0:T(8,128)(2,1)S(1)} %get-tuple-element.82.w_ref, bf16[8,4,64,128]{3,2,1,0:T(8,128)(2,1)S(1)} %get-tuple-element.83.v_ref, f32[8,128]{1,0:T(8,128)S(1)} %get-tuple-element.106.t_ref, ...), custom_call_target="tpu_custom_call" | custom-call | flops 1 | bytes 1 | tf_op jit(solution)/shard_map/pallas_call | solution.py:153
  67.8 0.5 collective-permute-done.22.y_ref
  68.3 1.4 %shard_map.87 = bf16[8,4,64,128]{3,2,1,0:T(8,128)(2,1)} custom-call(bf16[2,8,4,64,256]{4,3,2,1,0:T(8,128)(2,1)S(1)} %get-tuple-element.82.w_ref, bf16[8,4,64,128]{3,2,1,0:T(8,128)(2,1)S(1)} %get-tuple-element.83.v_ref, f32[8,128]{1,0:T(8,128)S(1)} %get-tuple-element.108.t_ref, bf16[4,4,64,128]{3,2,1,0:T(8,128)(2,1)S(1)} %get-tuple-element.109.x_ref, ...), custom_call_target="tpu_custom_call" | custom-call | flops 1 | bytes 1 | tf_op jit(solution)/shard_map/pallas_call | solution.py:239
  (19 shorter events, 0.0 us)
Async XLA Ops:
  0.0 1.0 %copy-start.1 = (bf16[32,64,128]{2,1,0:T(8,128)(2,1)S(1)}, bf16[32,64,128]{2,1,0:T(8,128)(2,1)}, u32[]{:S(2)}) copy-start(bf16[32,64,128]{2,1,0:T(8,128)(2,1)} %param.7) | copy-start | bytes 1572868
  0.0 1.2 %copy-start.2 = (bf16[32,64,128]{2,1,0:T(8,128)(2,1)S(1)}, bf16[32,64,128]{2,1,0:T(8,128)(2,1)}, u32[]{:S(2)}) copy-start(bf16[32,64,128]{2,1,0:T(8,128)(2,1)} %param.6) | copy-start | bytes 1572868
  1.2 8.3 %copy-start = (bf16[3,32,64,256]{3,2,1,0:T(8,128)(2,1)S(1)}, bf16[3,32,64,256]{3,2,1,0:T(8,128)(2,1)}, u32[]{:S(2)}) copy-start(bf16[3,32,64,256]{3,2,1,0:T(8,128)(2,1)} %param.8) | copy-start | bytes 9437188
  1.5 7.9 %collective-permute-start.1 = (bf16[8,1,64,128]{3,2,1,0:T(8,128)(2,1)S(1)}, bf16[8,1,64,128]{3,2,1,0:T(8,128)(2,1)S(1)}, u32[]{:S(2)}, u32[]{:S(2)}) collective-permute-start(bf16[8,1,64,128]{3,2,1,0:T(8,128)(2,1)S(1)} %get-tuple-element.60.x_ref), channel_id=1, source_target_pairs={{0,128},{8,136},{16,144},{24,152},{32,160},{40,168},{48,176},{56,1... | collective-permute-start | bytes 393224 | tf_op jit(solution)/shard_map/ppermute | solution.py:179
  5.5 7.1 %collective-permute-start = (bf16[8,1,64,128]{3,2,1,0:T(8,128)(2,1)S(1)}, bf16[8,1,64,128]{3,2,1,0:T(8,128)(2,1)S(1)}, u32[]{:S(2)}, u32[]{:S(2)}) collective-permute-start(bf16[8,1,64,128]{3,2,1,0:T(8,128)(2,1)S(1)} %get-tuple-element.59.x_ref), channel_id=1, source_target_pairs={{0,128},{8,136},{16,144},{24,152},{32,160},{40,168},{48,176},{56,1... | collective-permute-start | bytes 393224 | tf_op jit(solution)/shard_map/ppermute | solution.py:179
  6.0 9.5 %collective-permute-start.5 = (bf16[8,1,64,128]{3,2,1,0:T(8,128)(2,1)S(1)}, bf16[8,1,64,128]{3,2,1,0:T(8,128)(2,1)S(1)}, u32[]{:S(2)}, u32[]{:S(2)}) collective-permute-start(bf16[8,1,64,128]{3,2,1,0:T(8,128)(2,1)S(1)} %get-tuple-element.68.x_ref), channel_id=1, source_target_pairs={{0,128},{8,136},{16,144},{24,152},{32,160},{40,168},{48,176},{56,1... | collective-permute-start | bytes 393224 | tf_op jit(solution)/shard_map/ppermute | solution.py:179
  9.4 8.9 %collective-permute-start.4 = (bf16[8,1,64,128]{3,2,1,0:T(8,128)(2,1)S(1)}, bf16[8,1,64,128]{3,2,1,0:T(8,128)(2,1)S(1)}, u32[]{:S(2)}, u32[]{:S(2)}) collective-permute-start(bf16[8,1,64,128]{3,2,1,0:T(8,128)(2,1)S(1)} %get-tuple-element.67.x_ref), channel_id=1, source_target_pairs={{0,128},{8,136},{16,144},{24,152},{32,160},{40,168},{48,176},{56,1... | collective-permute-start | bytes 393224 | tf_op jit(solution)/shard_map/ppermute | solution.py:179
  9.8 9.9 %collective-permute-start.3 = (bf16[8,1,64,128]{3,2,1,0:T(8,128)(2,1)S(1)}, bf16[8,1,64,128]{3,2,1,0:T(8,128)(2,1)S(1)}, u32[]{:S(2)}, u32[]{:S(2)}) collective-permute-start(bf16[8,1,64,128]{3,2,1,0:T(8,128)(2,1)S(1)} %get-tuple-element.66.x_ref), channel_id=1, source_target_pairs={{0,64},{8,72},{16,80},{24,88},{32,96},{40,104},{48,112},{56,120},{... | collective-permute-start | bytes 393224 | tf_op jit(solution)/shard_map/ppermute | solution.py:179
  12.9 10.0 %collective-permute-start.2 = (bf16[8,1,64,128]{3,2,1,0:T(8,128)(2,1)S(1)}, bf16[8,1,64,128]{3,2,1,0:T(8,128)(2,1)S(1)}, u32[]{:S(2)}, u32[]{:S(2)}) collective-permute-start(bf16[8,1,64,128]{3,2,1,0:T(8,128)(2,1)S(1)} %get-tuple-element.65.x_ref), channel_id=1, source_target_pairs={{0,64},{8,72},{16,80},{24,88},{32,96},{40,104},{48,112},{56,120},{... | collective-permute-start | bytes 393224 | tf_op jit(solution)/shard_map/ppermute | solution.py:179
  15.8 10.0 %collective-permute-start.9 = (bf16[8,1,64,128]{3,2,1,0:T(8,128)(2,1)S(1)}, bf16[8,1,64,128]{3,2,1,0:T(8,128)(2,1)S(1)}, u32[]{:S(2)}, u32[]{:S(2)}) collective-permute-start(bf16[8,1,64,128]{3,2,1,0:T(8,128)(2,1)S(1)} %get-tuple-element.76.x_ref), channel_id=1, source_target_pairs={{0,64},{8,72},{16,80},{24,88},{32,96},{40,104},{48,112},{56,120},{... | collective-permute-start | bytes 393224 | tf_op jit(solution)/shard_map/ppermute | solution.py:179
  18.6 10.0 %collective-permute-start.8 = (bf16[8,1,64,128]{3,2,1,0:T(8,128)(2,1)S(1)}, bf16[8,1,64,128]{3,2,1,0:T(8,128)(2,1)S(1)}, u32[]{:S(2)}, u32[]{:S(2)}) collective-permute-start(bf16[8,1,64,128]{3,2,1,0:T(8,128)(2,1)S(1)} %get-tuple-element.75.x_ref), channel_id=1, source_target_pairs={{0,64},{8,72},{16,80},{24,88},{32,96},{40,104},{48,112},{56,120},{... | collective-permute-start | bytes 393224 | tf_op jit(solution)/shard_map/ppermute | solution.py:179
  20.0 11.4 %collective-permute-start.7 = (bf16[8,1,64,128]{3,2,1,0:T(8,128)(2,1)S(1)}, bf16[8,1,64,128]{3,2,1,0:T(8,128)(2,1)S(1)}, u32[]{:S(2)}, u32[]{:S(2)}) collective-permute-start(bf16[8,1,64,128]{3,2,1,0:T(8,128)(2,1)S(1)} %get-tuple-element.74.x_ref), channel_id=1, source_target_pairs={{0,32},{8,40},{16,48},{24,56},{32,0},{40,8},{48,16},{56,24},{64,96... | collective-permute-start | bytes 393224 | tf_op jit(solution)/shard_map/ppermute | solution.py:179
  23.3 8.5 %collective-permute-start.6 = (bf16[8,1,64,128]{3,2,1,0:T(8,128)(2,1)S(1)}, bf16[8,1,64,128]{3,2,1,0:T(8,128)(2,1)S(1)}, u32[]{:S(2)}, u32[]{:S(2)}) collective-permute-start(bf16[8,1,64,128]{3,2,1,0:T(8,128)(2,1)S(1)} %get-tuple-element.73.x_ref), channel_id=1, source_target_pairs={{0,32},{8,40},{16,48},{24,56},{32,0},{40,8},{48,16},{56,24},{64,96... | collective-permute-start | bytes 393224 | tf_op jit(solution)/shard_map/ppermute | solution.py:179
  26.1 8.0 %collective-permute-start.11 = (bf16[8,1,64,128]{3,2,1,0:T(8,128)(2,1)S(1)}, bf16[8,1,64,128]{3,2,1,0:T(8,128)(2,1)S(1)}, u32[]{:S(2)}, u32[]{:S(2)}) collective-permute-start(bf16[8,1,64,128]{3,2,1,0:T(8,128)(2,1)S(1)} %get-tuple-element.86.x_ref), channel_id=1, source_target_pairs={{0,32},{8,40},{16,48},{24,56},{32,0},{40,8},{48,16},{56,24},{64,96... | collective-permute-start | bytes 393224 | tf_op jit(solution)/shard_map/ppermute | solution.py:179
  28.9 6.5 %collective-permute-start.10 = (bf16[8,1,64,128]{3,2,1,0:T(8,128)(2,1)S(1)}, bf16[8,1,64,128]{3,2,1,0:T(8,128)(2,1)S(1)}, u32[]{:S(2)}, u32[]{:S(2)}) collective-permute-start(bf16[8,1,64,128]{3,2,1,0:T(8,128)(2,1)S(1)} %get-tuple-element.85.x_ref), channel_id=1, source_target_pairs={{0,32},{8,40},{16,48},{24,56},{32,0},{40,8},{48,16},{56,24},{64,96... | collective-permute-start | bytes 393224 | tf_op jit(solution)/shard_map/ppermute | solution.py:179
  31.4 1.6 %copy-start.4 = (bf16[2,32,64,256]{3,2,1,0:T(8,128)(2,1)S(1)}, bf16[2,32,64,256]{3,2,1,0:T(8,128)(2,1)}, u32[]{:S(2)}) copy-start(bf16[2,32,64,256]{3,2,1,0:T(8,128)(2,1)} %param.10) | copy-start | bytes 6291460
  31.7 2.0 %copy-start.3 = (bf16[2,32,64,256]{3,2,1,0:T(8,128)(2,1)S(1)}, bf16[2,32,64,256]{3,2,1,0:T(8,128)(2,1)}, u32[]{:S(2)}) copy-start(bf16[2,32,64,256]{3,2,1,0:T(8,128)(2,1)} %param.9) | copy-start | bytes 6291460
  31.7 2.0 %copy-start.5 = (bf16[32,64,128]{2,1,0:T(8,128)(2,1)S(1)}, bf16[32,64,128]{2,1,0:T(8,128)(2,1)}, u32[]{:S(2)}) copy-start(bf16[32,64,128]{2,1,0:T(8,128)(2,1)} %param.11) | copy-start | bytes 1572868
  35.7 12.6 %collective-permute-start.12 = (bf16[4,64,128]{2,1,0:T(8,128)(2,1)S(1)}, bf16[4,64,128]{2,1,0:T(8,128)(2,1)S(1)}, u32[]{:S(2)}, u32[]{:S(2)}) collective-permute-start(bf16[4,64,128]{2,1,0:T(8,128)(2,1)S(1)} %get-tuple-element.94), channel_id=1, source_target_pairs={{0,4},{1,5},{2,6},{3,7},{4,0},{5,1},{6,2},{7,3},{8,12},{9,13},{10,... | collective-permute-start | bytes 196616 | tf_op jit(solution)/shard_map/ppermute | solution.py:182
  42.7 6.2 %collective-permute-start.13 = (bf16[4,64,128]{2,1,0:T(8,128)(2,1)S(1)}, bf16[4,64,128]{2,1,0:T(8,128)(2,1)S(1)}, u32[]{:S(2)}, u32[]{:S(2)}) collective-permute-start(bf16[4,64,128]{2,1,0:T(8,128)(2,1)S(1)} %get-tuple-element.95), channel_id=1, source_target_pairs={{0,6},{1,7},{2,4},{3,5},{4,2},{5,3},{6,0},{7,1},{8,14},{9,15},{10,... | collective-permute-start | bytes 196616 | tf_op jit(solution)/shard_map/ppermute | solution.py:182
  42.7 7.6 %collective-permute-start.14 = (bf16[4,64,128]{2,1,0:T(8,128)(2,1)S(1)}, bf16[4,64,128]{2,1,0:T(8,128)(2,1)S(1)}, u32[]{:S(2)}, u32[]{:S(2)}) collective-permute-start(bf16[4,64,128]{2,1,0:T(8,128)(2,1)S(1)} %get-tuple-element.96), channel_id=1, source_target_pairs={{0,2},{1,3},{2,0},{3,1},{4,6},{5,7},{6,4},{7,5},{8,10},{9,11},{10,... | collective-permute-start | bytes 196616 | tf_op jit(solution)/shard_map/ppermute | solution.py:182
  43.9 8.3 %collective-permute-start.15 = (bf16[4,64,128]{2,1,0:T(8,128)(2,1)S(1)}, bf16[4,64,128]{2,1,0:T(8,128)(2,1)S(1)}, u32[]{:S(2)}, u32[]{:S(2)}) collective-permute-start(bf16[4,64,128]{2,1,0:T(8,128)(2,1)S(1)} %get-tuple-element.98), channel_id=1, source_target_pairs={{0,7},{1,6},{2,5},{3,4},{4,3},{5,2},{6,1},{7,0},{8,15},{9,14},{10,... | collective-permute-start | bytes 196616 | tf_op jit(solution)/shard_map/ppermute | solution.py:182
  47.1 6.6 %collective-permute-start.16 = (bf16[4,64,128]{2,1,0:T(8,128)(2,1)S(1)}, bf16[4,64,128]{2,1,0:T(8,128)(2,1)S(1)}, u32[]{:S(2)}, u32[]{:S(2)}) collective-permute-start(bf16[4,64,128]{2,1,0:T(8,128)(2,1)S(1)} %get-tuple-element.99), channel_id=1, source_target_pairs={{0,5},{1,4},{2,7},{3,6},{4,1},{5,0},{6,3},{7,2},{8,13},{9,12},{10,... | collective-permute-start | bytes 196616 | tf_op jit(solution)/shard_map/ppermute | solution.py:182
  48.4 5.3 %collective-permute-start.17 = (bf16[4,64,128]{2,1,0:T(8,128)(2,1)S(1)}, bf16[4,64,128]{2,1,0:T(8,128)(2,1)S(1)}, u32[]{:S(2)}, u32[]{:S(2)}) collective-permute-start(bf16[4,64,128]{2,1,0:T(8,128)(2,1)S(1)} %get-tuple-element.100), channel_id=1, source_target_pairs={{0,1},{1,0},{2,3},{3,2},{4,5},{5,4},{6,7},{7,6},{8,9},{9,8},{10,11... | collective-permute-start | bytes 196616 | tf_op jit(solution)/shard_map/ppermute | solution.py:182
  48.9 5.4 %collective-permute-start.18 = (bf16[4,64,128]{2,1,0:T(8,128)(2,1)S(1)}, bf16[4,64,128]{2,1,0:T(8,128)(2,1)S(1)}, u32[]{:S(2)}, u32[]{:S(2)}) collective-permute-start(bf16[4,64,128]{2,1,0:T(8,128)(2,1)S(1)} %get-tuple-element.101), channel_id=1, source_target_pairs={{0,3},{1,2},{2,1},{3,0},{4,7},{5,6},{6,5},{7,4},{8,11},{9,10},{10,... | collective-permute-start | bytes 196616 | tf_op jit(solution)/shard_map/ppermute | solution.py:182
  51.1 5.6 %collective-permute-start.20 = (bf16[4,4,64,128]{3,2,1,0:T(8,128)(2,1)S(1)}, bf16[4,4,64,128]{3,2,1,0:T(8,128)(2,1)S(1)}, u32[]{:S(2)}, u32[]{:S(2)}) collective-permute-start(bf16[4,4,64,128]{3,2,1,0:T(8,128)(2,1)S(1)} %get-tuple-element.103.x_ref), channel_id=1, source_target_pairs={{0,16},{8,24},{16,0},{24,8},{32,48},{40,56},{48,32},{56,40},{64,80... | collective-permute-start | bytes 786440 | tf_op jit(solution)/shard_map/ppermute | solution.py:179
  55.0 9.3 %collective-permute-start.19 = (bf16[4,4,64,128]{3,2,1,0:T(8,128)(2,1)S(1)}, bf16[4,4,64,128]{3,2,1,0:T(8,128)(2,1)S(1)}, u32[]{:S(2)}, u32[]{:S(2)}) collective-permute-start(bf16[4,4,64,128]{3,2,1,0:T(8,128)(2,1)S(1)} %get-tuple-element.102.x_ref), channel_id=1, source_target_pairs={{0,16},{8,24},{16,0},{24,8},{32,48},{40,56},{48,32},{56,40},{64,80... | collective-permute-start | bytes 786440 | tf_op jit(solution)/shard_map/ppermute | solution.py:179
  57.0 10.1 %collective-permute-start.21 = (bf16[4,4,64,128]{3,2,1,0:T(8,128)(2,1)S(1)}, bf16[4,4,64,128]{3,2,1,0:T(8,128)(2,1)S(1)}, u32[]{:S(2)}, u32[]{:S(2)}) collective-permute-start(bf16[4,4,64,128]{3,2,1,0:T(8,128)(2,1)S(1)} %get-tuple-element.107.x_ref), channel_id=1, source_target_pairs={{0,8},{8,0},{16,24},{24,16},{32,40},{40,32},{48,56},{56,48},{64,72... | collective-permute-start | bytes 786440 | tf_op jit(solution)/shard_map/ppermute | solution.py:179
  64.7 3.6 %collective-permute-start.22 = (bf16[4,4,64,128]{3,2,1,0:T(8,128)(2,1)S(1)}, bf16[4,4,64,128]{3,2,1,0:T(8,128)(2,1)S(1)}, u32[]{:S(2)}, u32[]{:S(2)}) collective-permute-start(bf16[4,4,64,128]{3,2,1,0:T(8,128)(2,1)S(1)} %get-tuple-element.109.x_ref), channel_id=1, source_target_pairs={{0,8},{8,0},{16,24},{24,16},{32,40},{40,32},{48,56},{56,48},{64,72... | collective-permute-start | bytes 786440 | tf_op jit(solution)/shard_map/ppermute | solution.py:179

commit v5 on v4

--- a/solution.py
+++ b/solution.py
@@ -28,8 +28,9 @@
     return jnp.where(lane < half, -rolled, rolled).astype(jnp.bfloat16)
 
 
-def product(weights, parts):
-    stacked = jnp.concatenate(list(parts) + [turn(p) for p in parts], axis=0)
+def product(weights, parts, turned=None):
+    turned = [turn(p) for p in parts] if turned is None else turned
+    stacked = jnp.concatenate(list(parts) + list(turned), axis=0)
     return jnp.dot(weights, stacked, preferred_element_type=jnp.float32).astype(jnp.bfloat16)
 
 
@@ -94,12 +95,24 @@
     u_ref[...] = t_ref[...]
     me = lax.axis_index("mid")
     width = outs[0].shape[1]
-    for i, q in enumerate(gaps):
-        for b in range(s_ref.shape[1]):
-            s_ref[i, b] = product(w_ref[0, me ^ q, b], [got[i][b], got[i ^ (count // 2)][b]])
-    for i, q in enumerate(gaps):
-        for b in range(s_ref.shape[1]):
-            outs[b // width][i, b % width] = product(w_ref[1, me ^ q, b], [s_ref[i, b], s_ref[i ^ (count // 4), b]])
+    for b in range(s_ref.shape[1]):
+        for i in range(count // 2):
+            pair = (i, i ^ (count // 2))
+            parts = {e: got[e][b] for e in pair}
+            turned = {e: turn(parts[e]) for e in pair}
+            for e in pair:
+                order = (e, e ^ (count // 2))
+                s_ref[e, b] = product(w_ref[0, me ^ gaps[e], b], [parts[o] for o in order], [turned[o] for o in order])
+    for b in range(s_ref.shape[1]):
+        for i in range(0, count, 2):
+            pair = (i, i ^ (count // 4))
+            parts = {e: s_ref[e, b] for e in pair}
+            turned = {e: turn(parts[e]) for e in pair}
+            for e in pair:
+                order = (e, e ^ (count // 4))
+                outs[b // width][e, b % width] = product(
+                    w_ref[1, me ^ gaps[e], b], [parts[o] for o in order], [turned[o] for o in order]
+                )
 
 
 def lower_kernel(gaps, first, step, w_ref, x_ref, y_ref, t_ref, o_ref, u_ref):

time: 70 us -> 70 us (level)
  no operation moved by 1% of the time
where the time goes in v5:
time: 70 us; the launch traced here: 69.8 us
  starting transfers between devices  45.5 us (65%)
  waiting for transfers between devices  11.5 us (16%)
  Pallas kernels  9.5 us (14%)
  local copies, waits for them, and re-layouts  2.92 us (4%)
    ppermute x16, starting transfers between devices, swap(): lax.ppermute(block, 'lvl', [(i, i ^ 1 << bit) for i in range(lvl_size)])  31.2 us
    ppermute x7, starting transfers between devices, across(): return lax.ppermute(block, 'mid', [(i, i ^ gap) for i in range(mid_size)])  14.3 us
    ppermute x16, waiting for transfers between devices, swap(): lax.ppermute(block, 'lvl', [(i, i ^ 1 << bit) for i in range(lvl_size)])  9.1 us
    pallas_call x23, Pallas kernels, call(): pl.pallas_call(kernel, out_shape=[jax.ShapeDtypeStruct(shape, jnp.bfloat1...  8.08 us
    unnamed x12, local copies, waits for them, and re-layouts  2.92 us
    ppermute x7, waiting for transfers between devices, across(): return lax.ppermute(block, 'mid', [(i, i ^ gap) for i in range(mid_size)])  2.44 us
    pallas_call x1, Pallas kernels, on_device(): pl.pallas_call(part(store_kernel, places, lower_count - 1), out_shape=jax...  1.41 us
  transfers between devices with their start and end apart: 23, of which 10 were waited for; matrix products, arithmetic and copies ran while one was open for 0% of the time, Pallas kernels for 11%

profile of v5, /device:TPU:1, one launch (start us, length us, event | category | flops | bytes accessed | tf_op | source)
XLA Modules:
  0.0 69.8 jit_solution(1006400834356244519)
XLA Ops:
  0.0 1.0 %copy-done.1 = bf16[32,64,128]{2,1,0:T(8,128)(2,1)S(1)} copy-done((bf16[32,64,128]{2,1,0:T(8,128)(2,1)S(1)}, bf16[32,64,128]{2,1,0:T(8,128)(2,1)}, u32[]{:S(2)}) %copy-start.1) | copy-done | bytes 524312
  1.0 0.2 copy-done.2
  1.2 0.3 shard_map.65
  1.5 3.7 %collective-permute-start.1 = (bf16[8,1,64,128]{3,2,1,0:T(8,128)(2,1)S(1)}, bf16[8,1,64,128]{3,2,1,0:T(8,128)(2,1)S(1)}, u32[]{:S(2)}, u32[]{:S(2)}) collective-permute-start(bf16[8,1,64,128]{3,2,1,0:T(8,128)(2,1)S(1)} %get-tuple-element.60.x_ref), channel_id=1, source_target_pairs={{0,128},{8,136},{16,144},{24,152},{32,160},{40,168},{48,176},{56,1... | collective-permute-start | bytes 393224 | tf_op jit(solution)/shard_map/ppermute | solution.py:192
  5.2 0.3 shard_map.66
  5.5 0.1 collective-permute-start
  5.6 0.3 shard_map.67
  6.0 3.0 %collective-permute-start.5 = (bf16[8,1,64,128]{3,2,1,0:T(8,128)(2,1)S(1)}, bf16[8,1,64,128]{3,2,1,0:T(8,128)(2,1)S(1)}, u32[]{:S(2)}, u32[]{:S(2)}) collective-permute-start(bf16[8,1,64,128]{3,2,1,0:T(8,128)(2,1)S(1)} %get-tuple-element.68.x_ref), channel_id=1, source_target_pairs={{0,128},{8,136},{16,144},{24,152},{32,160},{40,168},{48,176},{56,1... | collective-permute-start | bytes 393224 | tf_op jit(solution)/shard_map/ppermute | solution.py:192
  9.0 0.3 shard_map.68
  9.4 0.1 collective-permute-start.4
  9.5 0.3 shard_map.69
  9.8 1.5 %collective-permute-start.3 = (bf16[8,1,64,128]{3,2,1,0:T(8,128)(2,1)S(1)}, bf16[8,1,64,128]{3,2,1,0:T(8,128)(2,1)S(1)}, u32[]{:S(2)}, u32[]{:S(2)}) collective-permute-start(bf16[8,1,64,128]{3,2,1,0:T(8,128)(2,1)S(1)} %get-tuple-element.66.x_ref), channel_id=1, source_target_pairs={{0,64},{8,72},{16,80},{24,88},{32,96},{40,104},{48,112},{56,120},{... | collective-permute-start | bytes 393224 | tf_op jit(solution)/shard_map/ppermute | solution.py:192
  11.3 1.4 %collective-permute-done.y_ref = bf16[8,1,64,128]{3,2,1,0:T(8,128)(2,1)S(1)} collective-permute-done((bf16[8,1,64,128]{3,2,1,0:T(8,128)(2,1)S(1)}, bf16[8,1,64,128]{3,2,1,0:T(8,128)(2,1)S(1)}, u32[]{:S(2)}, u32[]{:S(2)}) %collective-permute-start) | collective-permute-done | bytes 131104 | tf_op jit(solution)/shard_map/ppermute | solution.py:192
  12.6 0.3 shard_map.70
  12.9 0.1 collective-permute-start.2
  13.0 2.4 %collective-permute-done.5.y_ref = bf16[8,1,64,128]{3,2,1,0:T(8,128)(2,1)S(1)} collective-permute-done((bf16[8,1,64,128]{3,2,1,0:T(8,128)(2,1)S(1)}, bf16[8,1,64,128]{3,2,1,0:T(8,128)(2,1)S(1)}, u32[]{:S(2)}, u32[]{:S(2)}) %collective-permute-start.5) | collective-permute-done | bytes 131104 | tf_op jit(solution)/shard_map/ppermute | solution.py:192
  15.5 0.3 shard_map.71
  15.8 0.1 collective-permute-start.9
  15.9 2.4 %collective-permute-done.4.y_ref = bf16[8,1,64,128]{3,2,1,0:T(8,128)(2,1)S(1)} collective-permute-done((bf16[8,1,64,128]{3,2,1,0:T(8,128)(2,1)S(1)}, bf16[8,1,64,128]{3,2,1,0:T(8,128)(2,1)S(1)}, u32[]{:S(2)}, u32[]{:S(2)}) %collective-permute-start.4) | collective-permute-done | bytes 131104 | tf_op jit(solution)/shard_map/ppermute | solution.py:192
  18.3 0.3 shard_map.72
  18.6 0.1 collective-permute-start.8
  18.7 1.0 %collective-permute-done.3.y_ref = bf16[8,1,64,128]{3,2,1,0:T(8,128)(2,1)S(1)} collective-permute-done((bf16[8,1,64,128]{3,2,1,0:T(8,128)(2,1)S(1)}, bf16[8,1,64,128]{3,2,1,0:T(8,128)(2,1)S(1)}, u32[]{:S(2)}, u32[]{:S(2)}) %collective-permute-start.3) | collective-permute-done | bytes 131104 | tf_op jit(solution)/shard_map/ppermute | solution.py:192
  19.6 0.3 shard_map.73
  20.0 3.0 %collective-permute-start.7 = (bf16[8,1,64,128]{3,2,1,0:T(8,128)(2,1)S(1)}, bf16[8,1,64,128]{3,2,1,0:T(8,128)(2,1)S(1)}, u32[]{:S(2)}, u32[]{:S(2)}) collective-permute-start(bf16[8,1,64,128]{3,2,1,0:T(8,128)(2,1)S(1)} %get-tuple-element.74.x_ref), channel_id=1, source_target_pairs={{0,32},{8,40},{16,48},{24,56},{32,0},{40,8},{48,16},{56,24},{64,96... | collective-permute-start | bytes 393224 | tf_op jit(solution)/shard_map/ppermute | solution.py:192
  23.0 0.0 collective-permute-done.2.y_ref
  23.0 0.3 shard_map.74
  23.3 2.5 %collective-permute-start.6 = (bf16[8,1,64,128]{3,2,1,0:T(8,128)(2,1)S(1)}, bf16[8,1,64,128]{3,2,1,0:T(8,128)(2,1)S(1)}, u32[]{:S(2)}, u32[]{:S(2)}) collective-permute-start(bf16[8,1,64,128]{3,2,1,0:T(8,128)(2,1)S(1)} %get-tuple-element.73.x_ref), channel_id=1, source_target_pairs={{0,32},{8,40},{16,48},{24,56},{32,0},{40,8},{48,16},{56,24},{64,96... | collective-permute-start | bytes 393224 | tf_op jit(solution)/shard_map/ppermute | solution.py:192
  25.8 0.0 collective-permute-done.9.y_ref
  25.8 0.3 shard_map.75
  26.1 2.5 %collective-permute-start.11 = (bf16[8,1,64,128]{3,2,1,0:T(8,128)(2,1)S(1)}, bf16[8,1,64,128]{3,2,1,0:T(8,128)(2,1)S(1)}, u32[]{:S(2)}, u32[]{:S(2)}) collective-permute-start(bf16[8,1,64,128]{3,2,1,0:T(8,128)(2,1)S(1)} %get-tuple-element.86.x_ref), channel_id=1, source_target_pairs={{0,32},{8,40},{16,48},{24,56},{32,0},{40,8},{48,16},{56,24},{64,96... | collective-permute-start | bytes 393224 | tf_op jit(solution)/shard_map/ppermute | solution.py:192
  28.6 0.3 shard_map.76
  28.9 2.5 %collective-permute-start.10 = (bf16[8,1,64,128]{3,2,1,0:T(8,128)(2,1)S(1)}, bf16[8,1,64,128]{3,2,1,0:T(8,128)(2,1)S(1)}, u32[]{:S(2)}, u32[]{:S(2)}) collective-permute-start(bf16[8,1,64,128]{3,2,1,0:T(8,128)(2,1)S(1)} %get-tuple-element.85.x_ref), channel_id=1, source_target_pairs={{0,32},{8,40},{16,48},{24,56},{32,0},{40,8},{48,16},{56,24},{64,96... | collective-permute-start | bytes 393224 | tf_op jit(solution)/shard_map/ppermute | solution.py:192
  31.4 0.3 shard_map.77
  31.7 0.0 copy-start.3
  31.7 0.0 copy-start.5
  31.7 0.3 shard_map.78
  32.0 1.0 %copy-done.4 = bf16[2,32,64,256]{3,2,1,0:T(8,128)(2,1)S(1)} copy-done((bf16[2,32,64,256]{3,2,1,0:T(8,128)(2,1)S(1)}, bf16[2,32,64,256]{3,2,1,0:T(8,128)(2,1)}, u32[]{:S(2)}) %copy-start.4) | copy-done | bytes 2097176
  33.0 0.7 %copy-done.3 = bf16[2,32,64,256]{3,2,1,0:T(8,128)(2,1)S(1)} copy-done((bf16[2,32,64,256]{3,2,1,0:T(8,128)(2,1)S(1)}, bf16[2,32,64,256]{3,2,1,0:T(8,128)(2,1)}, u32[]{:S(2)}) %copy-start.3) | copy-done | bytes 2097176
  33.7 0.1 copy-done.5
  33.8 0.3 shard_map.79
  34.1 0.3 shard_map.80
  34.4 1.0 %collective-permute-done.10.y_ref = bf16[8,1,64,128]{3,2,1,0:T(8,128)(2,1)S(1)} collective-permute-done((bf16[8,1,64,128]{3,2,1,0:T(8,128)(2,1)S(1)}, bf16[8,1,64,128]{3,2,1,0:T(8,128)(2,1)S(1)}, u32[]{:S(2)}, u32[]{:S(2)}) %collective-permute-start.10) | collective-permute-done | bytes 131104 | tf_op jit(solution)/shard_map/ppermute | solution.py:192
  35.4 0.3 shard_map.81
  35.7 7.0 %collective-permute-start.12 = (bf16[4,64,128]{2,1,0:T(8,128)(2,1)S(1)}, bf16[4,64,128]{2,1,0:T(8,128)(2,1)S(1)}, u32[]{:S(2)}, u32[]{:S(2)}) collective-permute-start(bf16[4,64,128]{2,1,0:T(8,128)(2,1)S(1)} %get-tuple-element.94), channel_id=1, source_target_pairs={{0,4},{1,5},{2,6},{3,7},{4,0},{5,1},{6,2},{7,3},{8,12},{9,13},{10,... | collective-permute-start | bytes 196616 | tf_op jit(solution)/shard_map/ppermute | solution.py:195
  42.7 1.2 %collective-permute-start.14 = (bf16[4,64,128]{2,1,0:T(8,128)(2,1)S(1)}, bf16[4,64,128]{2,1,0:T(8,128)(2,1)S(1)}, u32[]{:S(2)}, u32[]{:S(2)}) collective-permute-start(bf16[4,64,128]{2,1,0:T(8,128)(2,1)S(1)} %get-tuple-element.96), channel_id=1, source_target_pairs={{0,2},{1,3},{2,0},{3,1},{4,6},{5,7},{6,4},{7,5},{8,10},{9,11},{10,... | collective-permute-start | bytes 196616 | tf_op jit(solution)/shard_map/ppermute | solution.py:195
  43.9 3.1 %collective-permute-start.15 = (bf16[4,64,128]{2,1,0:T(8,128)(2,1)S(1)}, bf16[4,64,128]{2,1,0:T(8,128)(2,1)S(1)}, u32[]{:S(2)}, u32[]{:S(2)}) collective-permute-start(bf16[4,64,128]{2,1,0:T(8,128)(2,1)S(1)} %get-tuple-element.98), channel_id=1, source_target_pairs={{0,7},{1,6},{2,5},{3,4},{4,3},{5,2},{6,1},{7,0},{8,15},{9,14},{10,... | collective-permute-start | bytes 196616 | tf_op jit(solution)/shard_map/ppermute | solution.py:195
  47.1 1.3 %collective-permute-start.16 = (bf16[4,64,128]{2,1,0:T(8,128)(2,1)S(1)}, bf16[4,64,128]{2,1,0:T(8,128)(2,1)S(1)}, u32[]{:S(2)}, u32[]{:S(2)}) collective-permute-start(bf16[4,64,128]{2,1,0:T(8,128)(2,1)S(1)} %get-tuple-element.99), channel_id=1, source_target_pairs={{0,5},{1,4},{2,7},{3,6},{4,1},{5,0},{6,3},{7,2},{8,13},{9,12},{10,... | collective-permute-start | bytes 196616 | tf_op jit(solution)/shard_map/ppermute | solution.py:195
  48.4 0.3 collective-permute-start.17
  48.7 0.2 collective-permute-done.13.refs_2_
  48.9 1.4 %collective-permute-start.18 = (bf16[4,64,128]{2,1,0:T(8,128)(2,1)S(1)}, bf16[4,64,128]{2,1,0:T(8,128)(2,1)S(1)}, u32[]{:S(2)}, u32[]{:S(2)}) collective-permute-start(bf16[4,64,128]{2,1,0:T(8,128)(2,1)S(1)} %get-tuple-element.101), channel_id=1, source_target_pairs={{0,3},{1,2},{2,1},{3,0},{4,7},{5,6},{6,5},{7,4},{8,11},{9,10},{10,... | collective-permute-start | bytes 196616 | tf_op jit(solution)/shard_map/ppermute | solution.py:195
  50.3 0.7 shard_map.82
  51.0 1.1 %collective-permute-start.20 = (bf16[4,4,64,128]{3,2,1,0:T(8,128)(2,1)S(1)}, bf16[4,4,64,128]{3,2,1,0:T(8,128)(2,1)S(1)}, u32[]{:S(2)}, u32[]{:S(2)}) collective-permute-start(bf16[4,4,64,128]{3,2,1,0:T(8,128)(2,1)S(1)} %get-tuple-element.103.x_ref), channel_id=1, source_target_pairs={{0,16},{8,24},{16,0},{24,8},{32,48},{40,56},{48,32},{56,40},{64,80... | collective-permute-start | bytes 786440 | tf_op jit(solution)/shard_map/ppermute | solution.py:192
  52.1 1.5 %collective-permute-done.16.refs_1_ = bf16[4,64,128]{2,1,0:T(8,128)(2,1)S(1)} collective-permute-done((bf16[4,64,128]{2,1,0:T(8,128)(2,1)S(1)}, bf16[4,64,128]{2,1,0:T(8,128)(2,1)S(1)}, u32[]{:S(2)}, u32[]{:S(2)}) %collective-permute-start.16) | collective-permute-done | bytes 65568 | tf_op jit(solution)/shard_map/ppermute | solution.py:195
  53.7 0.7 collective-permute-done.18.refs_3_
  54.3 0.7 shard_map.83
  55.0 1.2 %collective-permute-start.19 = (bf16[4,4,64,128]{3,2,1,0:T(8,128)(2,1)S(1)}, bf16[4,4,64,128]{3,2,1,0:T(8,128)(2,1)S(1)}, u32[]{:S(2)}, u32[]{:S(2)}) collective-permute-start(bf16[4,4,64,128]{3,2,1,0:T(8,128)(2,1)S(1)} %get-tuple-element.102.x_ref), channel_id=1, source_target_pairs={{0,16},{8,24},{16,0},{24,8},{32,48},{40,56},{48,32},{56,40},{64,80... | collective-permute-start | bytes 786440 | tf_op jit(solution)/shard_map/ppermute | solution.py:192
  56.2 0.5 collective-permute-done.20.y_ref
  56.6 0.4 shard_map.84
  57.0 7.3 %collective-permute-start.21 = (bf16[4,4,64,128]{3,2,1,0:T(8,128)(2,1)S(1)}, bf16[4,4,64,128]{3,2,1,0:T(8,128)(2,1)S(1)}, u32[]{:S(2)}, u32[]{:S(2)}) collective-permute-start(bf16[4,4,64,128]{3,2,1,0:T(8,128)(2,1)S(1)} %get-tuple-element.107.x_ref), channel_id=1, source_target_pairs={{0,8},{8,0},{16,24},{24,16},{32,40},{40,32},{48,56},{56,48},{64,72... | collective-permute-start | bytes 786440 | tf_op jit(solution)/shard_map/ppermute | solution.py:192
  64.3 0.4 shard_map.85
  64.7 2.4 %collective-permute-start.22 = (bf16[4,4,64,128]{3,2,1,0:T(8,128)(2,1)S(1)}, bf16[4,4,64,128]{3,2,1,0:T(8,128)(2,1)S(1)}, u32[]{:S(2)}, u32[]{:S(2)}) collective-permute-start(bf16[4,4,64,128]{3,2,1,0:T(8,128)(2,1)S(1)} %get-tuple-element.109.x_ref), channel_id=1, source_target_pairs={{0,8},{8,0},{16,24},{24,16},{32,40},{40,32},{48,56},{56,48},{64,72... | collective-permute-start | bytes 786440 | tf_op jit(solution)/shard_map/ppermute | solution.py:192
  67.1 0.7 %shard_map.86 = (bf16[4,4,64,128]{3,2,1,0:T(8,128)(2,1)S(1)}, f32[8,128]{1,0:T(8,128)S(1)}) custom-call(bf16[2,8,4,64,256]{4,3,2,1,0:T(8,128)(2,1)S(1)} %get-tuple-element.82.w_ref, bf16[8,4,64,128]{3,2,1,0:T(8,128)(2,1)S(1)} %get-tuple-element.83.v_ref, f32[8,128]{1,0:T(8,128)S(1)} %get-tuple-element.106.t_ref, ...), custom_call_target="tpu_custom_call" | custom-call | flops 1 | bytes 1 | tf_op jit(solution)/shard_map/pallas_call | solution.py:166
  67.8 0.5 collective-permute-done.22.y_ref
  68.3 1.4 %shard_map.87 = bf16[8,4,64,128]{3,2,1,0:T(8,128)(2,1)} custom-call(bf16[2,8,4,64,256]{4,3,2,1,0:T(8,128)(2,1)S(1)} %get-tuple-element.82.w_ref, bf16[8,4,64,128]{3,2,1,0:T(8,128)(2,1)S(1)} %get-tuple-element.83.v_ref, f32[8,128]{1,0:T(8,128)S(1)} %get-tuple-element.108.t_ref, bf16[4,4,64,128]{3,2,1,0:T(8,128)(2,1)S(1)} %get-tuple-element.109.x_ref, ...), custom_call_target="tpu_custom_call" | custom-call | flops 1 | bytes 1 | tf_op jit(solution)/shard_map/pallas_call | solution.py:252
  (19 shorter events, 0.0 us)
Async XLA Ops:
  0.0 1.0 %copy-start.1 = (bf16[32,64,128]{2,1,0:T(8,128)(2,1)S(1)}, bf16[32,64,128]{2,1,0:T(8,128)(2,1)}, u32[]{:S(2)}) copy-start(bf16[32,64,128]{2,1,0:T(8,128)(2,1)} %param.7) | copy-start | bytes 1572868
  0.0 1.2 %copy-start.2 = (bf16[32,64,128]{2,1,0:T(8,128)(2,1)S(1)}, bf16[32,64,128]{2,1,0:T(8,128)(2,1)}, u32[]{:S(2)}) copy-start(bf16[32,64,128]{2,1,0:T(8,128)(2,1)} %param.6) | copy-start | bytes 1572868
  1.2 8.3 %copy-start = (bf16[3,32,64,256]{3,2,1,0:T(8,128)(2,1)S(1)}, bf16[3,32,64,256]{3,2,1,0:T(8,128)(2,1)}, u32[]{:S(2)}) copy-start(bf16[3,32,64,256]{3,2,1,0:T(8,128)(2,1)} %param.8) | copy-start | bytes 9437188
  1.5 7.9 %collective-permute-start.1 = (bf16[8,1,64,128]{3,2,1,0:T(8,128)(2,1)S(1)}, bf16[8,1,64,128]{3,2,1,0:T(8,128)(2,1)S(1)}, u32[]{:S(2)}, u32[]{:S(2)}) collective-permute-start(bf16[8,1,64,128]{3,2,1,0:T(8,128)(2,1)S(1)} %get-tuple-element.60.x_ref), channel_id=1, source_target_pairs={{0,128},{8,136},{16,144},{24,152},{32,160},{40,168},{48,176},{56,1... | collective-permute-start | bytes 393224 | tf_op jit(solution)/shard_map/ppermute | solution.py:192
  5.5 7.1 %collective-permute-start = (bf16[8,1,64,128]{3,2,1,0:T(8,128)(2,1)S(1)}, bf16[8,1,64,128]{3,2,1,0:T(8,128)(2,1)S(1)}, u32[]{:S(2)}, u32[]{:S(2)}) collective-permute-start(bf16[8,1,64,128]{3,2,1,0:T(8,128)(2,1)S(1)} %get-tuple-element.59.x_ref), channel_id=1, source_target_pairs={{0,128},{8,136},{16,144},{24,152},{32,160},{40,168},{48,176},{56,1... | collective-permute-start | bytes 393224 | tf_op jit(solution)/shard_map/ppermute | solution.py:192
  6.0 9.5 %collective-permute-start.5 = (bf16[8,1,64,128]{3,2,1,0:T(8,128)(2,1)S(1)}, bf16[8,1,64,128]{3,2,1,0:T(8,128)(2,1)S(1)}, u32[]{:S(2)}, u32[]{:S(2)}) collective-permute-start(bf16[8,1,64,128]{3,2,1,0:T(8,128)(2,1)S(1)} %get-tuple-element.68.x_ref), channel_id=1, source_target_pairs={{0,128},{8,136},{16,144},{24,152},{32,160},{40,168},{48,176},{56,1... | collective-permute-start | bytes 393224 | tf_op jit(solution)/shard_map/ppermute | solution.py:192
  9.4 8.9 %collective-permute-start.4 = (bf16[8,1,64,128]{3,2,1,0:T(8,128)(2,1)S(1)}, bf16[8,1,64,128]{3,2,1,0:T(8,128)(2,1)S(1)}, u32[]{:S(2)}, u32[]{:S(2)}) collective-permute-start(bf16[8,1,64,128]{3,2,1,0:T(8,128)(2,1)S(1)} %get-tuple-element.67.x_ref), channel_id=1, source_target_pairs={{0,128},{8,136},{16,144},{24,152},{32,160},{40,168},{48,176},{56,1... | collective-permute-start | bytes 393224 | tf_op jit(solution)/shard_map/ppermute | solution.py:192
  9.8 9.9 %collective-permute-start.3 = (bf16[8,1,64,128]{3,2,1,0:T(8,128)(2,1)S(1)}, bf16[8,1,64,128]{3,2,1,0:T(8,128)(2,1)S(1)}, u32[]{:S(2)}, u32[]{:S(2)}) collective-permute-start(bf16[8,1,64,128]{3,2,1,0:T(8,128)(2,1)S(1)} %get-tuple-element.66.x_ref), channel_id=1, source_target_pairs={{0,64},{8,72},{16,80},{24,88},{32,96},{40,104},{48,112},{56,120},{... | collective-permute-start | bytes 393224 | tf_op jit(solution)/shard_map/ppermute | solution.py:192
  12.9 10.0 %collective-permute-start.2 = (bf16[8,1,64,128]{3,2,1,0:T(8,128)(2,1)S(1)}, bf16[8,1,64,128]{3,2,1,0:T(8,128)(2,1)S(1)}, u32[]{:S(2)}, u32[]{:S(2)}) collective-permute-start(bf16[8,1,64,128]{3,2,1,0:T(8,128)(2,1)S(1)} %get-tuple-element.65.x_ref), channel_id=1, source_target_pairs={{0,64},{8,72},{16,80},{24,88},{32,96},{40,104},{48,112},{56,120},{... | collective-permute-start | bytes 393224 | tf_op jit(solution)/shard_map/ppermute | solution.py:192
  15.8 10.0 %collective-permute-start.9 = (bf16[8,1,64,128]{3,2,1,0:T(8,128)(2,1)S(1)}, bf16[8,1,64,128]{3,2,1,0:T(8,128)(2,1)S(1)}, u32[]{:S(2)}, u32[]{:S(2)}) collective-permute-start(bf16[8,1,64,128]{3,2,1,0:T(8,128)(2,1)S(1)} %get-tuple-element.76.x_ref), channel_id=1, source_target_pairs={{0,64},{8,72},{16,80},{24,88},{32,96},{40,104},{48,112},{56,120},{... | collective-permute-start | bytes 393224 | tf_op jit(solution)/shard_map/ppermute | solution.py:192
  18.6 10.0 %collective-permute-start.8 = (bf16[8,1,64,128]{3,2,1,0:T(8,128)(2,1)S(1)}, bf16[8,1,64,128]{3,2,1,0:T(8,128)(2,1)S(1)}, u32[]{:S(2)}, u32[]{:S(2)}) collective-permute-start(bf16[8,1,64,128]{3,2,1,0:T(8,128)(2,1)S(1)} %get-tuple-element.75.x_ref), channel_id=1, source_target_pairs={{0,64},{8,72},{16,80},{24,88},{32,96},{40,104},{48,112},{56,120},{... | collective-permute-start | bytes 393224 | tf_op jit(solution)/shard_map/ppermute | solution.py:192
  20.0 11.4 %collective-permute-start.7 = (bf16[8,1,64,128]{3,2,1,0:T(8,128)(2,1)S(1)}, bf16[8,1,64,128]{3,2,1,0:T(8,128)(2,1)S(1)}, u32[]{:S(2)}, u32[]{:S(2)}) collective-permute-start(bf16[8,1,64,128]{3,2,1,0:T(8,128)(2,1)S(1)} %get-tuple-element.74.x_ref), channel_id=1, source_target_pairs={{0,32},{8,40},{16,48},{24,56},{32,0},{40,8},{48,16},{56,24},{64,96... | collective-permute-start | bytes 393224 | tf_op jit(solution)/shard_map/ppermute | solution.py:192
  23.3 8.5 %collective-permute-start.6 = (bf16[8,1,64,128]{3,2,1,0:T(8,128)(2,1)S(1)}, bf16[8,1,64,128]{3,2,1,0:T(8,128)(2,1)S(1)}, u32[]{:S(2)}, u32[]{:S(2)}) collective-permute-start(bf16[8,1,64,128]{3,2,1,0:T(8,128)(2,1)S(1)} %get-tuple-element.73.x_ref), channel_id=1, source_target_pairs={{0,32},{8,40},{16,48},{24,56},{32,0},{40,8},{48,16},{56,24},{64,96... | collective-permute-start | bytes 393224 | tf_op jit(solution)/shard_map/ppermute | solution.py:192
  26.1 8.0 %collective-permute-start.11 = (bf16[8,1,64,128]{3,2,1,0:T(8,128)(2,1)S(1)}, bf16[8,1,64,128]{3,2,1,0:T(8,128)(2,1)S(1)}, u32[]{:S(2)}, u32[]{:S(2)}) collective-permute-start(bf16[8,1,64,128]{3,2,1,0:T(8,128)(2,1)S(1)} %get-tuple-element.86.x_ref), channel_id=1, source_target_pairs={{0,32},{8,40},{16,48},{24,56},{32,0},{40,8},{48,16},{56,24},{64,96... | collective-permute-start | bytes 393224 | tf_op jit(solution)/shard_map/ppermute | solution.py:192
  28.9 6.5 %collective-permute-start.10 = (bf16[8,1,64,128]{3,2,1,0:T(8,128)(2,1)S(1)}, bf16[8,1,64,128]{3,2,1,0:T(8,128)(2,1)S(1)}, u32[]{:S(2)}, u32[]{:S(2)}) collective-permute-start(bf16[8,1,64,128]{3,2,1,0:T(8,128)(2,1)S(1)} %get-tuple-element.85.x_ref), channel_id=1, source_target_pairs={{0,32},{8,40},{16,48},{24,56},{32,0},{40,8},{48,16},{56,24},{64,96... | collective-permute-start | bytes 393224 | tf_op jit(solution)/shard_map/ppermute | solution.py:192
  31.4 1.6 %copy-start.4 = (bf16[2,32,64,256]{3,2,1,0:T(8,128)(2,1)S(1)}, bf16[2,32,64,256]{3,2,1,0:T(8,128)(2,1)}, u32[]{:S(2)}) copy-start(bf16[2,32,64,256]{3,2,1,0:T(8,128)(2,1)} %param.10) | copy-start | bytes 6291460
  31.7 2.0 %copy-start.3 = (bf16[2,32,64,256]{3,2,1,0:T(8,128)(2,1)S(1)}, bf16[2,32,64,256]{3,2,1,0:T(8,128)(2,1)}, u32[]{:S(2)}) copy-start(bf16[2,32,64,256]{3,2,1,0:T(8,128)(2,1)} %param.9) | copy-start | bytes 6291460
  31.7 2.0 %copy-start.5 = (bf16[32,64,128]{2,1,0:T(8,128)(2,1)S(1)}, bf16[32,64,128]{2,1,0:T(8,128)(2,1)}, u32[]{:S(2)}) copy-start(bf16[32,64,128]{2,1,0:T(8,128)(2,1)} %param.11) | copy-start | bytes 1572868
  35.7 12.6 %collective-permute-start.12 = (bf16[4,64,128]{2,1,0:T(8,128)(2,1)S(1)}, bf16[4,64,128]{2,1,0:T(8,128)(2,1)S(1)}, u32[]{:S(2)}, u32[]{:S(2)}) collective-permute-start(bf16[4,64,128]{2,1,0:T(8,128)(2,1)S(1)} %get-tuple-element.94), channel_id=1, source_target_pairs={{0,4},{1,5},{2,6},{3,7},{4,0},{5,1},{6,2},{7,3},{8,12},{9,13},{10,... | collective-permute-start | bytes 196616 | tf_op jit(solution)/shard_map/ppermute | solution.py:195
  42.7 6.2 %collective-permute-start.13 = (bf16[4,64,128]{2,1,0:T(8,128)(2,1)S(1)}, bf16[4,64,128]{2,1,0:T(8,128)(2,1)S(1)}, u32[]{:S(2)}, u32[]{:S(2)}) collective-permute-start(bf16[4,64,128]{2,1,0:T(8,128)(2,1)S(1)} %get-tuple-element.95), channel_id=1, source_target_pairs={{0,6},{1,7},{2,4},{3,5},{4,2},{5,3},{6,0},{7,1},{8,14},{9,15},{10,... | collective-permute-start | bytes 196616 | tf_op jit(solution)/shard_map/ppermute | solution.py:195
  42.7 7.6 %collective-permute-start.14 = (bf16[4,64,128]{2,1,0:T(8,128)(2,1)S(1)}, bf16[4,64,128]{2,1,0:T(8,128)(2,1)S(1)}, u32[]{:S(2)}, u32[]{:S(2)}) collective-permute-start(bf16[4,64,128]{2,1,0:T(8,128)(2,1)S(1)} %get-tuple-element.96), channel_id=1, source_target_pairs={{0,2},{1,3},{2,0},{3,1},{4,6},{5,7},{6,4},{7,5},{8,10},{9,11},{10,... | collective-permute-start | bytes 196616 | tf_op jit(solution)/shard_map/ppermute | solution.py:195
  43.9 8.2 %collective-permute-start.15 = (bf16[4,64,128]{2,1,0:T(8,128)(2,1)S(1)}, bf16[4,64,128]{2,1,0:T(8,128)(2,1)S(1)}, u32[]{:S(2)}, u32[]{:S(2)}) collective-permute-start(bf16[4,64,128]{2,1,0:T(8,128)(2,1)S(1)} %get-tuple-element.98), channel_id=1, source_target_pairs={{0,7},{1,6},{2,5},{3,4},{4,3},{5,2},{6,1},{7,0},{8,15},{9,14},{10,... | collective-permute-start | bytes 196616 | tf_op jit(solution)/shard_map/ppermute | solution.py:195
  47.1 6.6 %collective-permute-start.16 = (bf16[4,64,128]{2,1,0:T(8,128)(2,1)S(1)}, bf16[4,64,128]{2,1,0:T(8,128)(2,1)S(1)}, u32[]{:S(2)}, u32[]{:S(2)}) collective-permute-start(bf16[4,64,128]{2,1,0:T(8,128)(2,1)S(1)} %get-tuple-element.99), channel_id=1, source_target_pairs={{0,5},{1,4},{2,7},{3,6},{4,1},{5,0},{6,3},{7,2},{8,13},{9,12},{10,... | collective-permute-start | bytes 196616 | tf_op jit(solution)/shard_map/ppermute | solution.py:195
  48.4 5.3 %collective-permute-start.17 = (bf16[4,64,128]{2,1,0:T(8,128)(2,1)S(1)}, bf16[4,64,128]{2,1,0:T(8,128)(2,1)S(1)}, u32[]{:S(2)}, u32[]{:S(2)}) collective-permute-start(bf16[4,64,128]{2,1,0:T(8,128)(2,1)S(1)} %get-tuple-element.100), channel_id=1, source_target_pairs={{0,1},{1,0},{2,3},{3,2},{4,5},{5,4},{6,7},{7,6},{8,9},{9,8},{10,11... | collective-permute-start | bytes 196616 | tf_op jit(solution)/shard_map/ppermute | solution.py:195
  48.9 5.4 %collective-permute-start.18 = (bf16[4,64,128]{2,1,0:T(8,128)(2,1)S(1)}, bf16[4,64,128]{2,1,0:T(8,128)(2,1)S(1)}, u32[]{:S(2)}, u32[]{:S(2)}) collective-permute-start(bf16[4,64,128]{2,1,0:T(8,128)(2,1)S(1)} %get-tuple-element.101), channel_id=1, source_target_pairs={{0,3},{1,2},{2,1},{3,0},{4,7},{5,6},{6,5},{7,4},{8,11},{9,10},{10,... | collective-permute-start | bytes 196616 | tf_op jit(solution)/shard_map/ppermute | solution.py:195
  51.0 5.6 %collective-permute-start.20 = (bf16[4,4,64,128]{3,2,1,0:T(8,128)(2,1)S(1)}, bf16[4,4,64,128]{3,2,1,0:T(8,128)(2,1)S(1)}, u32[]{:S(2)}, u32[]{:S(2)}) collective-permute-start(bf16[4,4,64,128]{3,2,1,0:T(8,128)(2,1)S(1)} %get-tuple-element.103.x_ref), channel_id=1, source_target_pairs={{0,16},{8,24},{16,0},{24,8},{32,48},{40,56},{48,32},{56,40},{64,80... | collective-permute-start | bytes 786440 | tf_op jit(solution)/shard_map/ppermute | solution.py:192
  55.0 9.3 %collective-permute-start.19 = (bf16[4,4,64,128]{3,2,1,0:T(8,128)(2,1)S(1)}, bf16[4,4,64,128]{3,2,1,0:T(8,128)(2,1)S(1)}, u32[]{:S(2)}, u32[]{:S(2)}) collective-permute-start(bf16[4,4,64,128]{3,2,1,0:T(8,128)(2,1)S(1)} %get-tuple-element.102.x_ref), channel_id=1, source_target_pairs={{0,16},{8,24},{16,0},{24,8},{32,48},{40,56},{48,32},{56,40},{64,80... | collective-permute-start | bytes 786440 | tf_op jit(solution)/shard_map/ppermute | solution.py:192
  57.0 10.1 %collective-permute-start.21 = (bf16[4,4,64,128]{3,2,1,0:T(8,128)(2,1)S(1)}, bf16[4,4,64,128]{3,2,1,0:T(8,128)(2,1)S(1)}, u32[]{:S(2)}, u32[]{:S(2)}) collective-permute-start(bf16[4,4,64,128]{3,2,1,0:T(8,128)(2,1)S(1)} %get-tuple-element.107.x_ref), channel_id=1, source_target_pairs={{0,8},{8,0},{16,24},{24,16},{32,40},{40,32},{48,56},{56,48},{64,72... | collective-permute-start | bytes 786440 | tf_op jit(solution)/shard_map/ppermute | solution.py:192
  64.7 3.6 %collective-permute-start.22 = (bf16[4,4,64,128]{3,2,1,0:T(8,128)(2,1)S(1)}, bf16[4,4,64,128]{3,2,1,0:T(8,128)(2,1)S(1)}, u32[]{:S(2)}, u32[]{:S(2)}) collective-permute-start(bf16[4,4,64,128]{3,2,1,0:T(8,128)(2,1)S(1)} %get-tuple-element.109.x_ref), channel_id=1, source_target_pairs={{0,8},{8,0},{16,24},{24,16},{32,40},{40,32},{48,56},{56,48},{64,72... | collective-permute-start | bytes 786440 | tf_op jit(solution)/shard_map/ppermute | solution.py:192
